TPU v7x, 32 devices: a whole 2x2x4 slice. The times are simulated.
32 devices in a mesh: dp: 8 (over z, x), rep: 4 (over y, core).
Axes of the slice: x: 2, y: 2, z: 4, core: 2. Of those that a mesh axis runs over, the one named last changes fastest.
Arguments:
- events: bfloat16 [16384, 512], P(('dp', 'rep')), may hold values from -6 to 6
- grad_out: bfloat16 [16384, 512], P(('dp', 'rep')), may hold values from -15 to 15
- w_uvqk: bfloat16 [512, 2048], replicated, may hold values from -0.25 to 0.25
- w_out: bfloat16 [512, 512], replicated, may hold values from -0.25 to 0.25
- send_place: int32 [32, 512], P(('dp', 'rep')), may hold values from 0 to 1023, as said below
- send_counts: int32 [32, 8], P(('dp', 'rep')), may hold values from 0 to 128, as said below
- user_ids: int32 [32, 512], P(('dp', 'rep')), may hold values from 0 to 15, never falling along the last dimension, each value on 1 to 256 neighbouring positions
Outputs:
- grad_events: bfloat16 [16384, 512], P(('dp', 'rep'))
- grad_w_uvqk: float32 [512, 2048], P(None, 'dp')
- grad_w_out: float32 [512, 512], P(None, 'dp')
Inputs may be any that keep to these rules, and one draw needn't show every extreme that they name: `send_counts`: row d * 4 + r gives, for each owner o of group r, how many events device (d, r) sends there; each row sums to 512, and the counts one owner receives from the 8 devices of its group also sum to 512. `send_place`: an event bound for owner o has place o * 128 + j, where j runs from 0 to that owner's count minus 1 over the device's events bound for o; each place at most once on a device. `user_ids`: each row lists an owner's users in the owner's order of events; ids never fall.
All inputs are finite; a program needn't handle non-finite values.
Results may differ from a plain program's by a relative error of at most 0.02.
Values may be sent and summed in bfloat16 or wider, within the bound.
No kernel may reach another device: no remote copies, remote signals or barrier semaphores. Data moves between devices by JAX's collectives and lax.ppermute only.
A program may use at most 192 MiB of HBM per device.

v0:
```python
import jax
import jax.numpy as jnp
from jax import lax
from jax.sharding import PartitionSpec as P

HEADS = 8


EPSILON = 1e-05


def normalized_row_block(values):
    center = values - jnp.mean(values, axis=-1, keepdims=True)
    spread = jnp.mean(center * center, axis=-1, keepdims=True)
    return center * lax.rsqrt(spread + EPSILON)


def hstu_layer(event_row_block, input_weight_matrix, weight_out, allowed):
    width = weight_out.shape[0]
    count = event_row_block.shape[0]
    head_size = width // HEADS
    normalized_input = normalized_row_block(event_row_block.astype(jnp.float32)).astype(
        jnp.bfloat16
    )
    activation_value = jax.nn.silu(
        jnp.dot(normalized_input, input_weight_matrix, preferred_element_type=jnp.float32)
    ).astype(jnp.bfloat16)
    gate_u = activation_value[:, :width]
    values = activation_value[:, width : 2 * width].reshape(count, HEADS, head_size)
    queries = activation_value[:, 2 * width : 3 * width].reshape(count, HEADS, head_size)
    keys = activation_value[:, 3 * width :].reshape(count, HEADS, head_size)
    scores = jnp.einsum(
        "qhd,khd->hqk", queries, keys, preferred_element_type=jnp.float32
    ) * head_size ** (-0.5)
    weights = (jax.nn.silu(scores) * allowed[None]).astype(jnp.bfloat16)
    attended = jnp.einsum(
        "hqk,khd->qhd", weights, values, preferred_element_type=jnp.float32
    ).reshape(count, width)
    gated = (normalized_row_block(attended) * gate_u.astype(jnp.float32)).astype(jnp.bfloat16)
    return event_row_block.astype(jnp.float32) + jnp.dot(
        gated, weight_out, preferred_element_type=jnp.float32
    )


def owner_grads(event_row_block, cotangent, input_weight_matrix, weight_out, allowed):
    result, pullback = jax.vjp(
        lambda first, second, third: hstu_layer(first, second, third, allowed),
        event_row_block,
        input_weight_matrix,
        weight_out,
    )
    return pullback(cotangent.astype(jnp.float32))


def compact_index(counts_in, owned, capacity):
    ends = jnp.cumsum(counts_in)
    starts = ends - counts_in
    target_positions = jnp.arange(owned, dtype=jnp.int32)
    source = jnp.sum((target_positions[:, None] >= ends[None, :]).astype(jnp.int32), axis=1)
    onehot = (jnp.arange(counts_in.shape[0], dtype=jnp.int32)[None, :] == source[:, None]).astype(
        jnp.int32
    )
    first = jnp.sum(onehot * starts[None, :], axis=1)
    return source * capacity + target_positions - first


def on_device(events, grad_out, w_uvqk, w_out, send_place, send_counts, user_ids):
    owners = lax.axis_size("dp")
    owned = events.shape[0]
    width = events.shape[1]
    capacity = 2 * owned // owners
    places_out = send_place[0]
    send_rows = jnp.zeros((owners * capacity, width), jnp.bfloat16).at[places_out].set(events)
    send_grads = jnp.zeros((owners * capacity, width), jnp.bfloat16).at[places_out].set(grad_out)
    recv_rows, recv_grads = (
        lax.all_to_all(send_rows, "dp", split_axis=0, concat_axis=0, tiled=True),
        lax.all_to_all(send_grads, "dp", split_axis=0, concat_axis=0, tiled=True),
    )
    count_table = lax.all_gather(send_counts, "dp", axis=0, tiled=True)
    own_index = lax.axis_index("dp")
    counts_in = lax.dynamic_slice_in_dim(count_table, own_index, 1, 1)[:, 0]
    users = user_ids[0]
    order_index = compact_index(counts_in, owned, capacity)
    owned_x = jnp.take(recv_rows, order_index, axis=0)
    owned_dy = jnp.take(recv_grads, order_index, axis=0)
    target_positions = jnp.arange(owned, dtype=jnp.int32)
    allowed = (
        (users[:, None] == users[None, :])
        & (target_positions[None, :] <= target_positions[:, None])
    ).astype(jnp.float32)
    grad_x, grad_in, grad_outw = owner_grads(owned_x, owned_dy, w_uvqk, w_out, allowed)
    grad_rows = jnp.zeros((owners * capacity, width), jnp.bfloat16).at[order_index].set(grad_x)
    returned = lax.all_to_all(grad_rows, "dp", split_axis=0, concat_axis=0, tiled=True)
    grad_events = jnp.take(returned, places_out, axis=0)
    grad_in = grad_in.astype(jnp.float32)
    grad_outw = grad_outw.astype(jnp.float32)
    part_in, part_out = (
        lax.psum_scatter(
            grad_in.astype(jnp.bfloat16), "dp", scatter_dimension=1, tiled=True
        ).astype(jnp.float32),
        lax.psum_scatter(
            grad_outw.astype(jnp.bfloat16), "dp", scatter_dimension=1, tiled=True
        ).astype(jnp.float32),
    )
    share_in, share_out = (
        lax.psum(part_in.astype(jnp.bfloat16), "rep").astype(jnp.float32),
        lax.psum(part_out.astype(jnp.bfloat16), "rep").astype(jnp.float32),
    )
    return (grad_events, share_in, share_out)


def solution(mesh):
    return jax.shard_map(
        on_device,
        mesh=mesh,
        in_specs=(
            P(("dp", "rep"), None),
            P(("dp", "rep"), None),
            P(),
            P(),
            P(("dp", "rep"), None),
            P(("dp", "rep"), None),
            P(("dp", "rep"), None),
        ),
        out_specs=(P(("dp", "rep"), None), P(None, "dp"), P(None, "dp")),
        check_vma=False,
    )
```

profile of v0, /device:TPU:0, one launch (start us, length us, event | category | flops | bytes accessed | tf_op | source)
XLA Modules:
  0.0 290.9 jit_solution(2502891289232212408)
XLA Ops:
  7.2 0.8 compare_select_fusion
  8.0 4.0 %scatter_custom_fusion.1 = bf16[1024,512]{1,0:T(8,128)(2,1)} fusion(s32[512]{0:T(512)S(1)} %bitcast.94, bf16[512,512]{1,0:T(8,128)(2,1)} %param.9, bf16[]{:T(256)} %constant.21.clone.1), kind=kCustom, calls=%fused_computation.57 | custom fusion | bytes 1049088 | tf_op jit(solution)/shard_map/scatter | solution.py:73
  12.0 7.3 %all-to-all-start.1 = ((bf16[8,128,512]{2,1,0:T(8,128)(2,1)}), bf16[8,128,512]{2,1,0:T(8,128)(2,1)S(1)}, u32[]{:S(2)}, u32[]{:S(2)}) async-start(bf16[8,128,512]{2,1,0:T(8,128)(2,1)} %bitcast.75), calls=%async_computation.1 | async-start | bytes 2097152 | tf_op jit(solution)/shard_map/all_to_all | solution.py:76
  19.3 31.6 %all-gather = s32[8,1,8]{2,1,0:T(1,128)S(1)} all-gather(s32[1,1,8]{2,1,0:T(1,128)} %bitcast.96), channel_id=1, replica_groups=mesh['dp'=8,'rep'=4] {'dp'}, dimensions={0}, use_global_device_ids=true | all-gather | bytes 288 | tf_op jit(solution)/shard_map/all_gather | solution.py:79
  50.8 0.3 dynamic-slice_reduce_fusion
  51.1 0.2 reduce-window.7
  51.3 4.0 %scatter_custom_fusion = bf16[1024,512]{1,0:T(8,128)(2,1)} fusion(s32[512]{0:T(512)S(1)} %bitcast.95, bf16[512,512]{1,0:T(8,128)(2,1)} %param.10, bf16[]{:T(256)} %constant.21.clone.1), kind=kCustom, calls=%fused_computation.59 | custom fusion | bytes 1049088 | tf_op jit(solution)/shard_map/scatter | solution.py:74
  55.5 1.2 fusion.16
  56.7 5.9 %all-to-all-start = ((bf16[8,128,512]{2,1,0:T(8,128)(2,1)}), bf16[8,128,512]{2,1,0:T(8,128)(2,1)}, u32[]{:S(2)}, u32[]{:S(2)}) async-start(bf16[8,128,512]{2,1,0:T(8,128)(2,1)} %bitcast.74), calls=%async_computation | async-start | bytes 2097152 | tf_op jit(solution)/shard_map/all_to_all | solution.py:77
  62.5 0.2 reduce-scatter.5.cloned.1.call-start
  62.8 2.6 gather_fusion.1
  65.4 1.3 copy.28
  66.8 0.2 fusion.9
  67.0 3.8 %multiply_convert_fusion.1 = (bf16[512,2048]{0,1:T(8,128)(2,1)S(1)}, f32[512,2048]{0,1:T(8,128)}) fusion(bf16[512,2048]{1,0:T(8,128)(2,1)S(1)} %copy-done, f32[512]{0:T(512)S(1)} %fusion.31, f32[512]{0:T(512)S(1)} %broadcast_multiply_fusion.1, bf16[512,512]{0,1:T(8,128)(2,1)S(1)} %copy.28, pred[512]{0:T(512)(128)(4,1)S(1)} %get-tuple-element.6), kind=kOutput, calls=%fused_computation.17 | convolution fusion | flops 1080295424 | bytes 8917504 | tf_op jit(solution)/shard_map/jvp()/dot_general | solution.py:26
  71.0 1.2 copy-done.5
  72.2 4.8 %multiply_convert_fusion = (bf16[8,512,512]{2,1,0:T(8,128)(2,1)S(1)}, f32[8,512,512]{2,1,0:T(8,128)}) fusion(f32[512,512]{1,0:T(8,128)S(1)} %copy-done.16, bf16[512,8,64]{0,2,1:T(8,128)(2,1)S(1)} %bitcast.82, bf16[512,8,64]{0,2,1:T(8,128)(2,1)S(1)} %bitcast.84), kind=kOutput, calls=%fused_computation.10 | convolution fusion | flops 283115520 | bytes 14680064 | tf_op jit(solution)/shard_map/jvp(qhd,khd->hqk)/dot_general | solution.py:32
  77.1 2.0 copy-done.1
  79.0 1.4 fusion.38
  80.4 5.4 %all-to-all-done = bf16[8,128,512]{2,1,0:T(8,128)(2,1)} async-done(((bf16[8,128,512]{2,1,0:T(8,128)(2,1)}), bf16[8,128,512]{2,1,0:T(8,128)(2,1)}, u32[]{:S(2)}, u32[]{:S(2)}) %all-to-all-start) | async-done | bytes 1048608 | tf_op jit(solution)/shard_map/all_to_all | solution.py:77
  85.9 4.0 %gather_fusion = bf16[512,512]{1,0:T(8,128)(2,1)} fusion(bf16[1024,512]{1,0:T(8,128)(2,1)} %bitcast.9, s32[1024]{0:T(1024)S(1)} %pad_clamp_fusion.1), kind=kCustom, calls=%fused_computation.clone | custom fusion | bytes 1050624 | tf_op jit(solution)/shard_map/jit(_take)/gather | solution.py:85
  89.9 2.0 copy.27
  91.9 0.2 fusion.14
  92.1 2.0 multiply_reduce_fusion
  94.1 1.3 fusion.11
  95.4 0.4 broadcast_add_fusion
  95.8 0.8 fusion.39
  96.6 0.2 copy-done.17
  96.8 6.9 %fusion.2 = bf16[8,512,512]{2,1,0:T(8,128)(2,1)S(1)} fusion(f32[8,512,512]{2,1,0:T(8,128)} %get-tuple-element.19, f32[512,512]{1,0:T(8,128)S(1)} %copy-done.17, bf16[8,64,512]{2,1,0:T(8,128)(2,1)S(1)} %bitcast.81, bf16[512,8,64]{0,2,1:T(8,128)(2,1)S(1)} %bitcast.87), kind=kOutput, calls=%fused_computation.9 | convolution fusion | flops 297795584 | bytes 14680064 | tf_op jit(solution)/shard_map/transpose(jvp(hqk,khd->qhd))/dot_general | solution.py:36
  103.8 2.2 fusion.40
  106.0 1.7 fusion.41
  107.6 1.3 convolution_convert_fusion.2
  109.0 3.5 %fusion.3 = bf16[512,2048]{0,1:T(8,128)(2,1)S(1)} fusion(f32[512,2048]{0,1:T(8,128)} %get-tuple-element.17, bf16[512,512]{0,1:T(8,128)(2,1)} %get-tuple-element.13, bf16[512,512]{0,1:T(8,128)(2,1)S(1)} %bitcast.77, bf16[512,512]{0,1:T(8,128)(2,1)} %bitcast.78, bf16[512,512]{0,1:T(8,128)(2,1)} %bitcast.79), kind=kLoop, calls=%fused_computation.15 | loop fusion | flops 18874368 | bytes 8388608 | tf_op jit(solution)/shard_map/transpose(jvp(jit(silu)))/add_any | solution.py:25
  112.5 1.3 copy-done.13
  113.8 2.7 convolution_convert_fusion
  116.5 2.9 %fusion.12 = (f32[512]{0:T(512)S(1)}, bf16[512,512]{0,1:T(8,128)(2,1)S(1)}) fusion(f32[512]{0:T(512)S(1)} %broadcast_multiply_fusion.1, bf16[512,512]{0,1:T(8,128)(2,1)S(1)} %copy-done.4, pred[512]{0:T(512)(128)(4,1)S(1)} %get-tuple-element.6, bf16[512,2048]{0,1:T(8,128)(2,1)} %copy-done.13, bf16[512,2048]{1,0:T(8,128)(2,1)S(1)} %copy-done), kind=kOutput, calls=%fused_computation.42 | convolution fusion | flops 1075314176 | bytes 5247488 | tf_op jit(solution)/shard_map/transpose(jvp())/dot_general | solution.py:26
  119.5 0.3 fusion.17
  119.8 0.4 fusion.18
  120.3 0.2 copy.32
  120.5 3.5 %scatter_custom_fusion.2 = bf16[1024,512]{1,0:T(8,128)(2,1)} fusion(s32[512]{0:T(512)S(1)} %bitcast.93, bf16[512,512]{1,0:T(8,128)(2,1)S(1)} %copy.32, bf16[]{:T(256)} %constant.21.clone.1), kind=kCustom, calls=%fused_computation.55 | custom fusion | bytes 1048578 | tf_op jit(solution)/shard_map/scatter | solution.py:92
  124.0 3.6 %all-to-all-start.2 = ((bf16[8,128,512]{2,1,0:T(8,128)(2,1)}), bf16[8,128,512]{2,1,0:T(8,128)(2,1)S(1)}, u32[]{:S(2)}, u32[]{:S(2)}) async-start(bf16[8,128,512]{2,1,0:T(8,128)(2,1)} %bitcast.76), calls=%async_computation.2 | async-start | bytes 2097152 | tf_op jit(solution)/shard_map/all_to_all | solution.py:93
  127.6 25.9 %all-to-all-done.2 = bf16[8,128,512]{2,1,0:T(8,128)(2,1)S(1)} async-done(((bf16[8,128,512]{2,1,0:T(8,128)(2,1)}), bf16[8,128,512]{2,1,0:T(8,128)(2,1)S(1)}, u32[]{:S(2)}, u32[]{:S(2)}) %all-to-all-start.2) | async-done | bytes 1048608 | tf_op jit(solution)/shard_map/all_to_all | solution.py:93
  153.5 2.6 gather_fusion.2
  156.1 19.5 %reduce-scatter.5.cloned.1.call-done = bf16[512,64]{0,1:T(8,128)(2,1)} async-done(((bf16[512,512]{0,1:T(8,128)(2,1)}), bf16[512,64]{0,1:T(8,128)(2,1)}) %reduce-scatter.5.cloned.1.call-update) | async-done | bytes 65552 | tf_op jit(solution)/shard_map/reduce_scatter | solution.py:101
  175.6 71.3 %reduce-scatter.3.cloned.1.call-done = bf16[512,256]{1,0:T(8,128)(2,1)} async-done(((bf16[512,2048]{1,0:T(8,128)(2,1)}), bf16[512,256]{1,0:T(8,128)(2,1)}) %reduce-scatter.3.cloned.1.call-update) | async-done | bytes 262160 | tf_op jit(solution)/shard_map/reduce_scatter | solution.py:98
  247.0 2.0 broadcast_select_fusion
  248.9 32.2 %all-reduce.7.cloned.1.call-done = (bf16[512,256]{1,0:T(8,128)(2,1)}, bf16[512,64]{0,1:T(8,128)(2,1)}) async-done(((bf16[512,256]{1,0:T(8,128)(2,1)}, bf16[512,64]{0,1:T(8,128)(2,1)}), (bf16[512,256]{1,0:T(8,128)(2,1)}, bf16[512,64]{0,1:T(8,128)(2,1)})) %all-reduce.7.cloned.1.call-update) | async-done | bytes 327696 | tf_op jit(solution)/shard_map/psum | solution.py:106
  281.1 1.8 convert_element_type.119
  282.9 1.5 convert_element_type.122
  (61 shorter events, 0.7 us)
Async XLA Ops:
  7.2 59.9 %copy-start = (bf16[512,2048]{1,0:T(8,128)(2,1)S(1)}, bf16[512,2048]{1,0:T(8,128)(2,1)}, u32[]{:S(2)}) copy-start(bf16[512,2048]{1,0:T(8,128)(2,1)} %param.11) | copy-start | bytes 6291460
  7.2 48.3 %copy-start.19 = (s32[1,512]{1,0:T(1,128)S(1)}, s32[1,512]{1,0:T(1,128)}, u32[]{:S(2)}) copy-start(s32[1,512]{1,0:T(1,128)} %param.15) | copy-start | bytes 6148
  12.0 44.7 %all-to-all-start.1 = ((bf16[8,128,512]{2,1,0:T(8,128)(2,1)}), bf16[8,128,512]{2,1,0:T(8,128)(2,1)S(1)}, u32[]{:S(2)}, u32[]{:S(2)}) async-start(bf16[8,128,512]{2,1,0:T(8,128)(2,1)} %bitcast.75), calls=%async_computation.1 | async-start | bytes 2097152 | tf_op jit(solution)/shard_map/all_to_all | solution.py:76
  56.7 29.2 %all-to-all-start = ((bf16[8,128,512]{2,1,0:T(8,128)(2,1)}), bf16[8,128,512]{2,1,0:T(8,128)(2,1)}, u32[]{:S(2)}, u32[]{:S(2)}) async-start(bf16[8,128,512]{2,1,0:T(8,128)(2,1)} %bitcast.74), calls=%async_computation | async-start | bytes 2097152 | tf_op jit(solution)/shard_map/all_to_all | solution.py:77
  62.5 113.1 %reduce-scatter.5.cloned.1.call-start = ((), (), s32[]{:S(2)}) async-start(), calls=%async_computation.6 | async-start | bytes 589824 | tf_op jit(solution)/shard_map/reduce_scatter | solution.py:101
  66.6 4.2 %copy-start.3 = (bf16[512,512]{0,1:T(8,128)(2,1)}, bf16[512,512]{0,1:T(8,128)(2,1)S(1)}, u32[]{:S(2)}) copy-start(bf16[512,512]{0,1:T(8,128)(2,1)S(1)} %copy.28) | copy-start | bytes 1572868
  67.0 5.2 %copy-start.16 = (f32[512,512]{1,0:T(8,128)S(1)}, f32[512,512]{1,0:T(8,128)}, u32[]{:S(2)}) copy-start(f32[512,512]{1,0:T(8,128)} %fusion.16) | copy-start | bytes 3145732
  70.9 1.4 copy-start.5
  71.0 6.1 %copy-start.9 = (bf16[512,512]{0,1:T(8,128)(2,1)}, bf16[512,512]{0,1:T(8,128)(2,1)S(1)}, u32[]{:S(2)}) copy-start(bf16[512,512]{0,1:T(8,128)(2,1)S(1)} %get-tuple-element.11) | copy-start | bytes 1572868
  71.0 6.1 %copy-start.11 = (bf16[512,512]{0,1:T(8,128)(2,1)}, bf16[512,512]{0,1:T(8,128)(2,1)S(1)}, u32[]{:S(2)}) copy-start(bf16[512,512]{0,1:T(8,128)(2,1)S(1)} %get-tuple-element.10) | copy-start | bytes 1572868
  71.0 6.1 %copy-start.14 = (bf16[512,512]{0,1:T(8,128)(2,1)}, bf16[512,512]{0,1:T(8,128)(2,1)S(1)}, u32[]{:S(2)}) copy-start(bf16[512,512]{0,1:T(8,128)(2,1)S(1)} %get-tuple-element.12) | copy-start | bytes 1572868
  77.1 2.0 copy-start.1
  91.9 2.2 copy-start.6
  92.1 3.7 %copy-start.2 = (bf16[8,512,512]{2,1,0:T(8,128)(2,1)S(1)}, bf16[8,512,512]{2,1,0:T(8,128)(2,1)}, u32[]{:S(2)}) copy-start(bf16[8,512,512]{2,1,0:T(8,128)(2,1)} %copy-done.1) | copy-start | bytes 12582916
  95.4 1.2 copy-start.15
  95.4 1.4 copy-start.17
  96.8 6.9 %copy-start.12 = (bf16[512,512]{0,1:T(8,128)(2,1)S(1)}, bf16[512,512]{0,1:T(8,128)(2,1)}, u32[]{:S(2)}) copy-start(bf16[512,512]{0,1:T(8,128)(2,1)} %copy-done.11) | copy-start | bytes 1572868
  103.8 2.2 copy-start.10
  103.8 3.9 %copy-start.7 = (bf16[512,512]{0,1:T(8,128)(2,1)S(1)}, bf16[512,512]{0,1:T(8,128)(2,1)}, u32[]{:S(2)}) copy-start(bf16[512,512]{0,1:T(8,128)(2,1)} %copy.27) | copy-start | bytes 1572868
  108.9 138.0 %reduce-scatter.3.cloned.1.call-start = ((), (), s32[]{:S(2)}) async-start(), calls=%async_computation.5 | async-start | bytes 2359296 | tf_op jit(solution)/shard_map/reduce_scatter | solution.py:98
  109.0 4.8 %copy-start.4 = (bf16[512,512]{0,1:T(8,128)(2,1)S(1)}, bf16[512,512]{0,1:T(8,128)(2,1)}, u32[]{:S(2)}) copy-start(bf16[512,512]{0,1:T(8,128)(2,1)} %copy-done.3) | copy-start | bytes 1572868
  112.5 1.3 copy-start.13
  116.5 3.3 %copy-start.8 = (bf16[512,512]{0,1:T(8,128)(2,1)S(1)}, bf16[512,512]{0,1:T(8,128)(2,1)}, u32[]{:S(2)}) copy-start(bf16[512,512]{0,1:T(8,128)(2,1)} %copy.27) | copy-start | bytes 1572868
  119.5 8.1 %copy-start.18 = (s32[1,512]{1,0:T(1,128)S(1)}, s32[1,512]{1,0:T(1,128)}, u32[]{:S(2)}) copy-start(s32[1,512]{1,0:T(1,128)} %param.13) | copy-start | bytes 6148
  124.0 29.5 %all-to-all-start.2 = ((bf16[8,128,512]{2,1,0:T(8,128)(2,1)}), bf16[8,128,512]{2,1,0:T(8,128)(2,1)S(1)}, u32[]{:S(2)}, u32[]{:S(2)}) async-start(bf16[8,128,512]{2,1,0:T(8,128)(2,1)} %bitcast.76), calls=%async_computation.2 | async-start | bytes 2097152 | tf_op jit(solution)/shard_map/all_to_all | solution.py:93
  127.5 153.6 %all-reduce.7.cloned.1.call-start = ((), (), s32[]{:S(2)}) async-start(), calls=%async_computation.7 | async-start | bytes 655360 | tf_op jit(solution)/shard_map/psum | solution.py:106
Sparse Core Ops, SparseCore 0:
  109.0 66.5 reduce-scatter.4
  179.6 67.3 reduce-scatter.2
  249.6 31.5 all-reduce.6
where the time goes:
time: 292 us; the launch traced here: 291 us
  waiting for transfers between devices  154 us (53%)
  blocking collectives  31.6 us (11%)
  matrix products  30.5 us (10%)
  local copies, waits for them, and re-layouts  29.3 us (10%)
  starting transfers between devices  17 us (6%)
  other arithmetic  14.2 us (5%)
  between operations  14.1 us (5%)
    reduce_scatter x1, waiting for transfers between devices, on_device(): lax.psum_scatter(grad_in.astype(jnp.bfloat16), 'dp', scatter_dimension=1,...  71.3 us
    psum x1, waiting for transfers between devices, on_device(): lax.psum(part_in.astype(jnp.bfloat16), 'rep').astype(jnp.float32)  32.2 us
    all_gather x1, blocking collectives, on_device(): count_table = lax.all_gather(send_counts, 'dp', axis=0, tiled=True)  31.6 us
    all_to_all x1, waiting for transfers between devices, on_device(): lax.all_to_all(grad_rows, 'dp', split_axis=0, concat_axis=0, tiled=True)  25.9 us
    reduce_scatter x1, waiting for transfers between devices, on_device(): lax.psum_scatter(grad_outw.astype(jnp.bfloat16), 'dp', scatter_dimension=...  19.5 us
    dot_general x3, matrix products, hstu_layer(): jnp.dot(normalized_input, input_weight_matrix, preferred_element_type=jnp...  9.43 us
    dot_general x3, matrix products, hstu_layer(): jnp.einsum('hqk,khd->qhd', weights, values, preferred_element_type=jnp.fl...  9.09 us
    dot_general x3, matrix products, hstu_layer(): jnp.einsum('qhd,khd->hqk', queries, keys, preferred_element_type=jnp.floa...  8.66 us
  transfers between devices with their start and end apart: 6, of which 5 were waited for; matrix products, arithmetic and copies ran while one was open for 13% of the time, Pallas kernels for 0%

commit v1 on v0

v1 whole, which is shorter than its diff:
```python
import functools

import jax
import jax.numpy as jnp
from jax import lax
from jax.experimental import pallas as pl
from jax.experimental.pallas import tpu as pltpu
from jax.sharding import PartitionSpec as P

HEADS = 8
LONGEST = 256
EPSILON = 1e-05
EMPTY = 128.0
BLOCK = 128
LANES = 128
F32 = jnp.float32
BF16 = jnp.bfloat16
VMEM_LIMIT = 40 * 1024 * 1024


def dot(a, b):
    return jnp.dot(a, b, preferred_element_type=F32)


def dot_nt(a, b):
    return lax.dot_general(a, b, (((1,), (1,)), ((), ())), preferred_element_type=F32)


def iota(shape, dim):
    return lax.broadcasted_iota(jnp.int32, shape, dim)


def call(kernel, out_shape, *args, flops=0, transcendentals=0):
    moved = sum(a.size * a.dtype.itemsize for a in args)
    moved += sum(o.size * o.dtype.itemsize for o in jax.tree.leaves(out_shape))
    return pl.pallas_call(
        kernel,
        out_shape=out_shape,
        compiler_params=pltpu.CompilerParams(vmem_limit_bytes=VMEM_LIMIT),
        cost_estimate=pl.CostEstimate(
            flops=flops, bytes_accessed=moved, transcendentals=transcendentals
        ),
    )(*args)


def shape(dims, dtype=BF16):
    return jax.ShapeDtypeStruct(tuple(dims), dtype)


def spread_kernel(owners, capacity, mark, place_ref, rows_ref, *out_refs):
    me = lax.axis_index("dp")
    place = place_ref[...]
    rows = rows_ref[...]
    count = rows.shape[0]
    for k in range(owners):
        first = (me ^ k) * capacity
        onehot = (iota((capacity, count), 0) + first == place).astype(F32)
        block = dot(onehot.astype(BF16), rows)
        if mark:
            filled = jnp.sum(onehot, axis=1, keepdims=True)
            block = block + (1.0 - filled) * EMPTY
        out_refs[k][...] = block.astype(BF16)


def lookup_kernel(owners, capacity, place_ref, out_ref):
    me = lax.axis_index("dp")
    count = place_ref.shape[1]
    column = jnp.broadcast_to(place_ref[...].astype(F32), (LANES, count)).T[:, 0:1].astype(jnp.int32)
    slot = iota((count, owners * capacity), 1)
    at = (me ^ (slot // capacity)) * capacity + slot % capacity
    out_ref[...] = (at == column).astype(F32).astype(BF16)


def forward_kernel(owners, capacity, *refs):
    blocks = refs[:owners]
    users_ref, w_ref = refs[owners : owners + 2]
    (
        place_ref, unplace_ref, act_ref, slope_ref, xhat_ref, xhat_t_ref, x_rstd_ref,
        weights_ref, tangent_ref, nhat_ref, a_rstd_ref, gated_t_ref, q_t_ref, att_ref,
    ) = refs[owners + 2 :]
    me = lax.axis_index("dp")
    count, width = xhat_ref.shape
    half = width // HEADS
    valid = [blocks[k][:, 0:LANES].astype(F32) != EMPTY for k in range(owners)]
    counts = [jnp.sum(v.astype(F32), axis=0, keepdims=True) for v in valid]
    source = iota((owners, LANES), 0) ^ me
    starts = jnp.zeros((owners, LANES), F32)
    for k in range(owners):
        starts = starts + jnp.where(source > (me ^ k), counts[k], 0.0)
    within = iota((capacity, LANES), 0).astype(F32)
    target = jnp.concatenate(
        [jnp.where(valid[k], starts[k : k + 1] + within, -1.0) for k in range(owners)], axis=0
    )
    target_t = target.T[0:1, :]
    slots = owners * capacity
    place = (iota((count, slots), 0) == target_t.astype(jnp.int32)).astype(F32).astype(BF16)
    place_ref[...] = place
    column = target[:, 0:1].astype(jnp.int32)
    unplace_ref[...] = (iota((slots, count), 1) == column).astype(F32).astype(BF16)
    received = jnp.concatenate([blocks[k][...] for k in range(owners)], axis=0)
    x = dot(place, received)
    center = x - jnp.mean(x, axis=1, keepdims=True)
    rstd = lax.rsqrt(jnp.mean(center * center, axis=1, keepdims=True) + EPSILON)
    xhat32 = center * rstd
    xhat = xhat32.astype(BF16)
    xhat_ref[...] = xhat
    xhat_t_ref[...] = xhat32.T.astype(BF16)
    x_rstd_ref[...] = jnp.broadcast_to(rstd, (count, LANES))
    for part in range(4):
        columns = slice(part * width, (part + 1) * width)
        pre = dot(xhat, w_ref[:, columns])
        sig = 0.5 * jnp.tanh(0.5 * pre) + 0.5
        act = pre * sig
        act_ref[:, columns] = act.astype(BF16)
        slope_ref[:, columns] = (sig + act * (1.0 - sig)).astype(BF16)
        if part == 2:
            q_t_ref[...] = act.T.astype(BF16)
    users = users_ref[...]
    users_column = jnp.broadcast_to(users.astype(F32), (LANES, count)).T[:, 0:1].astype(jnp.int32)
    scale = half ** (-0.5)
    lane = iota((BLOCK, LANES), 1)
    for i in range(count // BLOCK):
        low = max(0, i - LONGEST // BLOCK) * BLOCK
        high = (i + 1) * BLOCK
        span = high - low
        rows = slice(i * BLOCK, high)
        keep = (users_column[rows] == users[:, low:high]) & (
            iota((BLOCK, span), 1) + low <= iota((BLOCK, span), 0) + i * BLOCK
        )
        for pair in range(width // LANES):
            lanes = slice(pair * LANES, (pair + 1) * LANES)
            v = act_ref[low:high, width + lanes.start : width + lanes.stop]
            q = act_ref[rows, 2 * width + lanes.start : 2 * width + lanes.stop]
            k = act_ref[low:high, 3 * width + lanes.start : 3 * width + lanes.stop]
            attended = jnp.zeros((BLOCK, LANES), F32)
            for inner in range(LANES // half):
                mine = lane // half == inner
                score = dot_nt(jnp.where(mine, q, jnp.zeros_like(q)), k) * scale
                sig = 0.5 * jnp.tanh(0.5 * score) + 0.5
                value = score * sig
                weight = jnp.where(keep, value, 0.0).astype(BF16)
                tangent = jnp.where(keep, (sig + value * (1.0 - sig)) * scale, 0.0)
                head = pair * (LANES // half) + inner
                weights_ref[head, i, :, 0:span] = weight
                tangent_ref[head, i, :, 0:span] = tangent.astype(BF16)
                attended = jnp.where(mine, dot(weight, v), attended)
            att_ref[rows, lanes] = attended
    attended = att_ref[...]
    center = attended - jnp.mean(attended, axis=1, keepdims=True)
    rstd = lax.rsqrt(jnp.mean(center * center, axis=1, keepdims=True) + EPSILON)
    nhat = center * rstd
    nhat_ref[...] = nhat.astype(BF16)
    a_rstd_ref[...] = jnp.broadcast_to(rstd, (count, LANES))
    gated_t_ref[...] = (nhat * act_ref[:, 0:width].astype(F32)).T.astype(BF16)


def backward_kernel(owners, capacity, *refs):
    blocks = refs[:owners]
    (
        place_ref, unplace_ref, act_ref, slope_ref, xhat_ref, x_rstd_ref, weights_ref,
        tangent_ref, nhat_ref, a_rstd_ref, q_t_ref, w_ref, w_out_ref,
    ) = refs[owners : owners + 13]
    dy_ref, dpre_ref = refs[owners + 13 : owners + 15]
    out_refs = refs[owners + 15 : 2 * owners + 15]
    datt_ref, datt_t_ref, dkv_t_ref = refs[2 * owners + 15 :]
    count, width = xhat_ref.shape
    half = width // HEADS
    received = jnp.concatenate([blocks[k][...] for k in range(owners)], axis=0)
    dy32 = dot(place_ref[...], received)
    dy = dy32.astype(BF16)
    dy_ref[...] = dy
    dgated = dot_nt(dy, w_out_ref[...])
    nhat = nhat_ref[...].astype(F32)
    dpre_ref[:, 0:width] = (dgated * nhat * slope_ref[:, 0:width].astype(F32)).astype(BF16)
    dnhat = dgated * act_ref[:, 0:width].astype(F32)
    datt = a_rstd_ref[:, 0:1] * (
        dnhat
        - jnp.mean(dnhat, axis=1, keepdims=True)
        - nhat * jnp.mean(dnhat * nhat, axis=1, keepdims=True)
    )
    datt_ref[...] = datt.astype(BF16)
    datt_t_ref[...] = datt.T.astype(BF16)
    lane = iota((BLOCK, LANES), 1)
    steps = count // BLOCK
    for pair in range(width // LANES):
        lanes = slice(pair * LANES, (pair + 1) * LANES)
        dq = [jnp.zeros((BLOCK, LANES), F32) for _ in range(steps)]
        for inner in range(LANES // half):
            mine = lane // half == inner
            head = pair * (LANES // half) + inner
            own = slice(head * half, (head + 1) * half)
            dk_t = [None] * steps
            dv_t = [None] * steps
            for i in range(steps):
                start = max(0, i - LONGEST // BLOCK)
                low, high = start * BLOCK, (i + 1) * BLOCK
                span = high - low
                rows = slice(i * BLOCK, high)
                v = act_ref[low:high, width + lanes.start : width + lanes.stop]
                k = act_ref[low:high, 3 * width + lanes.start : 3 * width + lanes.stop]
                da = datt_ref[rows, lanes]
                dweight = dot_nt(jnp.where(mine, da, jnp.zeros_like(da)), v)
                dscore = (dweight * tangent_ref[head, i, :, 0:span].astype(F32)).astype(BF16)
                dq[i] = jnp.where(mine, dot(dscore, k), dq[i])
                add_k = dot(q_t_ref[own, rows], dscore)
                add_v = dot(datt_t_ref[own, rows], weights_ref[head, i, :, 0:span])
                for j in range(start, i + 1):
                    at = slice((j - start) * BLOCK, (j - start + 1) * BLOCK)
                    dk_t[j] = add_k[:, at] if dk_t[j] is None else dk_t[j] + add_k[:, at]
                    dv_t[j] = add_v[:, at] if dv_t[j] is None else dv_t[j] + add_v[:, at]
            for j in range(steps):
                at = slice(j * BLOCK, (j + 1) * BLOCK)
                dkv_t_ref[0, inner * half : (inner + 1) * half, at] = dv_t[j]
                dkv_t_ref[1, inner * half : (inner + 1) * half, at] = dk_t[j]
        for part, grad in (
            (1, dkv_t_ref[0].T),
            (2, jnp.concatenate(dq, axis=0)),
            (3, dkv_t_ref[1].T),
        ):
            columns = slice(part * width + lanes.start, part * width + lanes.stop)
            dpre_ref[:, columns] = (grad * slope_ref[:, columns].astype(F32)).astype(BF16)
    dxhat = dot_nt(dpre_ref[...], w_ref[...])
    xhat = xhat_ref[...].astype(F32)
    dx = dy32 + x_rstd_ref[:, 0:1] * (
        dxhat
        - jnp.mean(dxhat, axis=1, keepdims=True)
        - xhat * jnp.mean(dxhat * xhat, axis=1, keepdims=True)
    )
    dx = dx.astype(BF16)
    for k in range(owners):
        rows = slice(k * capacity, (k + 1) * capacity)
        out_refs[k][...] = dot(unplace_ref[rows, :], dx).astype(BF16)


def fold(piece):
    rows, columns = piece.shape
    if columns >= LANES:
        return jnp.concatenate(
            [piece[:, c : c + LANES] for c in range(0, columns, LANES)], axis=0
        )
    step = rows * columns // LANES
    return jnp.concatenate([piece[r : r + step] for r in range(0, rows, step)], axis=1)


def unfold(piece, rows, columns):
    if columns >= LANES:
        return jnp.concatenate(
            [piece[r : r + rows] for r in range(0, piece.shape[0], rows)], axis=1
        )
    return jnp.concatenate(
        [piece[:, c : c + columns] for c in range(0, LANES, columns)], axis=0
    )


def halves_first(index, size):
    return (index & 1) * (size // 2) + (index >> 1)


def weight_kernel(owners, groups, xhat_t_ref, dpre_ref, gated_t_ref, dy_ref, keep_ref, send_ref):
    me = lax.axis_index("dp")
    group = lax.axis_index("rep")
    width = xhat_t_ref.shape[0]
    part = width // groups
    in_grad = dot(xhat_t_ref[...], dpre_ref[...])
    out_grad = dot(gated_t_ref[...], dy_ref[...])
    in_cols = in_grad.shape[1] // owners
    out_cols = out_grad.shape[1] // owners
    in_rows = part * in_cols // LANES
    for r in range(groups):
        rows = slice(r * part, (r + 1) * part)
        relative = group ^ r
        for target, ref in ((0, keep_ref), (1, send_ref)):

            @pl.when((relative & 1) == target)
            def _():
                for d in range(owners):
                    at = halves_first(me ^ d, owners)
                    ref[relative >> 1, at, 0:in_rows, :] = fold(
                        in_grad[rows, d * in_cols : (d + 1) * in_cols]
                    ).astype(BF16)
                    ref[relative >> 1, at, in_rows:, :] = fold(
                        out_grad[rows, d * out_cols : (d + 1) * out_cols]
                    ).astype(BF16)


def add_kernel(kept_ref, got_ref, keep_ref, send_ref):
    half = kept_ref.shape[0] // 2
    send_ref[...] = (kept_ref[half:].astype(F32) + got_ref[half:].astype(F32)).astype(BF16)
    keep_ref[...] = (kept_ref[:half].astype(F32) + got_ref[:half].astype(F32)).astype(BF16)


def total_kernel(*refs):
    total = refs[0][...].astype(F32)
    for ref in refs[1:-1]:
        total = total + ref[...].astype(F32)
    refs[-1][...] = total.astype(BF16)


def result_kernel(groups, in_cols, out_cols, *refs):
    in_ref, out_ref = refs[groups:]
    group = lax.axis_index("rep")
    part = in_ref.shape[0] // groups
    in_rows = part * in_cols // LANES
    for k in range(groups):
        rows = pl.ds(pl.multiple_of((group ^ k) * part, part), part)
        piece = refs[k][...].astype(F32)
        in_ref[rows, :] = unfold(piece[:in_rows], part, in_cols)
        out_ref[rows, :] = unfold(piece[in_rows:], part, out_cols)


def collect_kernel(owners, *refs):
    lookup_ref, out_ref = refs[owners:]
    rows = jnp.concatenate([refs[k][...] for k in range(owners)], axis=0)
    out_ref[...] = dot(lookup_ref[...], rows).astype(BF16)


def swap(value, axis, distance):
    size = lax.axis_size(axis)
    return lax.ppermute(value, axis, [(i, i ^ distance) for i in range(size)])


def exchange(blocks):
    return [blocks[0]] + [swap(blocks[k], "dp", k) for k in range(1, len(blocks))]


def on_device(events, grad_out, w_uvqk, w_out, send_place, send_counts, user_ids):
    owners = lax.axis_size("dp")
    groups = lax.axis_size("rep")
    count, width = events.shape
    capacity = 2 * count // owners
    slots = owners * capacity
    spans = (LONGEST // BLOCK + 1) * BLOCK
    steps = count // BLOCK
    block_shapes = [shape((capacity, width))] * owners
    route = 2 * slots * count * width

    spread = functools.partial(spread_kernel, owners, capacity)
    x_blocks = call(functools.partial(spread, True), block_shapes, send_place, events, flops=route)
    dy_blocks = call(
        functools.partial(spread, False), block_shapes, send_place, grad_out, flops=route
    )
    lookup = call(
        functools.partial(lookup_kernel, owners, capacity), shape((count, slots)), send_place
    )
    x_blocks = exchange(x_blocks)
    dy_blocks = exchange(dy_blocks)
    square = shape((count, width))
    square_t = shape((width, count))
    wide = shape((count, 4 * width))
    column = shape((count, LANES), F32)
    scores = shape((HEADS, steps, BLOCK, spans))
    project = 2 * count * width * 4 * width
    attend = 2 * count * spans * width
    (
        place, unplace, act, slope, xhat, xhat_t, x_rstd,
        weights, tangent, nhat, a_rstd, gated_t, q_t, _,
    ) = call(
        functools.partial(forward_kernel, owners, capacity),
        [
            shape((count, slots)), shape((slots, count)), wide, wide, square, square_t, column,
            scores, scores, square, column, square_t, square_t, shape((count, width), F32),
        ],
        *x_blocks, user_ids, w_uvqk,
        flops=route + project + 2 * attend, transcendentals=HEADS * count * spans,
    )
    backward = functools.partial(backward_kernel, owners, capacity)
    moved = 24 * 1024 * 1024
    results = pl.pallas_call(
        backward,
        out_shape=[square, wide] + block_shapes,
        scratch_shapes=[
            pltpu.VMEM((count, width), BF16),
            pltpu.VMEM((width, count), BF16),
            pltpu.VMEM((2, LANES, count), F32),
        ],
        compiler_params=pltpu.CompilerParams(vmem_limit_bytes=VMEM_LIMIT),
        cost_estimate=pl.CostEstimate(
            flops=2 * route + project + 4 * attend, bytes_accessed=moved, transcendentals=0
        ),
    )(
        *dy_blocks, place, unplace, act, slope, xhat, x_rstd, weights, tangent, nhat, a_rstd,
        q_t, w_uvqk, w_out,
    )
    owned_dy, dpre = results[:2]
    back = exchange(results[2:])
    rows = 5 * width * width // (owners * groups * LANES)
    kept, sent = call(
        functools.partial(weight_kernel, owners, groups),
        [shape((groups // 2, owners, rows, LANES))] * 2,
        xhat_t, dpre, gated_t, owned_dy, flops=project + project // 4,
    )
    got = swap(sent, "rep", 1)
    distance = 2
    while distance < groups:
        half = kept.shape[0] // 2
        kept, sent = call(add_kernel, [shape((half,) + kept.shape[1:])] * 2, kept, got)
        got = swap(sent, "rep", distance)
        distance *= 2
    kept, got = kept[0], got[0]
    kept, sent = call(add_kernel, [shape((owners // 2,) + kept.shape[1:])] * 2, kept, got)
    got = swap(sent, "dp", 1)
    total = call(total_kernel, shape(kept.shape), kept, got)
    pieces = [total[0]] + [swap(total[k], "dp", 2 * k) for k in range(1, owners // 2)]
    own = call(total_kernel, shape((rows, LANES)), *pieces)
    shares = [own] + [swap(own, "rep", k) for k in range(1, groups)]
    in_cols = 4 * width // owners
    out_cols = width // owners
    share_in, share_out = call(
        functools.partial(result_kernel, groups, in_cols, out_cols),
        [shape((width, in_cols), F32), shape((width, out_cols), F32)],
        *shares,
    )
    grad_events = call(
        functools.partial(collect_kernel, owners), square, *back, lookup, flops=route
    )
    return (grad_events, share_in, share_out)


def solution(mesh):
    return jax.shard_map(
        on_device,
        mesh=mesh,
        in_specs=(
            P(("dp", "rep"), None),
            P(("dp", "rep"), None),
            P(),
            P(),
            P(("dp", "rep"), None),
            P(("dp", "rep"), None),
            P(("dp", "rep"), None),
        ),
        out_specs=(P(("dp", "rep"), None), P(None, "dp"), P(None, "dp")),
        check_vma=False,
    )
```

time: 292 us -> 143 us (0.49)
  waiting for transfers between devices: 154 us -> 48 us
  starting transfers between devices: 17 us -> 57.4 us
  Pallas kernels: 0 us -> 31.9 us
  blocking collectives: 31.6 us -> 0 us
  matrix products: 30.5 us -> 0 us
  local copies, waits for them, and re-layouts: 29.3 us -> 4.4 us
  other arithmetic: 14.2 us -> 0 us
  between operations: 14.1 us -> 0.78 us
    reduce_scatter x2 -> x0, waiting for transfers between devices: 90.8 us -> none  [the longest x1 71.3 us: on_device(): lax.psum_scatter(grad_in.astype(jnp.bfloat16), 'dp', scatter_dimension=1,...]
    ppermute x0 -> x30, starting transfers between devices: none -> 57.4 us  [swap(): return lax.ppermute(value, axis, [(i, i ^ distance) for i in range(size)])]
    ppermute x0 -> x30, waiting for transfers between devices: none -> 48 us  [swap(): return lax.ppermute(value, axis, [(i, i ^ distance) for i in range(size)])]
    psum x1 -> x0, waiting for transfers between devices: 32.2 us -> none  [on_device(): lax.psum(part_in.astype(jnp.bfloat16), 'rep').astype(jnp.float32)]
    pallas_call x0 -> x12, Pallas kernels: none -> 31.9 us  [the longest x11 18.4 us: call(): pl.pallas_call(kernel, out_shape=out_shape, compiler_params=pltpu.Compile...]
    all_gather x1 -> x0, blocking collectives: 31.6 us -> none  [on_device(): count_table = lax.all_gather(send_counts, 'dp', axis=0, tiled=True)]
    all_to_all x3 -> x0, waiting for transfers between devices: 31.3 us -> none  [the longest x1 25.9 us: on_device(): lax.all_to_all(grad_rows, 'dp', split_axis=0, concat_axis=0, tiled=True)]
    dot_general x11 -> x0, matrix products: 30.5 us -> none  [the longest x3 9.43 us: hstu_layer(): jnp.dot(normalized_input, input_weight_matrix, preferred_element_type=jnp...]
  transfers between devices with their start and end apart: 6 -> 30, of which waited for: 5 -> 11; matrix products, arithmetic and copies ran while one was open for 13% -> 0% of each run, Pallas kernels for 0% -> 10%
where the time goes in v1:
time: 143 us; the launch traced here: 142 us
  starting transfers between devices  57.4 us (40%)
  waiting for transfers between devices  48 us (34%)
  Pallas kernels  31.9 us (22%)
  local copies, waits for them, and re-layouts  4.4 us (3%)
    ppermute x30, starting transfers between devices, swap(): return lax.ppermute(value, axis, [(i, i ^ distance) for i in range(size)])  57.4 us
    ppermute x30, waiting for transfers between devices, swap(): return lax.ppermute(value, axis, [(i, i ^ distance) for i in range(size)])  48 us
    pallas_call x11, Pallas kernels, call(): pl.pallas_call(kernel, out_shape=out_shape, compiler_params=pltpu.Compile...  18.4 us
    pallas_call x1, Pallas kernels, on_device(): pl.pallas_call(backward, out_shape=[square, wide] + block_shapes, scratch...  13.4 us
    unnamed x15, local copies, waits for them, and re-layouts  4.38 us
  transfers between devices with their start and end apart: 30, of which 11 were waited for; matrix products, arithmetic and copies ran while one was open for 0% of the time, Pallas kernels for 10%

profile of v1, /device:TPU:0, one launch (start us, length us, event | category | flops | bytes accessed | tf_op | source)
XLA Modules:
  0.0 142.4 jit_solution(18097254731330921)
XLA Ops:
  0.7 0.8 copy-done.2
  1.5 1.0 copy-done.4
  2.5 0.7 shard_map.86
  3.3 4.1 %collective-permute-start.10 = (bf16[128,512]{1,0:T(8,128)(2,1)S(1)}, bf16[128,512]{1,0:T(8,128)(2,1)S(1)}, u32[]{:S(2)}, u32[]{:S(2)}) collective-permute-start(bf16[128,512]{1,0:T(8,128)(2,1)S(1)} %get-tuple-element.62), channel_id=1, source_target_pairs={{0,16},{4,20},{8,24},{12,28},{16,0},{20,4},{24,8},{28,12},{1,17},{... | collective-permute-start | bytes 393224 | tf_op jit(solution)/shard_map/ppermute | solution.py:319
  7.4 1.3 collective-permute-start.11
  8.6 3.6 %collective-permute-start.12 = (bf16[128,512]{1,0:T(8,128)(2,1)S(1)}, bf16[128,512]{1,0:T(8,128)(2,1)S(1)}, u32[]{:S(2)}, u32[]{:S(2)}) collective-permute-start(bf16[128,512]{1,0:T(8,128)(2,1)S(1)} %get-tuple-element.64), channel_id=1, source_target_pairs={{0,24},{4,28},{8,16},{12,20},{16,8},{20,12},{24,0},{28,4},{1,25},{... | collective-permute-start | bytes 393224 | tf_op jit(solution)/shard_map/ppermute | solution.py:319
  12.2 1.7 %collective-permute-start.7 = (bf16[128,512]{1,0:T(8,128)(2,1)S(1)}, bf16[128,512]{1,0:T(8,128)(2,1)S(1)}, u32[]{:S(2)}, u32[]{:S(2)}) collective-permute-start(bf16[128,512]{1,0:T(8,128)(2,1)S(1)} %get-tuple-element.59), channel_id=1, source_target_pairs={{0,4},{4,0},{8,12},{12,8},{16,20},{20,16},{24,28},{28,24},{1,5},{5... | collective-permute-start | bytes 393224 | tf_op jit(solution)/shard_map/ppermute | solution.py:319
  13.9 1.0 copy-done.5
  14.9 0.7 shard_map.85
  15.7 7.2 %collective-permute-done.10.refs_4_ = bf16[128,512]{1,0:T(8,128)(2,1)S(1)} collective-permute-done((bf16[128,512]{1,0:T(8,128)(2,1)S(1)}, bf16[128,512]{1,0:T(8,128)(2,1)S(1)}, u32[]{:S(2)}, u32[]{:S(2)}) %collective-permute-start.10) | collective-permute-done | bytes 131104 | tf_op jit(solution)/shard_map/ppermute | solution.py:319
  22.9 4.1 %collective-permute-done.11.refs_5_ = bf16[128,512]{1,0:T(8,128)(2,1)S(1)} collective-permute-done((bf16[128,512]{1,0:T(8,128)(2,1)S(1)}, bf16[128,512]{1,0:T(8,128)(2,1)S(1)}, u32[]{:S(2)}, u32[]{:S(2)}) %collective-permute-start.11) | collective-permute-done | bytes 131104 | tf_op jit(solution)/shard_map/ppermute | solution.py:319
  27.0 0.2 collective-permute-start
  27.2 7.0 %collective-permute-start.1 = (bf16[128,512]{1,0:T(8,128)(2,1)S(1)}, bf16[128,512]{1,0:T(8,128)(2,1)S(1)}, u32[]{:S(2)}, u32[]{:S(2)}) collective-permute-start(bf16[128,512]{1,0:T(8,128)(2,1)S(1)} %get-tuple-element.52), channel_id=1, source_target_pairs={{0,8},{4,12},{8,0},{12,4},{16,24},{20,28},{24,16},{28,20},{1,9},{5... | collective-permute-start | bytes 393224 | tf_op jit(solution)/shard_map/ppermute | solution.py:319
  34.2 4.3 %collective-permute-start.3 = (bf16[128,512]{1,0:T(8,128)(2,1)S(1)}, bf16[128,512]{1,0:T(8,128)(2,1)S(1)}, u32[]{:S(2)}, u32[]{:S(2)}) collective-permute-start(bf16[128,512]{1,0:T(8,128)(2,1)S(1)} %get-tuple-element.54), channel_id=1, source_target_pairs={{0,16},{4,20},{8,24},{12,28},{16,0},{20,4},{24,8},{28,12},{1,17},{... | collective-permute-start | bytes 393224 | tf_op jit(solution)/shard_map/ppermute | solution.py:319
  38.5 1.0 collective-permute-start.4
  39.5 2.3 %collective-permute-start.5 = (bf16[128,512]{1,0:T(8,128)(2,1)S(1)}, bf16[128,512]{1,0:T(8,128)(2,1)S(1)}, u32[]{:S(2)}, u32[]{:S(2)}) collective-permute-start(bf16[128,512]{1,0:T(8,128)(2,1)S(1)} %get-tuple-element.56), channel_id=1, source_target_pairs={{0,24},{4,28},{8,16},{12,20},{16,8},{20,12},{24,0},{28,4},{1,25},{... | collective-permute-start | bytes 393224 | tf_op jit(solution)/shard_map/ppermute | solution.py:319
  41.8 1.5 %collective-permute-start.6 = (bf16[128,512]{1,0:T(8,128)(2,1)S(1)}, bf16[128,512]{1,0:T(8,128)(2,1)S(1)}, u32[]{:S(2)}, u32[]{:S(2)}) collective-permute-start(bf16[128,512]{1,0:T(8,128)(2,1)S(1)} %get-tuple-element.57), channel_id=1, source_target_pairs={{0,28},{4,24},{8,20},{12,16},{16,12},{20,8},{24,4},{28,0},{1,29},{... | collective-permute-start | bytes 393224 | tf_op jit(solution)/shard_map/ppermute | solution.py:319
  43.4 0.7 copy-done.6
  44.1 11.6 %shard_map.87 = (bf16[512,1024]{1,0:T(8,128)(2,1)S(1)}, bf16[1024,512]{1,0:T(8,128)(2,1)S(1)}, bf16[512,2048]{1,0:T(8,128)(2,1)S(1)}, bf16[512,2048]{1,0:T(8,128...) custom-call(bf16[128,512]{1,0:T(8,128)(2,1)S(1)} %get-tuple-element., ...), custom_call_target="tpu_custom_call" | custom-call | flops 2013265920 | bytes 19924992 | tf_op jit(solution)/shard_map/pallas_call | solution.py:36
  55.6 1.6 %collective-permute-done.4.refs_5_ = bf16[128,512]{1,0:T(8,128)(2,1)S(1)} collective-permute-done((bf16[128,512]{1,0:T(8,128)(2,1)S(1)}, bf16[128,512]{1,0:T(8,128)(2,1)S(1)}, u32[]{:S(2)}, u32[]{:S(2)}) %collective-permute-start.4) | collective-permute-done | bytes 131104 | tf_op jit(solution)/shard_map/ppermute | solution.py:319
  57.3 13.4 %shard_map.88 = (bf16[512,512]{1,0:T(8,128)(2,1)S(1)}, bf16[512,2048]{1,0:T(8,128)(2,1)S(1)}, bf16[128,512]{1,0:T(8,128)(2,1)S(1)}, bf16[128,512]{1,0:T(8,128)(2...) custom-call(bf16[128,512]{1,0:T(8,128)(2,1)S(1)} %get-tuple-element., ...), custom_call_target="tpu_custom_call" | custom-call | flops 2952790016 | bytes 25165824 | tf_op jit(solution)/shard_map/pallas_call | solution.py:368
  70.7 2.1 %shard_map.91 = (bf16[2,8,320,128]{3,2,1,0:T(8,128)(2,1)S(1)}, bf16[2,8,320,128]{3,2,1,0:T(8,128)(2,1)S(1)}) custom-call(bf16[512,512]{1,0:T(8,128)(2,1)S(1)} %get-tuple-element.85.xhat_t_ref, bf16[512,2048]{1,0:T(8,128)(2,1)S(1)} %get-tuple-element.86.dpre_ref, bf16[512,512]{1,0:T(8,128)(2,1)S(1)} %get-tuple-element.87.gated_t_ref, ...), custom_call_target="tpu_custom_call" | custom-call | flops 1342177280 | bytes 6291456 | tf_op jit(solution)/shard_map/pallas_call | solution.py:36
  72.9 3.0 %collective-permute-done.21.got_ref = bf16[2,8,320,128]{3,2,1,0:T(8,128)(2,1)S(1)} collective-permute-done((bf16[2,8,320,128]{3,2,1,0:T(8,128)(2,1)S(1)}, bf16[2,8,320,128]{3,2,1,0:T(8,128)(2,1)S(1)}, u32[]{:S(2)}, u32[]{:S(2)}) %collective-permute-start.21) | collective-permute-done | bytes 1310752 | tf_op jit(solution)/shard_map/ppermute | solution.py:319
  76.0 0.3 shard_map.92
  76.3 1.6 %collective-permute-start.22 = (bf16[1,8,320,128]{3,2,1,0:T(8,128)(2,1)S(1)}, bf16[1,8,320,128]{3,2,1,0:T(8,128)(2,1)S(1)}, u32[]{:S(2)}, u32[]{:S(2)}) collective-permute-start(bf16[1,8,320,128]{3,2,1,0:T(8,128)(2,1)S(1)} %get-tuple-element.92), channel_id=1, source_target_pairs={{0,2},{1,3},{2,0},{3,1},{4,6},{5,7},{6,4},{7,5},{8,10},{9,11},{10,... | collective-permute-start | bytes 1966088 | tf_op jit(solution)/shard_map/ppermute | solution.py:319
  77.9 15.3 %collective-permute-done.22 = bf16[1,8,320,128]{3,2,1,0:T(8,128)(2,1)S(1)} collective-permute-done((bf16[1,8,320,128]{3,2,1,0:T(8,128)(2,1)S(1)}, bf16[1,8,320,128]{3,2,1,0:T(8,128)(2,1)S(1)}, u32[]{:S(2)}, u32[]{:S(2)}) %collective-permute-start.22) | collective-permute-done | bytes 655392 | tf_op jit(solution)/shard_map/ppermute | solution.py:319
  93.3 1.6 %collective-permute-start.23 = (bf16[4,320,128]{2,1,0:T(8,128)(2,1)S(1)}, bf16[4,320,128]{2,1,0:T(8,128)(2,1)S(1)}, u32[]{:S(2)}, u32[]{:S(2)}) collective-permute-start(bf16[4,320,128]{2,1,0:T(8,128)(2,1)S(1)} %get-tuple-element.94), channel_id=1, source_target_pairs={{0,4},{4,0},{8,12},{12,8},{16,20},{20,16},{24,28},{28,24},{1,5},{5... | collective-permute-start | bytes 983048 | tf_op jit(solution)/shard_map/ppermute | solution.py:319
  94.9 0.4 collective-permute-start.14
  95.4 5.3 %collective-permute-start.15 = (bf16[128,512]{1,0:T(8,128)(2,1)S(1)}, bf16[128,512]{1,0:T(8,128)(2,1)S(1)}, u32[]{:S(2)}, u32[]{:S(2)}) collective-permute-start(bf16[128,512]{1,0:T(8,128)(2,1)S(1)} %get-tuple-element.79), channel_id=1, source_target_pairs={{0,8},{4,12},{8,0},{12,4},{16,24},{20,28},{24,16},{28,20},{1,9},{5... | collective-permute-start | bytes 393224 | tf_op jit(solution)/shard_map/ppermute | solution.py:319
  100.7 3.0 %collective-permute-done.23.refs_1_ = bf16[4,320,128]{2,1,0:T(8,128)(2,1)S(1)} collective-permute-done((bf16[4,320,128]{2,1,0:T(8,128)(2,1)S(1)}, bf16[4,320,128]{2,1,0:T(8,128)(2,1)S(1)}, u32[]{:S(2)}, u32[]{:S(2)}) %collective-permute-start.23) | collective-permute-done | bytes 327712 | tf_op jit(solution)/shard_map/ppermute | solution.py:319
  103.8 5.4 %collective-permute-start.24 = (bf16[320,128]{1,0:T(8,128)(2,1)S(1)}, bf16[320,128]{1,0:T(8,128)(2,1)S(1)}, u32[]{:S(2)}, u32[]{:S(2)}) collective-permute-start(bf16[320,128]{1,0:T(8,128)(2,1)S(1)} %get-tuple-element.102), channel_id=1, source_target_pairs={{0,8},{4,12},{8,0},{12,4},{16,24},{20,28},{24,16},{28,20},{1,9},{5... | collective-permute-start | bytes 245768 | tf_op jit(solution)/shard_map/ppermute | solution.py:319
  109.2 0.9 collective-permute-start.25
  110.0 1.5 %collective-permute-start.26 = (bf16[320,128]{1,0:T(8,128)(2,1)S(1)}, bf16[320,128]{1,0:T(8,128)(2,1)S(1)}, u32[]{:S(2)}, u32[]{:S(2)}) collective-permute-start(bf16[320,128]{1,0:T(8,128)(2,1)S(1)} %get-tuple-element.100), channel_id=1, source_target_pairs={{0,24},{4,28},{8,16},{12,20},{16,8},{20,12},{24,0},{28,4},{1,25},{... | collective-permute-start | bytes 245768 | tf_op jit(solution)/shard_map/ppermute | solution.py:319
  111.6 1.4 collective-permute-start.16
  113.0 1.5 %collective-permute-start.17 = (bf16[128,512]{1,0:T(8,128)(2,1)S(1)}, bf16[128,512]{1,0:T(8,128)(2,1)S(1)}, u32[]{:S(2)}, u32[]{:S(2)}) collective-permute-start(bf16[128,512]{1,0:T(8,128)(2,1)S(1)} %get-tuple-element.81), channel_id=1, source_target_pairs={{0,16},{4,20},{8,24},{12,28},{16,0},{20,4},{24,8},{28,12},{1,17},{... | collective-permute-start | bytes 393224 | tf_op jit(solution)/shard_map/ppermute | solution.py:319
  114.5 0.3 collective-permute-done.24.refs_1_
  114.8 1.7 %collective-permute-start.18 = (bf16[128,512]{1,0:T(8,128)(2,1)S(1)}, bf16[128,512]{1,0:T(8,128)(2,1)S(1)}, u32[]{:S(2)}, u32[]{:S(2)}) collective-permute-start(bf16[128,512]{1,0:T(8,128)(2,1)S(1)} %get-tuple-element.82), channel_id=1, source_target_pairs={{0,20},{4,16},{8,28},{12,24},{16,4},{20,0},{24,12},{28,8},{1,21},{... | collective-permute-start | bytes 393224 | tf_op jit(solution)/shard_map/ppermute | solution.py:319
  116.5 4.1 %collective-permute-done.25.refs_2_ = bf16[320,128]{1,0:T(8,128)(2,1)S(1)} collective-permute-done((bf16[320,128]{1,0:T(8,128)(2,1)S(1)}, bf16[320,128]{1,0:T(8,128)(2,1)S(1)}, u32[]{:S(2)}, u32[]{:S(2)}) %collective-permute-start.25) | collective-permute-done | bytes 81952 | tf_op jit(solution)/shard_map/ppermute | solution.py:319
  120.6 7.0 %collective-permute-start.19 = (bf16[128,512]{1,0:T(8,128)(2,1)S(1)}, bf16[128,512]{1,0:T(8,128)(2,1)S(1)}, u32[]{:S(2)}, u32[]{:S(2)}) collective-permute-start(bf16[128,512]{1,0:T(8,128)(2,1)S(1)} %get-tuple-element.83), channel_id=1, source_target_pairs={{0,24},{4,28},{8,16},{12,20},{16,8},{20,12},{24,0},{28,4},{1,25},{... | collective-permute-start | bytes 393224 | tf_op jit(solution)/shard_map/ppermute | solution.py:319
  127.6 0.4 collective-permute-start.20
  128.1 3.5 %collective-permute-done.17.refs_4_ = bf16[128,512]{1,0:T(8,128)(2,1)S(1)} collective-permute-done((bf16[128,512]{1,0:T(8,128)(2,1)S(1)}, bf16[128,512]{1,0:T(8,128)(2,1)S(1)}, u32[]{:S(2)}, u32[]{:S(2)}) %collective-permute-start.17) | collective-permute-done | bytes 131104 | tf_op jit(solution)/shard_map/ppermute | solution.py:319
  131.6 1.5 %collective-permute-start.28 = (bf16[320,128]{1,0:T(8,128)(2,1)S(1)}, bf16[320,128]{1,0:T(8,128)(2,1)S(1)}, u32[]{:S(2)}, u32[]{:S(2)}) collective-permute-start(bf16[320,128]{1,0:T(8,128)(2,1)S(1)} %shard_map.95.refs_0_), channel_id=1, source_target_pairs={{0,2},{1,3},{2,0},{3,1},{4,6},{5,7},{6,4},{7,5},{8,10},{9,11},{10,... | collective-permute-start | bytes 245768 | tf_op jit(solution)/shard_map/ppermute | solution.py:319
  133.1 3.1 %collective-permute-done.18.refs_5_ = bf16[128,512]{1,0:T(8,128)(2,1)S(1)} collective-permute-done((bf16[128,512]{1,0:T(8,128)(2,1)S(1)}, bf16[128,512]{1,0:T(8,128)(2,1)S(1)}, u32[]{:S(2)}, u32[]{:S(2)}) %collective-permute-start.18) | collective-permute-done | bytes 131104 | tf_op jit(solution)/shard_map/ppermute | solution.py:319
  136.2 0.3 shard_map.89.refs_8_
  136.5 1.5 %shard_map.90 = bf16[512,512]{1,0:T(8,128)(2,1)} custom-call(bf16[128,512]{1,0:T(8,128)(2,1)S(1)} %get-tuple-element.77.refs_0_, bf16[128,512]{1,0:T(8,128)(2,1)S(1)} %collective-permute-done.14.refs_1_, bf16[128,512]{1,0:T(8,128)(2,1)S(1)} %collective-permute-done.15.refs_2_, bf16[128,512]{1,0:T(8,128)(2,1)S(1)} %collective-permute-done.16.refs_3_, ...), custom_call_target="tpu_custom_call" | custom-call | flops 536870912 | bytes 2621440 | tf_op jit(solution)/shard_map/pallas_call | solution.py:36
  138.0 2.8 %collective-permute-done.29.refs_3_ = bf16[320,128]{1,0:T(8,128)(2,1)S(1)} collective-permute-done((bf16[320,128]{1,0:T(8,128)(2,1)S(1)}, bf16[320,128]{1,0:T(8,128)(2,1)S(1)}, u32[]{:S(2)}, u32[]{:S(2)}) %collective-permute-start.29) | collective-permute-done | bytes 81952 | tf_op jit(solution)/shard_map/ppermute | solution.py:319
  140.8 0.8 shard_map.96
  141.7 0.8 copy.9
  (40 shorter events, 0.5 us)
Async XLA Ops:
  0.6 42.7 %copy-start = (bf16[512,2048]{1,0:T(8,128)(2,1)S(1)}, bf16[512,2048]{1,0:T(8,128)(2,1)}, u32[]{:S(2)}) copy-start(bf16[512,2048]{1,0:T(8,128)(2,1)} %refs_19_.1) | copy-start | bytes 6291460
  0.6 0.8 copy-start.2
  1.5 1.0 copy-start.4
  3.3 19.7 %collective-permute-start.10 = (bf16[128,512]{1,0:T(8,128)(2,1)S(1)}, bf16[128,512]{1,0:T(8,128)(2,1)S(1)}, u32[]{:S(2)}, u32[]{:S(2)}) collective-permute-start(bf16[128,512]{1,0:T(8,128)(2,1)S(1)} %get-tuple-element.62), channel_id=1, source_target_pairs={{0,16},{4,20},{8,24},{12,28},{16,0},{20,4},{24,8},{28,12},{1,17},{... | collective-permute-start | bytes 393224 | tf_op jit(solution)/shard_map/ppermute | solution.py:319
  7.4 19.6 %collective-permute-start.11 = (bf16[128,512]{1,0:T(8,128)(2,1)S(1)}, bf16[128,512]{1,0:T(8,128)(2,1)S(1)}, u32[]{:S(2)}, u32[]{:S(2)}) collective-permute-start(bf16[128,512]{1,0:T(8,128)(2,1)S(1)} %get-tuple-element.63), channel_id=1, source_target_pairs={{0,20},{4,16},{8,28},{12,24},{16,4},{20,0},{24,12},{28,8},{1,21},{... | collective-permute-start | bytes 393224 | tf_op jit(solution)/shard_map/ppermute | solution.py:319
  8.6 18.4 %collective-permute-start.12 = (bf16[128,512]{1,0:T(8,128)(2,1)S(1)}, bf16[128,512]{1,0:T(8,128)(2,1)S(1)}, u32[]{:S(2)}, u32[]{:S(2)}) collective-permute-start(bf16[128,512]{1,0:T(8,128)(2,1)S(1)} %get-tuple-element.64), channel_id=1, source_target_pairs={{0,24},{4,28},{8,16},{12,20},{16,8},{20,12},{24,0},{28,4},{1,25},{... | collective-permute-start | bytes 393224 | tf_op jit(solution)/shard_map/ppermute | solution.py:319
  12.2 15.0 %collective-permute-start.13 = (bf16[128,512]{1,0:T(8,128)(2,1)S(1)}, bf16[128,512]{1,0:T(8,128)(2,1)S(1)}, u32[]{:S(2)}, u32[]{:S(2)}) collective-permute-start(bf16[128,512]{1,0:T(8,128)(2,1)S(1)} %get-tuple-element.65), channel_id=1, source_target_pairs={{0,28},{4,24},{8,20},{12,16},{16,12},{20,8},{24,4},{28,0},{1,29},{... | collective-permute-start | bytes 393224 | tf_op jit(solution)/shard_map/ppermute | solution.py:319
  12.2 22.0 %collective-permute-start.7 = (bf16[128,512]{1,0:T(8,128)(2,1)S(1)}, bf16[128,512]{1,0:T(8,128)(2,1)S(1)}, u32[]{:S(2)}, u32[]{:S(2)}) collective-permute-start(bf16[128,512]{1,0:T(8,128)(2,1)S(1)} %get-tuple-element.59), channel_id=1, source_target_pairs={{0,4},{4,0},{8,12},{12,8},{16,20},{20,16},{24,28},{28,24},{1,5},{5... | collective-permute-start | bytes 393224 | tf_op jit(solution)/shard_map/ppermute | solution.py:319
  13.9 1.0 copy-start.5
  22.9 11.3 %collective-permute-start.8 = (bf16[128,512]{1,0:T(8,128)(2,1)S(1)}, bf16[128,512]{1,0:T(8,128)(2,1)S(1)}, u32[]{:S(2)}, u32[]{:S(2)}) collective-permute-start(bf16[128,512]{1,0:T(8,128)(2,1)S(1)} %get-tuple-element.60), channel_id=1, source_target_pairs={{0,8},{4,12},{8,0},{12,4},{16,24},{20,28},{24,16},{28,20},{1,9},{5... | collective-permute-start | bytes 393224 | tf_op jit(solution)/shard_map/ppermute | solution.py:319
  27.0 11.5 %collective-permute-start.9 = (bf16[128,512]{1,0:T(8,128)(2,1)S(1)}, bf16[128,512]{1,0:T(8,128)(2,1)S(1)}, u32[]{:S(2)}, u32[]{:S(2)}) collective-permute-start(bf16[128,512]{1,0:T(8,128)(2,1)S(1)} %get-tuple-element.61), channel_id=1, source_target_pairs={{0,12},{4,8},{8,4},{12,0},{16,28},{20,24},{24,20},{28,16},{1,13},{... | collective-permute-start | bytes 393224 | tf_op jit(solution)/shard_map/ppermute | solution.py:319
  27.0 12.5 %collective-permute-start = (bf16[128,512]{1,0:T(8,128)(2,1)S(1)}, bf16[128,512]{1,0:T(8,128)(2,1)S(1)}, u32[]{:S(2)}, u32[]{:S(2)}) collective-permute-start(bf16[128,512]{1,0:T(8,128)(2,1)S(1)} %get-tuple-element.51), channel_id=1, source_target_pairs={{0,4},{4,0},{8,12},{12,8},{16,20},{20,16},{24,28},{28,24},{1,5},{5... | collective-permute-start | bytes 393224 | tf_op jit(solution)/shard_map/ppermute | solution.py:319
  27.2 14.6 %collective-permute-start.1 = (bf16[128,512]{1,0:T(8,128)(2,1)S(1)}, bf16[128,512]{1,0:T(8,128)(2,1)S(1)}, u32[]{:S(2)}, u32[]{:S(2)}) collective-permute-start(bf16[128,512]{1,0:T(8,128)(2,1)S(1)} %get-tuple-element.52), channel_id=1, source_target_pairs={{0,8},{4,12},{8,0},{12,4},{16,24},{20,28},{24,16},{28,20},{1,9},{5... | collective-permute-start | bytes 393224 | tf_op jit(solution)/shard_map/ppermute | solution.py:319
  34.2 21.4 %collective-permute-start.2 = (bf16[128,512]{1,0:T(8,128)(2,1)S(1)}, bf16[128,512]{1,0:T(8,128)(2,1)S(1)}, u32[]{:S(2)}, u32[]{:S(2)}) collective-permute-start(bf16[128,512]{1,0:T(8,128)(2,1)S(1)} %get-tuple-element.53), channel_id=1, source_target_pairs={{0,12},{4,8},{8,4},{12,0},{16,28},{20,24},{24,20},{28,16},{1,13},{... | collective-permute-start | bytes 393224 | tf_op jit(solution)/shard_map/ppermute | solution.py:319
  34.2 21.4 %collective-permute-start.3 = (bf16[128,512]{1,0:T(8,128)(2,1)S(1)}, bf16[128,512]{1,0:T(8,128)(2,1)S(1)}, u32[]{:S(2)}, u32[]{:S(2)}) collective-permute-start(bf16[128,512]{1,0:T(8,128)(2,1)S(1)} %get-tuple-element.54), channel_id=1, source_target_pairs={{0,16},{4,20},{8,24},{12,28},{16,0},{20,4},{24,8},{28,12},{1,17},{... | collective-permute-start | bytes 393224 | tf_op jit(solution)/shard_map/ppermute | solution.py:319
  38.5 18.7 %collective-permute-start.4 = (bf16[128,512]{1,0:T(8,128)(2,1)S(1)}, bf16[128,512]{1,0:T(8,128)(2,1)S(1)}, u32[]{:S(2)}, u32[]{:S(2)}) collective-permute-start(bf16[128,512]{1,0:T(8,128)(2,1)S(1)} %get-tuple-element.55), channel_id=1, source_target_pairs={{0,20},{4,16},{8,28},{12,24},{16,4},{20,0},{24,12},{28,8},{1,21},{... | collective-permute-start | bytes 393224 | tf_op jit(solution)/shard_map/ppermute | solution.py:319
  39.5 17.7 %collective-permute-start.5 = (bf16[128,512]{1,0:T(8,128)(2,1)S(1)}, bf16[128,512]{1,0:T(8,128)(2,1)S(1)}, u32[]{:S(2)}, u32[]{:S(2)}) collective-permute-start(bf16[128,512]{1,0:T(8,128)(2,1)S(1)} %get-tuple-element.56), channel_id=1, source_target_pairs={{0,24},{4,28},{8,16},{12,20},{16,8},{20,12},{24,0},{28,4},{1,25},{... | collective-permute-start | bytes 393224 | tf_op jit(solution)/shard_map/ppermute | solution.py:319
  41.8 15.4 %collective-permute-start.6 = (bf16[128,512]{1,0:T(8,128)(2,1)S(1)}, bf16[128,512]{1,0:T(8,128)(2,1)S(1)}, u32[]{:S(2)}, u32[]{:S(2)}) collective-permute-start(bf16[128,512]{1,0:T(8,128)(2,1)S(1)} %get-tuple-element.57), channel_id=1, source_target_pairs={{0,28},{4,24},{8,20},{12,16},{16,12},{20,8},{24,4},{28,0},{1,29},{... | collective-permute-start | bytes 393224 | tf_op jit(solution)/shard_map/ppermute | solution.py:319
  43.4 0.7 copy-start.6
  44.0 13.2 %copy-start.1 = (bf16[512,512]{1,0:T(8,128)(2,1)S(1)}, bf16[512,512]{1,0:T(8,128)(2,1)}, u32[]{:S(2)}) copy-start(bf16[512,512]{1,0:T(8,128)(2,1)} %refs_20_.1) | copy-start | bytes 1572868
  72.9 3.1 %collective-permute-start.21 = (bf16[2,8,320,128]{3,2,1,0:T(8,128)(2,1)S(1)}, bf16[2,8,320,128]{3,2,1,0:T(8,128)(2,1)S(1)}, u32[]{:S(2)}, u32[]{:S(2)}) collective-permute-start(bf16[2,8,320,128]{3,2,1,0:T(8,128)(2,1)S(1)} %get-tuple-element.90), channel_id=1, source_target_pairs={{0,1},{1,0},{2,3},{3,2},{4,5},{5,4},{6,7},{7,6},{8,9},{9,8},{10,11... | collective-permute-start | bytes 3932168 | tf_op jit(solution)/shard_map/ppermute | solution.py:319
  76.3 59.9 %copy-start.3 = (s32[1,512]{1,0:T(1,128)S(1)}, s32[1,512]{1,0:T(1,128)}, u32[]{:S(2)}) copy-start(s32[1,512]{1,0:T(1,128)} %place_ref.5) | copy-start | bytes 6148
  76.3 16.8 %collective-permute-start.22 = (bf16[1,8,320,128]{3,2,1,0:T(8,128)(2,1)S(1)}, bf16[1,8,320,128]{3,2,1,0:T(8,128)(2,1)S(1)}, u32[]{:S(2)}, u32[]{:S(2)}) collective-permute-start(bf16[1,8,320,128]{3,2,1,0:T(8,128)(2,1)S(1)} %get-tuple-element.92), channel_id=1, source_target_pairs={{0,2},{1,3},{2,0},{3,1},{4,6},{5,7},{6,4},{7,5},{8,10},{9,11},{10,... | collective-permute-start | bytes 1966088 | tf_op jit(solution)/shard_map/ppermute | solution.py:319
  93.3 10.4 %collective-permute-start.23 = (bf16[4,320,128]{2,1,0:T(8,128)(2,1)S(1)}, bf16[4,320,128]{2,1,0:T(8,128)(2,1)S(1)}, u32[]{:S(2)}, u32[]{:S(2)}) collective-permute-start(bf16[4,320,128]{2,1,0:T(8,128)(2,1)S(1)} %get-tuple-element.94), channel_id=1, source_target_pairs={{0,4},{4,0},{8,12},{12,8},{16,20},{20,16},{24,28},{28,24},{1,5},{5... | collective-permute-start | bytes 983048 | tf_op jit(solution)/shard_map/ppermute | solution.py:319
  94.9 16.7 %collective-permute-start.14 = (bf16[128,512]{1,0:T(8,128)(2,1)S(1)}, bf16[128,512]{1,0:T(8,128)(2,1)S(1)}, u32[]{:S(2)}, u32[]{:S(2)}) collective-permute-start(bf16[128,512]{1,0:T(8,128)(2,1)S(1)} %get-tuple-element.78), channel_id=1, source_target_pairs={{0,4},{4,0},{8,12},{12,8},{16,20},{20,16},{24,28},{28,24},{1,5},{5... | collective-permute-start | bytes 393224 | tf_op jit(solution)/shard_map/ppermute | solution.py:319
  95.4 17.6 %collective-permute-start.15 = (bf16[128,512]{1,0:T(8,128)(2,1)S(1)}, bf16[128,512]{1,0:T(8,128)(2,1)S(1)}, u32[]{:S(2)}, u32[]{:S(2)}) collective-permute-start(bf16[128,512]{1,0:T(8,128)(2,1)S(1)} %get-tuple-element.79), channel_id=1, source_target_pairs={{0,8},{4,12},{8,0},{12,4},{16,24},{20,28},{24,16},{28,20},{1,9},{5... | collective-permute-start | bytes 393224 | tf_op jit(solution)/shard_map/ppermute | solution.py:319
  103.8 11.0 %collective-permute-start.24 = (bf16[320,128]{1,0:T(8,128)(2,1)S(1)}, bf16[320,128]{1,0:T(8,128)(2,1)S(1)}, u32[]{:S(2)}, u32[]{:S(2)}) collective-permute-start(bf16[320,128]{1,0:T(8,128)(2,1)S(1)} %get-tuple-element.102), channel_id=1, source_target_pairs={{0,8},{4,12},{8,0},{12,4},{16,24},{20,28},{24,16},{28,20},{1,9},{5... | collective-permute-start | bytes 245768 | tf_op jit(solution)/shard_map/ppermute | solution.py:319
  109.2 11.4 %collective-permute-start.25 = (bf16[320,128]{1,0:T(8,128)(2,1)S(1)}, bf16[320,128]{1,0:T(8,128)(2,1)S(1)}, u32[]{:S(2)}, u32[]{:S(2)}) collective-permute-start(bf16[320,128]{1,0:T(8,128)(2,1)S(1)} %get-tuple-element.101), channel_id=1, source_target_pairs={{0,16},{4,20},{8,24},{12,28},{16,0},{20,4},{24,8},{28,12},{1,17},{... | collective-permute-start | bytes 245768 | tf_op jit(solution)/shard_map/ppermute | solution.py:319
  110.0 17.6 %collective-permute-start.26 = (bf16[320,128]{1,0:T(8,128)(2,1)S(1)}, bf16[320,128]{1,0:T(8,128)(2,1)S(1)}, u32[]{:S(2)}, u32[]{:S(2)}) collective-permute-start(bf16[320,128]{1,0:T(8,128)(2,1)S(1)} %get-tuple-element.100), channel_id=1, source_target_pairs={{0,24},{4,28},{8,16},{12,20},{16,8},{20,12},{24,0},{28,4},{1,25},{... | collective-permute-start | bytes 245768 | tf_op jit(solution)/shard_map/ppermute | solution.py:319
  111.6 16.4 %collective-permute-start.16 = (bf16[128,512]{1,0:T(8,128)(2,1)S(1)}, bf16[128,512]{1,0:T(8,128)(2,1)S(1)}, u32[]{:S(2)}, u32[]{:S(2)}) collective-permute-start(bf16[128,512]{1,0:T(8,128)(2,1)S(1)} %get-tuple-element.80), channel_id=1, source_target_pairs={{0,12},{4,8},{8,4},{12,0},{16,28},{20,24},{24,20},{28,16},{1,13},{... | collective-permute-start | bytes 393224 | tf_op jit(solution)/shard_map/ppermute | solution.py:319
  113.0 18.6 %collective-permute-start.17 = (bf16[128,512]{1,0:T(8,128)(2,1)S(1)}, bf16[128,512]{1,0:T(8,128)(2,1)S(1)}, u32[]{:S(2)}, u32[]{:S(2)}) collective-permute-start(bf16[128,512]{1,0:T(8,128)(2,1)S(1)} %get-tuple-element.81), channel_id=1, source_target_pairs={{0,16},{4,20},{8,24},{12,28},{16,0},{20,4},{24,8},{28,12},{1,17},{... | collective-permute-start | bytes 393224 | tf_op jit(solution)/shard_map/ppermute | solution.py:319
  114.8 21.4 %collective-permute-start.18 = (bf16[128,512]{1,0:T(8,128)(2,1)S(1)}, bf16[128,512]{1,0:T(8,128)(2,1)S(1)}, u32[]{:S(2)}, u32[]{:S(2)}) collective-permute-start(bf16[128,512]{1,0:T(8,128)(2,1)S(1)} %get-tuple-element.82), channel_id=1, source_target_pairs={{0,20},{4,16},{8,28},{12,24},{16,4},{20,0},{24,12},{28,8},{1,21},{... | collective-permute-start | bytes 393224 | tf_op jit(solution)/shard_map/ppermute | solution.py:319
  120.6 15.9 %collective-permute-start.19 = (bf16[128,512]{1,0:T(8,128)(2,1)S(1)}, bf16[128,512]{1,0:T(8,128)(2,1)S(1)}, u32[]{:S(2)}, u32[]{:S(2)}) collective-permute-start(bf16[128,512]{1,0:T(8,128)(2,1)S(1)} %get-tuple-element.83), channel_id=1, source_target_pairs={{0,24},{4,28},{8,16},{12,20},{16,8},{20,12},{24,0},{28,4},{1,25},{... | collective-permute-start | bytes 393224 | tf_op jit(solution)/shard_map/ppermute | solution.py:319
  127.6 8.9 %collective-permute-start.20 = (bf16[128,512]{1,0:T(8,128)(2,1)S(1)}, bf16[128,512]{1,0:T(8,128)(2,1)S(1)}, u32[]{:S(2)}, u32[]{:S(2)}) collective-permute-start(bf16[128,512]{1,0:T(8,128)(2,1)S(1)} %get-tuple-element.84), channel_id=1, source_target_pairs={{0,28},{4,24},{8,20},{12,16},{16,12},{20,8},{24,4},{28,0},{1,29},{... | collective-permute-start | bytes 393224 | tf_op jit(solution)/shard_map/ppermute | solution.py:319
  128.0 10.0 %collective-permute-start.27 = (bf16[320,128]{1,0:T(8,128)(2,1)S(1)}, bf16[320,128]{1,0:T(8,128)(2,1)S(1)}, u32[]{:S(2)}, u32[]{:S(2)}) collective-permute-start(bf16[320,128]{1,0:T(8,128)(2,1)S(1)} %shard_map.95.refs_0_), channel_id=1, source_target_pairs={{0,1},{1,0},{2,3},{3,2},{4,5},{5,4},{6,7},{7,6},{8,9},{9,8},{10,11... | collective-permute-start | bytes 245768 | tf_op jit(solution)/shard_map/ppermute | solution.py:319
  131.6 6.4 %collective-permute-start.28 = (bf16[320,128]{1,0:T(8,128)(2,1)S(1)}, bf16[320,128]{1,0:T(8,128)(2,1)S(1)}, u32[]{:S(2)}, u32[]{:S(2)}) collective-permute-start(bf16[320,128]{1,0:T(8,128)(2,1)S(1)} %shard_map.95.refs_0_), channel_id=1, source_target_pairs={{0,2},{1,3},{2,0},{3,1},{4,6},{5,7},{6,4},{7,5},{8,10},{9,11},{10,... | collective-permute-start | bytes 245768 | tf_op jit(solution)/shard_map/ppermute | solution.py:319
  136.2 4.7 %collective-permute-start.29 = (bf16[320,128]{1,0:T(8,128)(2,1)S(1)}, bf16[320,128]{1,0:T(8,128)(2,1)S(1)}, u32[]{:S(2)}, u32[]{:S(2)}) collective-permute-start(bf16[320,128]{1,0:T(8,128)(2,1)S(1)} %shard_map.95.refs_0_), channel_id=1, source_target_pairs={{0,3},{1,2},{2,1},{3,0},{4,7},{5,6},{6,5},{7,4},{8,11},{9,10},{10,... | collective-permute-start | bytes 245768 | tf_op jit(solution)/shard_map/ppermute | solution.py:319

commit v2 on v1

v2 whole, which is shorter than its diff:
```python
import functools

import jax
import jax.numpy as jnp
from jax import lax
from jax.experimental import pallas as pl
from jax.experimental.pallas import tpu as pltpu
from jax.sharding import PartitionSpec as P

HEADS = 8
LONGEST = 256
EPSILON = 1e-05
EMPTY = 128.0
BLOCK = 128
QUERIES = 256
LANES = 128
F32 = jnp.float32
BF16 = jnp.bfloat16


def dot(a, b):
    return jnp.dot(a, b, preferred_element_type=F32)


def dot_nt(a, b):
    return lax.dot_general(a, b, (((1,), (1,)), ((), ())), preferred_element_type=F32)


def iota(shape, dim):
    return lax.broadcasted_iota(jnp.int32, shape, dim)


def call(kernel, out_shape, *args, flops=0, transcendentals=0, scratch=(), vmem=16):
    moved = sum(a.size * a.dtype.itemsize for a in args)
    moved += sum(o.size * o.dtype.itemsize for o in jax.tree.leaves(out_shape))
    return pl.pallas_call(
        kernel,
        out_shape=out_shape,
        scratch_shapes=scratch,
        compiler_params=pltpu.CompilerParams(vmem_limit_bytes=vmem * 1024 * 1024),
        cost_estimate=pl.CostEstimate(
            flops=flops, bytes_accessed=moved, transcendentals=transcendentals
        ),
    )(*args)


def shape(dims, dtype=BF16):
    return jax.ShapeDtypeStruct(tuple(dims), dtype)


def spread_kernel(owners, capacity, mark, place_ref, rows_ref, *out_refs):
    me = lax.axis_index("dp")
    place = place_ref[...]
    rows = rows_ref[...]
    count = rows.shape[0]
    for k in range(owners):
        first = (me ^ k) * capacity
        onehot = (iota((capacity, count), 0) + first == place).astype(F32)
        block = dot(onehot.astype(BF16), rows)
        if mark:
            filled = jnp.sum(onehot, axis=1, keepdims=True)
            block = block + (1.0 - filled) * EMPTY
        out_refs[k][...] = block.astype(BF16)


def lookup_kernel(place_ref, out_ref):
    count = place_ref.shape[1]
    column = jnp.broadcast_to(place_ref[...].astype(F32), (LANES, count)).T[:, 0:1].astype(jnp.int32)
    out_ref[...] = (iota(out_ref.shape, 1) == column).astype(F32).astype(BF16)


def key_range(i):
    return max(0, (i * QUERIES - LONGEST + 1) // QUERIES) * QUERIES, (i + 1) * QUERIES


def by_head(rows, lane, half):
    heads = range(LANES // half)
    return jnp.concatenate(
        [jnp.where(lane // half == h, rows, jnp.zeros_like(rows)) for h in heads], axis=0
    )


def own_head(rows, lane, half):
    total = rows[:QUERIES]
    for h in range(1, LANES // half):
        total = jnp.where(lane // half == h, rows[h * QUERIES : (h + 1) * QUERIES], total)
    return total


def forward_kernel(owners, capacity, *refs):
    blocks = refs[:owners]
    users_ref, w_ref = refs[owners : owners + 2]
    (
        place_ref, unplace_ref, act_ref, slope_ref, xhat_ref, xhat_t_ref, x_rstd_ref,
        weights_ref, tangent_ref, nhat_ref, a_rstd_ref, gated_t_ref, q_t_ref, att_ref,
    ) = refs[owners + 2 :]
    me = lax.axis_index("dp")
    count, width = xhat_ref.shape
    half = width // HEADS
    valid = [blocks[k][:, 0:LANES].astype(F32) != EMPTY for k in range(owners)]
    counts = [jnp.sum(v.astype(F32), axis=0, keepdims=True) for v in valid]
    source = iota((owners, LANES), 0) ^ me
    starts = jnp.zeros((owners, LANES), F32)
    for k in range(owners):
        starts = starts + jnp.where(source > (me ^ k), counts[k], 0.0)
    within = iota((capacity, LANES), 0).astype(F32)
    target = jnp.concatenate(
        [jnp.where(valid[k], starts[k : k + 1] + within, -1.0) for k in range(owners)], axis=0
    )
    target_t = target.T[0:1, :]
    slots = owners * capacity
    place = (iota((count, slots), 0) == target_t.astype(jnp.int32)).astype(F32).astype(BF16)
    place_ref[...] = place
    column = target[:, 0:1].astype(jnp.int32)
    unplace_ref[...] = (iota((slots, count), 1) == column).astype(F32).astype(BF16)
    received = jnp.concatenate([blocks[k][...] for k in range(owners)], axis=0)
    x = dot(place, received)
    center = x - jnp.mean(x, axis=1, keepdims=True)
    rstd = lax.rsqrt(jnp.mean(center * center, axis=1, keepdims=True) + EPSILON)
    xhat32 = center * rstd
    xhat = xhat32.astype(BF16)
    xhat_ref[...] = xhat
    xhat_t_ref[...] = xhat32.T.astype(BF16)
    x_rstd_ref[...] = jnp.broadcast_to(rstd, (count, LANES))
    for part in range(4):
        columns = slice(part * width, (part + 1) * width)
        pre = dot(xhat, w_ref[:, columns])
        sig = 0.5 * jnp.tanh(0.5 * pre) + 0.5
        act = pre * sig
        act_ref[:, columns] = act.astype(BF16)
        slope_ref[:, columns] = (sig + act * (1.0 - sig)).astype(BF16)
        if part == 2:
            q_t_ref[...] = act.T.astype(BF16)
    users = users_ref[...]
    users_column = jnp.broadcast_to(users.astype(F32), (LANES, count)).T[:, 0:1].astype(jnp.int32)
    scale = half ** (-0.5)
    lane = iota((QUERIES, LANES), 1)
    for i in range(count // QUERIES):
        low, high = key_range(i)
        rows = slice(i * QUERIES, high)
        keep = (users_column[rows] == users[:, low:high]) & (
            iota((QUERIES, high - low), 1) + low <= iota((QUERIES, high - low), 0) + i * QUERIES
        )
        for pair in range(width // LANES):
            lanes = slice(pair * LANES, (pair + 1) * LANES)
            v = act_ref[low:high, width + lanes.start : width + lanes.stop]
            q = act_ref[rows, 2 * width + lanes.start : 2 * width + lanes.stop]
            k = act_ref[low:high, 3 * width + lanes.start : 3 * width + lanes.stop]
            scores = dot_nt(by_head(q, lane, half), k)
            weights = []
            for inner in range(LANES // half):
                head = pair * (LANES // half) + inner
                for r in range(0, QUERIES, BLOCK):
                    for c in range(low, high, BLOCK):
                        at = (slice(r, r + BLOCK), slice(c - low, c - low + BLOCK))
                        first = i * QUERIES + r
                        if c > first or c + LONGEST < first:
                            weights_ref[(head, i) + at] = jnp.zeros((BLOCK, BLOCK), BF16)
                            tangent_ref[(head, i) + at] = jnp.zeros((BLOCK, BLOCK), BF16)
                            continue
                        score = scores[inner * QUERIES + r : inner * QUERIES + r + BLOCK, at[1]]
                        sig = 0.5 * jnp.tanh(score * (0.5 * scale)) + 0.5
                        value = score * scale * sig
                        slope = (sig + value * (1.0 - sig)) * scale
                        weights_ref[(head, i) + at] = jnp.where(keep[at], value, 0.0).astype(BF16)
                        tangent_ref[(head, i) + at] = jnp.where(keep[at], slope, 0.0).astype(BF16)
                weights.append(weights_ref[head, i, :, 0 : high - low])
            att_ref[rows, lanes] = own_head(dot(jnp.concatenate(weights, axis=0), v), lane, half)
    attended = att_ref[...]
    center = attended - jnp.mean(attended, axis=1, keepdims=True)
    rstd = lax.rsqrt(jnp.mean(center * center, axis=1, keepdims=True) + EPSILON)
    nhat = center * rstd
    nhat_ref[...] = nhat.astype(BF16)
    a_rstd_ref[...] = jnp.broadcast_to(rstd, (count, LANES))
    gated_t_ref[...] = (nhat * act_ref[:, 0:width].astype(F32)).T.astype(BF16)


def fold(piece):
    rows, columns = piece.shape
    if columns >= LANES:
        return jnp.concatenate(
            [piece[:, c : c + LANES] for c in range(0, columns, LANES)], axis=0
        )
    step = rows * columns // LANES
    return jnp.concatenate([piece[r : r + step] for r in range(0, rows, step)], axis=1)


def unfold(piece, rows, columns):
    if columns >= LANES:
        return jnp.concatenate(
            [piece[r : r + rows] for r in range(0, piece.shape[0], rows)], axis=1
        )
    return jnp.concatenate(
        [piece[:, c : c + columns] for c in range(0, LANES, columns)], axis=0
    )


def backward_kernel(owners, *refs):
    blocks = refs[:owners]
    (
        place_ref, act_ref, slope_ref, nhat_ref, a_rstd_ref, weights_ref, tangent_ref, q_t_ref,
        w_out_ref, dy_ref, dpre_ref, datt_ref, datt_t_ref, dkv_t_ref,
    ) = refs[owners:]
    count, width = dy_ref.shape
    half = width // HEADS
    received = jnp.concatenate([blocks[k][...] for k in range(owners)], axis=0)
    dy = dot(place_ref[...], received).astype(BF16)
    dy_ref[...] = dy
    dgated = dot_nt(dy, w_out_ref[...])
    nhat = nhat_ref[...].astype(F32)
    dpre_ref[:, 0:width] = (dgated * nhat * slope_ref[:, 0:width].astype(F32)).astype(BF16)
    dnhat = dgated * act_ref[:, 0:width].astype(F32)
    datt = a_rstd_ref[:, 0:1] * (
        dnhat
        - jnp.mean(dnhat, axis=1, keepdims=True)
        - nhat * jnp.mean(dnhat * nhat, axis=1, keepdims=True)
    )
    datt_ref[...] = datt.astype(BF16)
    datt_t_ref[...] = datt.T.astype(BF16)
    lane = iota((QUERIES, LANES), 1)
    steps = count // QUERIES
    heads = LANES // half
    for pair in range(width // LANES):
        lanes = slice(pair * LANES, (pair + 1) * LANES)
        dq = []
        dk_t = [[None] * steps for _ in range(heads)]
        dv_t = [[None] * steps for _ in range(heads)]
        for i in range(steps):
            low, high = key_range(i)
            rows = slice(i * QUERIES, high)
            v = act_ref[low:high, width + lanes.start : width + lanes.stop]
            k = act_ref[low:high, 3 * width + lanes.start : 3 * width + lanes.stop]
            dweight = dot_nt(by_head(datt_ref[rows, lanes], lane, half), v)
            dscore = []
            for inner in range(heads):
                head = pair * heads + inner
                own = slice(head * half, (head + 1) * half)
                tangent = tangent_ref[head, i, :, 0 : high - low].astype(F32)
                one = (dweight[inner * QUERIES : (inner + 1) * QUERIES] * tangent).astype(BF16)
                dscore.append(one)
                add_k = dot(q_t_ref[own, rows], one)
                add_v = dot(datt_t_ref[own, rows], weights_ref[head, i, :, 0 : high - low])
                for j in range(low // QUERIES, i + 1):
                    at = slice(j * QUERIES - low, (j + 1) * QUERIES - low)
                    for sums, add in ((dk_t[inner], add_k), (dv_t[inner], add_v)):
                        sums[j] = add[:, at] if sums[j] is None else sums[j] + add[:, at]
            dq.append(own_head(dot(jnp.concatenate(dscore, axis=0), k), lane, half))
        for inner in range(heads):
            for j in range(steps):
                at = slice(j * QUERIES, (j + 1) * QUERIES)
                dkv_t_ref[0, inner * half : (inner + 1) * half, at] = dv_t[inner][j]
                dkv_t_ref[1, inner * half : (inner + 1) * half, at] = dk_t[inner][j]
        for part, grad in (
            (1, dkv_t_ref[0].T),
            (2, jnp.concatenate(dq, axis=0)),
            (3, dkv_t_ref[1].T),
        ):
            columns = slice(part * width + lanes.start, part * width + lanes.stop)
            slope = slope_ref[:, columns].astype(F32)
            dpre_ref[:, columns] = (grad * slope).astype(BF16)


def input_kernel(
    owners, capacity, dpre_ref, w_ref, xhat_ref, x_rstd_ref, dy_ref, unplace_ref, out_ref
):
    me = lax.axis_index("dp")
    dxhat = dot_nt(dpre_ref[...], w_ref[...])
    xhat = xhat_ref[...].astype(F32)
    dx = dy_ref[...].astype(F32) + x_rstd_ref[:, 0:1] * (
        dxhat
        - jnp.mean(dxhat, axis=1, keepdims=True)
        - xhat * jnp.mean(dxhat * xhat, axis=1, keepdims=True)
    )
    rows = dot(unplace_ref[...], dx.astype(BF16)).astype(BF16)
    for k in range(owners):
        at = pl.ds(pl.multiple_of((me ^ k) * capacity, capacity), capacity)
        out_ref[at, :] = rows[k * capacity : (k + 1) * capacity]


def weight_kernel(owners, groups, xhat_t_ref, dpre_ref, gated_t_ref, dy_ref, kept_ref, sent_ref):
    me = lax.axis_index("dp")
    group = lax.axis_index("rep")
    in_grad = dot(xhat_t_ref[...], dpre_ref[...])
    out_grad = dot(gated_t_ref[...], dy_ref[...])
    in_cols = in_grad.shape[1] // owners
    out_cols = out_grad.shape[1] // owners
    part = in_grad.shape[0] // groups
    in_rows = part * in_cols // LANES
    for r in range(groups):
        rows = slice(r * part, (r + 1) * part)
        relative = group ^ r
        for target, ref in ((0, kept_ref), (1, sent_ref)):

            @pl.when((relative & 1) == target)
            def _():
                for d in range(owners):
                    side = (me ^ d) & 1
                    ref[relative >> 1, side, d // 2, 0:in_rows, :] = fold(
                        in_grad[rows, d * in_cols : (d + 1) * in_cols]
                    ).astype(BF16)
                    ref[relative >> 1, side, d // 2, in_rows:, :] = fold(
                        out_grad[rows, d * out_cols : (d + 1) * out_cols]
                    ).astype(BF16)


def added(first, second):
    return first.astype(F32) + second.astype(F32)


def core_sum_kernel(kept_ref, got_ref, a_kept_ref, a_sent_ref, b_kept_ref, b_sent_ref):
    half = kept_ref.shape[2] // 2
    a_sent_ref[...] = added(kept_ref[1, :, :half], got_ref[1, :, :half]).astype(BF16)
    b_sent_ref[...] = added(kept_ref[:, 1, half:], got_ref[:, 1, half:]).astype(BF16)
    a_kept_ref[...] = added(kept_ref[0, :, :half], got_ref[0, :, :half]).astype(BF16)
    b_kept_ref[...] = added(kept_ref[:, 0, half:], got_ref[:, 0, half:]).astype(BF16)


def side_sum_kernel(
    a_ref, a_got_ref, b_ref, b_got_ref, a_kept_ref, a_sent_ref, b_kept_ref, b_sent_ref
):
    a_sent_ref[...] = added(a_ref[1], a_got_ref[1]).astype(BF16)
    b_sent_ref[...] = added(b_ref[1], b_got_ref[1]).astype(BF16)
    a_kept_ref[...] = added(a_ref[0], a_got_ref[0]).astype(BF16)
    b_kept_ref[...] = added(b_ref[0], b_got_ref[0]).astype(BF16)


def plane_sum_kernel(a_ref, a_got_ref, b_ref, b_got_ref, *refs):
    outs, total_ref = refs[:-1], refs[-1]
    half = a_ref.shape[0]
    total_ref[:half] = added(a_ref[...], a_got_ref[...]).astype(BF16)
    total_ref[half:] = added(b_ref[...], b_got_ref[...]).astype(BF16)
    pair = lax.axis_index("dp") >> 1
    for k, ref in enumerate(outs):
        ref[...] = total_ref[pair ^ k]


def total_kernel(*refs):
    total = refs[0][...].astype(F32)
    for ref in refs[1:-1]:
        total = total + ref[...].astype(F32)
    refs[-1][...] = total.astype(BF16)


def result_kernel(groups, in_rows, *refs):
    in_ref, out_ref = refs[groups:]
    group = lax.axis_index("rep")
    part = in_ref.shape[0] // groups
    for k in range(groups):
        rows = pl.ds(pl.multiple_of((group ^ k) * part, part), part)
        piece = refs[k][...].astype(F32)
        in_ref[rows, :] = unfold(piece[:in_rows], part, in_ref.shape[1])
        out_ref[:, rows] = unfold(piece[in_rows:], part, out_ref.shape[0]).T


def collect_kernel(lookup_ref, rows_ref, out_ref):
    out_ref[...] = dot(lookup_ref[...], rows_ref[...]).astype(BF16)


def swap(value, axis, distance):
    size = lax.axis_size(axis)
    return lax.ppermute(value, axis, [(i, i ^ distance) for i in range(size)])


def exchange(blocks, after=None):
    got = [blocks[0]]
    for k in range(1, len(blocks)):
        block = blocks[k]
        if after is not None:
            block, after[k] = lax.optimization_barrier((block, after[k]))
        got.append(swap(block, "dp", k))
    return got


def ordered(value, *earlier):
    return lax.optimization_barrier((value,) + earlier)[0]


def on_device(events, grad_out, w_uvqk, w_out, send_place, send_counts, user_ids):
    owners = lax.axis_size("dp")
    groups = lax.axis_size("rep")
    count, width = events.shape
    capacity = 2 * count // owners
    slots = owners * capacity
    steps = count // QUERIES
    spans = max(high - low for low, high in map(key_range, range(steps)))
    block_shapes = [shape((capacity, width))] * owners
    route = 2 * slots * count * width
    square = shape((count, width))
    square_t = shape((width, count))
    wide = shape((count, 4 * width))
    column = shape((count, LANES), F32)
    scores = shape((HEADS, steps, QUERIES, spans))
    project = 2 * count * width * 4 * width
    attend = 2 * count * spans * width

    spread = functools.partial(spread_kernel, owners, capacity)
    x_blocks = call(functools.partial(spread, True), block_shapes, send_place, events, flops=route)
    dy_blocks = call(
        functools.partial(spread, False), block_shapes, send_place, grad_out, flops=route
    )
    lookup = call(lookup_kernel, shape((count, slots)), send_place)
    x_blocks = exchange(x_blocks)
    dy_blocks = exchange(dy_blocks, x_blocks)
    (
        place, unplace, act, slope, xhat, xhat_t, x_rstd,
        weights, tangent, nhat, a_rstd, gated_t, q_t,
    ) = call(
        functools.partial(forward_kernel, owners, capacity),
        [
            shape((count, slots)), shape((slots, count)), wide, wide, square, square_t, column,
            scores, scores, square, column, square_t, square_t,
        ],
        *x_blocks, user_ids, w_uvqk,
        flops=route + project + 2 * attend, transcendentals=HEADS * count * spans,
        scratch=[pltpu.VMEM((count, width), F32)], vmem=28,
    )
    owned_dy, dpre = call(
        functools.partial(backward_kernel, owners), [square, wide],
        *dy_blocks, place, act, slope, nhat, a_rstd, weights, tangent, q_t, w_out,
        flops=route + project // 4 + 4 * attend,
        scratch=[
            pltpu.VMEM((count, width), BF16),
            pltpu.VMEM((width, count), BF16),
            pltpu.VMEM((2, LANES, count), F32),
        ],
        vmem=28,
    )
    pairs = owners // 2
    in_rows = width // groups * (4 * width // owners) // LANES
    rows = in_rows + width // groups * (width // owners) // LANES
    kept, sent = call(
        functools.partial(weight_kernel, owners, groups),
        [shape((2, 2, pairs, rows, LANES))] * 2,
        xhat_t, dpre, gated_t, owned_dy, flops=project + project // 4,
    )
    back = call(
        functools.partial(input_kernel, owners, capacity), shape((slots, width)),
        ordered(dpre, sent), w_uvqk, xhat, x_rstd, owned_dy, unplace, flops=project + route,
    )
    a_kept, a_sent, b_kept, b_sent = call(
        core_sum_kernel, [shape((2, pairs // 2, rows, LANES))] * 4, kept, swap(sent, "rep", 1)
    )
    back = ordered(back, a_sent, b_sent)
    back = lax.all_to_all(back, "dp", split_axis=0, concat_axis=0, tiled=True)
    a_kept, a_sent, b_kept, b_sent = call(
        side_sum_kernel, [shape((pairs // 2, rows, LANES))] * 4,
        a_kept, swap(a_sent, "rep", 2), b_kept, swap(b_sent, "dp", 1),
    )
    pieces = call(
        plane_sum_kernel, [shape((rows, LANES))] * pairs,
        a_kept, swap(a_sent, "dp", 1), b_kept, swap(b_sent, "rep", 2),
        scratch=[pltpu.VMEM((pairs, rows, LANES), BF16)],
    )
    pieces = [pieces[0]] + [swap(pieces[k], "dp", 2 * k) for k in range(1, pairs)]
    own = call(total_kernel, shape((rows, LANES)), *pieces)
    far = swap(own, "rep", 2)
    shares = [own, swap(own, "rep", 1), far, swap(far, "rep", 1)]
    share_in, share_out = call(
        functools.partial(result_kernel, groups, in_rows),
        [shape((width, 4 * width // owners), F32), shape((width // owners, width), F32)],
        *shares,
    )
    grad_events = call(collect_kernel, square, lookup, back, flops=route)
    return (grad_events, share_in, share_out.T)


def solution(mesh):
    return jax.shard_map(
        on_device,
        mesh=mesh,
        in_specs=(
            P(("dp", "rep"), None),
            P(("dp", "rep"), None),
            P(),
            P(),
            P(("dp", "rep"), None),
            P(("dp", "rep"), None),
            P(("dp", "rep"), None),
        ),
        out_specs=(P(("dp", "rep"), None), P(None, "dp"), P(None, "dp")),
        check_vma=False,
    )
```

time: 143 us -> 117 us (0.82)
  starting transfers between devices: 57.4 us -> 41.5 us
  Pallas kernels: 31.9 us -> 22.5 us
    ppermute x30 -> x25, starting transfers between devices: 57.4 us -> 37.9 us  [swap(): return lax.ppermute(value, axis, [(i, i ^ distance) for i in range(size)])]
    pallas_call x12 -> x13, Pallas kernels: 31.9 us -> 22.5 us  [call(): pl.pallas_call(kernel, out_shape=out_shape, scratch_shapes=scratch, compi...]
    all_to_all x0 -> x1, starting transfers between devices: none -> 3.57 us  [on_device(): back = lax.all_to_all(back, 'dp', split_axis=0, concat_axis=0, tiled=True)]
    unnamed x15 -> x14, local copies, waits for them, and re-layouts: 4.38 us -> 3.6 us
    ppermute x30 -> x25, waiting for transfers between devices: 48 us -> 48.1 us  [swap(): return lax.ppermute(value, axis, [(i, i ^ distance) for i in range(size)])]
  transfers between devices with their start and end apart: 30 -> 26, of which waited for: 11 -> 14; matrix products, arithmetic and copies ran while one was open for 0% -> 0% of each run, Pallas kernels for 10% -> 11%
where the time goes in v2:
time: 117 us
  waiting for transfers between devices  48.1 us (41%)
  starting transfers between devices  41.5 us (35%)
  Pallas kernels  22.5 us (19%)
  local copies, waits for them, and re-layouts  3.6 us (3%)
    ppermute x25, waiting for transfers between devices, swap(): return lax.ppermute(value, axis, [(i, i ^ distance) for i in range(size)])  48.1 us
    ppermute x25, starting transfers between devices, swap(): return lax.ppermute(value, axis, [(i, i ^ distance) for i in range(size)])  37.9 us
    pallas_call x13, Pallas kernels, call(): pl.pallas_call(kernel, out_shape=out_shape, scratch_shapes=scratch, compi...  22.5 us
    unnamed x14, local copies, waits for them, and re-layouts  3.6 us
    all_to_all x1, starting transfers between devices, on_device(): back = lax.all_to_all(back, 'dp', split_axis=0, concat_axis=0, tiled=True)  3.57 us
  transfers between devices with their start and end apart: 26, of which 14 were waited for; matrix products, arithmetic and copies ran while one was open for 0% of the time, Pallas kernels for 11%

profile of v2, /device:TPU:0, one launch (start us, length us, event | category | flops | bytes accessed | tf_op | source)
XLA Modules:
  0.0 116.5 jit_solution(15171146921681652111)
XLA Ops:
  0.7 0.8 copy-done.2
  1.5 1.0 copy-done.4
  2.5 0.7 shard_map.87
  3.3 3.0 %collective-permute-start = (bf16[128,512]{1,0:T(8,128)(2,1)S(1)}, bf16[128,512]{1,0:T(8,128)(2,1)S(1)}, u32[]{:S(2)}, u32[]{:S(2)}) collective-permute-start(bf16[128,512]{1,0:T(8,128)(2,1)S(1)} %get-tuple-element.68), channel_id=1, source_target_pairs={{0,4},{4,0},{8,12},{12,8},{16,20},{20,16},{24,28},{28,24},{1,5},{5... | collective-permute-start | bytes 393224 | tf_op jit(solution)/shard_map/ppermute | solution.py:361
  6.3 3.6 %collective-permute-start.10 = (bf16[128,512]{1,0:T(8,128)(2,1)S(1)}, bf16[128,512]{1,0:T(8,128)(2,1)S(1)}, u32[]{:S(2)}, u32[]{:S(2)}) collective-permute-start(bf16[128,512]{1,0:T(8,128)(2,1)S(1)} %get-tuple-element.83), channel_id=1, source_target_pairs={{0,24},{4,28},{8,16},{12,20},{16,8},{20,12},{24,0},{28,4},{1,25},{... | collective-permute-start | bytes 393224 | tf_op jit(solution)/shard_map/ppermute | solution.py:361
  9.9 2.0 %collective-permute-start.4 = (bf16[128,512]{1,0:T(8,128)(2,1)S(1)}, bf16[128,512]{1,0:T(8,128)(2,1)S(1)}, u32[]{:S(2)}, u32[]{:S(2)}) collective-permute-start(bf16[128,512]{1,0:T(8,128)(2,1)S(1)} %get-tuple-element.74), channel_id=1, source_target_pairs={{0,12},{4,8},{8,4},{12,0},{16,28},{20,24},{24,20},{28,16},{1,13},{... | collective-permute-start | bytes 393224 | tf_op jit(solution)/shard_map/ppermute | solution.py:361
  11.9 3.8 %collective-permute-start.8 = (bf16[128,512]{1,0:T(8,128)(2,1)S(1)}, bf16[128,512]{1,0:T(8,128)(2,1)S(1)}, u32[]{:S(2)}, u32[]{:S(2)}) collective-permute-start(bf16[128,512]{1,0:T(8,128)(2,1)S(1)} %get-tuple-element.80), channel_id=1, source_target_pairs={{0,20},{4,16},{8,28},{12,24},{16,4},{20,0},{24,12},{28,8},{1,21},{... | collective-permute-start | bytes 393224 | tf_op jit(solution)/shard_map/ppermute | solution.py:361
  15.7 2.3 %collective-permute-start.12 = (bf16[128,512]{1,0:T(8,128)(2,1)S(1)}, bf16[128,512]{1,0:T(8,128)(2,1)S(1)}, u32[]{:S(2)}, u32[]{:S(2)}) collective-permute-start(bf16[128,512]{1,0:T(8,128)(2,1)S(1)} %get-tuple-element.86), channel_id=1, source_target_pairs={{0,28},{4,24},{8,20},{12,16},{16,12},{20,8},{24,4},{28,0},{1,29},{... | collective-permute-start | bytes 393224 | tf_op jit(solution)/shard_map/ppermute | solution.py:361
  18.1 1.0 copy-done.5
  19.1 0.7 shard_map.86
  19.8 0.8 collective-permute-done.2.refs_2_
  20.6 0.8 collective-permute-start.1
  21.4 1.0 collective-permute-done.4.refs_3_
  22.4 2.9 %collective-permute-start.11 = (bf16[128,512]{1,0:T(8,128)(2,1)S(1)}, bf16[128,512]{1,0:T(8,128)(2,1)S(1)}, u32[]{:S(2)}, u32[]{:S(2)}) collective-permute-start(bf16[128,512]{1,0:T(8,128)(2,1)S(1)} %get-tuple-element.84), channel_id=1, source_target_pairs={{0,24},{4,28},{8,16},{12,20},{16,8},{20,12},{24,0},{28,4},{1,25},{... | collective-permute-start | bytes 393224 | tf_op jit(solution)/shard_map/ppermute | solution.py:361
  25.3 5.1 %collective-permute-done.6.refs_4_ = bf16[128,512]{1,0:T(8,128)(2,1)S(1)} collective-permute-done((bf16[128,512]{1,0:T(8,128)(2,1)S(1)}, bf16[128,512]{1,0:T(8,128)(2,1)S(1)}, u32[]{:S(2)}, u32[]{:S(2)}) %collective-permute-start.6) | collective-permute-done | bytes 131104 | tf_op jit(solution)/shard_map/ppermute | solution.py:361
  30.4 5.1 %collective-permute-done.8.refs_5_ = bf16[128,512]{1,0:T(8,128)(2,1)S(1)} collective-permute-done((bf16[128,512]{1,0:T(8,128)(2,1)S(1)}, bf16[128,512]{1,0:T(8,128)(2,1)S(1)}, u32[]{:S(2)}, u32[]{:S(2)}) %collective-permute-start.8) | collective-permute-done | bytes 131104 | tf_op jit(solution)/shard_map/ppermute | solution.py:361
  35.6 1.9 %collective-permute-start.13 = (bf16[128,512]{1,0:T(8,128)(2,1)S(1)}, bf16[128,512]{1,0:T(8,128)(2,1)S(1)}, u32[]{:S(2)}, u32[]{:S(2)}) collective-permute-start(bf16[128,512]{1,0:T(8,128)(2,1)S(1)} %get-tuple-element.87), channel_id=1, source_target_pairs={{0,28},{4,24},{8,20},{12,16},{16,12},{20,8},{24,4},{28,0},{1,29},{... | collective-permute-start | bytes 393224 | tf_op jit(solution)/shard_map/ppermute | solution.py:361
  37.5 2.5 %collective-permute-start.3 = (bf16[128,512]{1,0:T(8,128)(2,1)S(1)}, bf16[128,512]{1,0:T(8,128)(2,1)S(1)}, u32[]{:S(2)}, u32[]{:S(2)}) collective-permute-start(bf16[128,512]{1,0:T(8,128)(2,1)S(1)} %get-tuple-element.72), channel_id=1, source_target_pairs={{0,8},{4,12},{8,0},{12,4},{16,24},{20,28},{24,16},{28,20},{1,9},{5... | collective-permute-start | bytes 393224 | tf_op jit(solution)/shard_map/ppermute | solution.py:361
  40.0 2.5 %collective-permute-start.7 = (bf16[128,512]{1,0:T(8,128)(2,1)S(1)}, bf16[128,512]{1,0:T(8,128)(2,1)S(1)}, u32[]{:S(2)}, u32[]{:S(2)}) collective-permute-start(bf16[128,512]{1,0:T(8,128)(2,1)S(1)} %get-tuple-element.78), channel_id=1, source_target_pairs={{0,16},{4,20},{8,24},{12,28},{16,0},{20,4},{24,8},{28,12},{1,17},{... | collective-permute-start | bytes 393224 | tf_op jit(solution)/shard_map/ppermute | solution.py:361
  42.5 1.3 %collective-permute-start.9 = (bf16[128,512]{1,0:T(8,128)(2,1)S(1)}, bf16[128,512]{1,0:T(8,128)(2,1)S(1)}, u32[]{:S(2)}, u32[]{:S(2)}) collective-permute-start(bf16[128,512]{1,0:T(8,128)(2,1)S(1)} %get-tuple-element.81), channel_id=1, source_target_pairs={{0,20},{4,16},{8,28},{12,24},{16,4},{20,0},{24,12},{28,8},{1,21},{... | collective-permute-start | bytes 393224 | tf_op jit(solution)/shard_map/ppermute | solution.py:361
  43.8 0.7 copy-done.6
  44.5 7.5 %shard_map.88 = (bf16[512,1024]{1,0:T(8,128)(2,1)S(1)}, bf16[1024,512]{1,0:T(8,128)(2,1)S(1)}, bf16[512,2048]{1,0:T(8,128)(2,1)S(1)}, bf16[512,2048]{1,0:T(8,128...) custom-call(bf16[128,512]{1,0:T(8,128)(2,1)S(1)} %get-tuple-element., ...), custom_call_target="tpu_custom_call" | custom-call | flops 2147483648 | bytes 20973568 | tf_op jit(solution)/shard_map/pallas_call | solution.py:36
  52.1 0.8 collective-permute-done.7.refs_4_
  52.9 3.1 %collective-permute-done.9.refs_5_ = bf16[128,512]{1,0:T(8,128)(2,1)S(1)} collective-permute-done((bf16[128,512]{1,0:T(8,128)(2,1)S(1)}, bf16[128,512]{1,0:T(8,128)(2,1)S(1)}, u32[]{:S(2)}, u32[]{:S(2)}) %collective-permute-start.9) | collective-permute-done | bytes 131104 | tf_op jit(solution)/shard_map/ppermute | solution.py:361
  56.0 4.8 %shard_map.89 = (bf16[512,512]{1,0:T(8,128)(2,1)S(1)}, bf16[512,2048]{1,0:T(8,128)(2,1)S(1)}) custom-call(bf16[128,512]{1,0:T(8,128)(2,1)S(1)} %get-tuple-element.66.refs_0_, bf16[128,512]{1,0:T(8,128)(2,1)S(1)} %collective-permute-done.1.refs_1_, bf16[128,512]{1,0:T(8,128)(2,1)S(1)} %collective-permute-done.3.refs_2_, ...), custom_call_target="tpu_custom_call" | custom-call | flops 1879048192 | bytes 19136512 | tf_op jit(solution)/shard_map/pallas_call | solution.py:36
  60.8 2.1 %shard_map.90 = (bf16[2,2,4,320,128]{4,3,2,1,0:T(8,128)(2,1)S(1)}, bf16[2,2,4,320,128]{4,3,2,1,0:T(8,128)(2,1)S(1)}) custom-call(bf16[512,512]{1,0:T(8,128)(2,1)S(1)} %get-tuple-element.105.xhat_t_ref, bf16[512,2048]{1,0:T(8,128)(2,1)S(1)} %get-tuple-element.109.dpre_ref, bf16[512,512]{1,0:T(8,128)(2,1)S(1)} %get-tuple-element.106.gated_t_ref, ...), custom_call_target="tpu_custom_call" | custom-call | flops 1342177280 | bytes 6291456 | tf_op jit(solution)/shard_map/pallas_call | solution.py:36
  63.0 3.1 %shard_map.91 = bf16[1024,512]{1,0:T(8,128)(2,1)} custom-call(bf16[512,2048]{1,0:T(8,128)(2,1)S(1)} %get-tuple-element.109.dpre_ref, bf16[512,2048]{1,0:T(8,128)(2,1)S(1)} %copy-done, bf16[512,512]{1,0:T(8,128)(2,1)S(1)} %get-tuple-element.110.xhat_ref, f32[512,128]{1,0:T(8,128)S(1)} %get-tuple-element.111.x_rstd_ref, ...), custom_call_target="tpu_custom_call" | custom-call | flops 1610612736 | bytes 7602176 | tf_op jit(solution)/shard_map/pallas_call | solution.py:36
  66.1 0.3 shard_map.92
  66.5 3.6 %all-to-all-start = ((bf16[8,128,512]{2,1,0:T(8,128)(2,1)}), bf16[8,128,512]{2,1,0:T(8,128)(2,1)S(1)}, u32[]{:S(2)}, u32[]{:S(2)}) async-start(bf16[8,128,512]{2,1,0:T(8,128)(2,1)} %bitcast), calls=%async_computation | async-start | bytes 2097152 | tf_op jit(solution)/shard_map/all_to_all | solution.py:444
  70.0 1.6 %collective-permute-start.15 = (bf16[2,2,320,128]{3,2,1,0:T(8,128)(2,1)S(1)}, bf16[2,2,320,128]{3,2,1,0:T(8,128)(2,1)S(1)}, u32[]{:S(2)}, u32[]{:S(2)}) collective-permute-start(bf16[2,2,320,128]{3,2,1,0:T(8,128)(2,1)S(1)} %get-tuple-element.114), channel_id=1, source_target_pairs={{0,2},{1,3},{2,0},{3,1},{4,6},{5,7},{6,4},{7,5},{8,10},{9,11},{10,... | collective-permute-start | bytes 983048 | tf_op jit(solution)/shard_map/ppermute | solution.py:361
  71.6 1.9 %collective-permute-start.16 = (bf16[2,2,320,128]{3,2,1,0:T(8,128)(2,1)S(1)}, bf16[2,2,320,128]{3,2,1,0:T(8,128)(2,1)S(1)}, u32[]{:S(2)}, u32[]{:S(2)}) collective-permute-start(bf16[2,2,320,128]{3,2,1,0:T(8,128)(2,1)S(1)} %get-tuple-element.115), channel_id=1, source_target_pairs={{0,4},{4,0},{8,12},{12,8},{16,20},{20,16},{24,28},{28,24},{1,5},{5... | collective-permute-start | bytes 983048 | tf_op jit(solution)/shard_map/ppermute | solution.py:361
  73.5 6.7 %collective-permute-done.15.a_got_ref = bf16[2,2,320,128]{3,2,1,0:T(8,128)(2,1)S(1)} collective-permute-done((bf16[2,2,320,128]{3,2,1,0:T(8,128)(2,1)S(1)}, bf16[2,2,320,128]{3,2,1,0:T(8,128)(2,1)S(1)}, u32[]{:S(2)}, u32[]{:S(2)}) %collective-permute-start.15) | collective-permute-done | bytes 327712 | tf_op jit(solution)/shard_map/ppermute | solution.py:361
  80.2 11.3 %collective-permute-done.16.b_got_ref = bf16[2,2,320,128]{3,2,1,0:T(8,128)(2,1)S(1)} collective-permute-done((bf16[2,2,320,128]{3,2,1,0:T(8,128)(2,1)S(1)}, bf16[2,2,320,128]{3,2,1,0:T(8,128)(2,1)S(1)}, u32[]{:S(2)}, u32[]{:S(2)}) %collective-permute-start.16) | collective-permute-done | bytes 327712 | tf_op jit(solution)/shard_map/ppermute | solution.py:361
  91.5 0.2 shard_map.94
  91.7 1.6 %collective-permute-start.18 = (bf16[2,320,128]{2,1,0:T(8,128)(2,1)S(1)}, bf16[2,320,128]{2,1,0:T(8,128)(2,1)S(1)}, u32[]{:S(2)}, u32[]{:S(2)}) collective-permute-start(bf16[2,320,128]{2,1,0:T(8,128)(2,1)S(1)} %get-tuple-element.122), channel_id=1, source_target_pairs={{0,2},{1,3},{2,0},{3,1},{4,6},{5,7},{6,4},{7,5},{8,10},{9,11},{10,... | collective-permute-start | bytes 491528 | tf_op jit(solution)/shard_map/ppermute | solution.py:361
  93.3 4.2 %collective-permute-done.17.a_got_ref = bf16[2,320,128]{2,1,0:T(8,128)(2,1)S(1)} collective-permute-done((bf16[2,320,128]{2,1,0:T(8,128)(2,1)S(1)}, bf16[2,320,128]{2,1,0:T(8,128)(2,1)S(1)}, u32[]{:S(2)}, u32[]{:S(2)}) %collective-permute-start.17) | collective-permute-done | bytes 163872 | tf_op jit(solution)/shard_map/ppermute | solution.py:361
  97.6 0.1 shard_map.95
  97.7 1.7 %collective-permute-start.19 = (bf16[320,128]{1,0:T(8,128)(2,1)S(1)}, bf16[320,128]{1,0:T(8,128)(2,1)S(1)}, u32[]{:S(2)}, u32[]{:S(2)}) collective-permute-start(bf16[320,128]{1,0:T(8,128)(2,1)S(1)} %get-tuple-element.124), channel_id=1, source_target_pairs={{0,8},{4,12},{8,0},{12,4},{16,24},{20,28},{24,16},{28,20},{1,9},{5... | collective-permute-start | bytes 245768 | tf_op jit(solution)/shard_map/ppermute | solution.py:361
  99.5 2.2 %collective-permute-start.20 = (bf16[320,128]{1,0:T(8,128)(2,1)S(1)}, bf16[320,128]{1,0:T(8,128)(2,1)S(1)}, u32[]{:S(2)}, u32[]{:S(2)}) collective-permute-start(bf16[320,128]{1,0:T(8,128)(2,1)S(1)} %get-tuple-element.125), channel_id=1, source_target_pairs={{0,16},{4,20},{8,24},{12,28},{16,0},{20,4},{24,8},{28,12},{1,17},{... | collective-permute-start | bytes 245768 | tf_op jit(solution)/shard_map/ppermute | solution.py:361
  101.7 0.5 collective-permute-start.21
  102.2 0.1 collective-permute-done.19.refs_1_
  102.3 5.9 %collective-permute-done.20.refs_2_ = bf16[320,128]{1,0:T(8,128)(2,1)S(1)} collective-permute-done((bf16[320,128]{1,0:T(8,128)(2,1)S(1)}, bf16[320,128]{1,0:T(8,128)(2,1)S(1)}, u32[]{:S(2)}, u32[]{:S(2)}) %collective-permute-start.20) | collective-permute-done | bytes 81952 | tf_op jit(solution)/shard_map/ppermute | solution.py:361
  108.3 1.6 %collective-permute-start.23 = (bf16[320,128]{1,0:T(8,128)(2,1)S(1)}, bf16[320,128]{1,0:T(8,128)(2,1)S(1)}, u32[]{:S(2)}, u32[]{:S(2)}) collective-permute-start(bf16[320,128]{1,0:T(8,128)(2,1)S(1)} %shard_map.96.refs_0_), channel_id=1, source_target_pairs={{0,2},{1,3},{2,0},{3,1},{4,6},{5,7},{6,4},{7,5},{8,10},{9,11},{10,... | collective-permute-start | bytes 245768 | tf_op jit(solution)/shard_map/ppermute | solution.py:361
  109.9 2.9 %collective-permute-done.23.refs_2_ = bf16[320,128]{1,0:T(8,128)(2,1)S(1)} collective-permute-done((bf16[320,128]{1,0:T(8,128)(2,1)S(1)}, bf16[320,128]{1,0:T(8,128)(2,1)S(1)}, u32[]{:S(2)}, u32[]{:S(2)}) %collective-permute-start.23) | collective-permute-done | bytes 81952 | tf_op jit(solution)/shard_map/ppermute | solution.py:361
  112.8 0.3 shard_map.85.lookup_ref
  113.1 0.9 collective-permute-done.24.refs_3_
  114.0 1.0 shard_map.97
  115.0 1.5 %shard_map.93 = bf16[512,512]{1,0:T(8,128)(2,1)} custom-call(bf16[512,1024]{1,0:T(8,128)(2,1)S(1)} %shard_map.85.lookup_ref, bf16[1024,512]{1,0:T(8,128)(2,1)S(1)} %bitcast.3), custom_call_target="tpu_custom_call" | custom-call | flops 536870912 | bytes 2621440 | tf_op jit(solution)/shard_map/pallas_call | solution.py:36
  (31 shorter events, 0.3 us)
Async XLA Ops:
  0.6 43.2 %copy-start = (bf16[512,2048]{1,0:T(8,128)(2,1)S(1)}, bf16[512,2048]{1,0:T(8,128)(2,1)}, u32[]{:S(2)}) copy-start(bf16[512,2048]{1,0:T(8,128)(2,1)} %w_ref.1) | copy-start | bytes 6291460
  0.6 0.8 copy-start.2
  1.5 1.0 copy-start.4
  3.3 8.6 %collective-permute-start = (bf16[128,512]{1,0:T(8,128)(2,1)S(1)}, bf16[128,512]{1,0:T(8,128)(2,1)S(1)}, u32[]{:S(2)}, u32[]{:S(2)}) collective-permute-start(bf16[128,512]{1,0:T(8,128)(2,1)S(1)} %get-tuple-element.68), channel_id=1, source_target_pairs={{0,4},{4,0},{8,12},{12,8},{16,20},{20,16},{24,28},{28,24},{1,5},{5... | collective-permute-start | bytes 393224 | tf_op jit(solution)/shard_map/ppermute | solution.py:361
  6.3 9.5 %collective-permute-start.10 = (bf16[128,512]{1,0:T(8,128)(2,1)S(1)}, bf16[128,512]{1,0:T(8,128)(2,1)S(1)}, u32[]{:S(2)}, u32[]{:S(2)}) collective-permute-start(bf16[128,512]{1,0:T(8,128)(2,1)S(1)} %get-tuple-element.83), channel_id=1, source_target_pairs={{0,24},{4,28},{8,16},{12,20},{16,8},{20,12},{24,0},{28,4},{1,25},{... | collective-permute-start | bytes 393224 | tf_op jit(solution)/shard_map/ppermute | solution.py:361
  9.9 10.8 %collective-permute-start.2 = (bf16[128,512]{1,0:T(8,128)(2,1)S(1)}, bf16[128,512]{1,0:T(8,128)(2,1)S(1)}, u32[]{:S(2)}, u32[]{:S(2)}) collective-permute-start(bf16[128,512]{1,0:T(8,128)(2,1)S(1)} %get-tuple-element.71), channel_id=1, source_target_pairs={{0,8},{4,12},{8,0},{12,4},{16,24},{20,28},{24,16},{28,20},{1,9},{5... | collective-permute-start | bytes 393224 | tf_op jit(solution)/shard_map/ppermute | solution.py:361
  9.9 12.6 %collective-permute-start.4 = (bf16[128,512]{1,0:T(8,128)(2,1)S(1)}, bf16[128,512]{1,0:T(8,128)(2,1)S(1)}, u32[]{:S(2)}, u32[]{:S(2)}) collective-permute-start(bf16[128,512]{1,0:T(8,128)(2,1)S(1)} %get-tuple-element.74), channel_id=1, source_target_pairs={{0,12},{4,8},{8,4},{12,0},{16,28},{20,24},{24,20},{28,16},{1,13},{... | collective-permute-start | bytes 393224 | tf_op jit(solution)/shard_map/ppermute | solution.py:361
  11.9 18.6 %collective-permute-start.6 = (bf16[128,512]{1,0:T(8,128)(2,1)S(1)}, bf16[128,512]{1,0:T(8,128)(2,1)S(1)}, u32[]{:S(2)}, u32[]{:S(2)}) collective-permute-start(bf16[128,512]{1,0:T(8,128)(2,1)S(1)} %get-tuple-element.77), channel_id=1, source_target_pairs={{0,16},{4,20},{8,24},{12,28},{16,0},{20,4},{24,8},{28,12},{1,17},{... | collective-permute-start | bytes 393224 | tf_op jit(solution)/shard_map/ppermute | solution.py:361
  11.9 23.7 %collective-permute-start.8 = (bf16[128,512]{1,0:T(8,128)(2,1)S(1)}, bf16[128,512]{1,0:T(8,128)(2,1)S(1)}, u32[]{:S(2)}, u32[]{:S(2)}) collective-permute-start(bf16[128,512]{1,0:T(8,128)(2,1)S(1)} %get-tuple-element.80), channel_id=1, source_target_pairs={{0,20},{4,16},{8,28},{12,24},{16,4},{20,0},{24,12},{28,8},{1,21},{... | collective-permute-start | bytes 393224 | tf_op jit(solution)/shard_map/ppermute | solution.py:361
  15.7 19.9 %collective-permute-start.12 = (bf16[128,512]{1,0:T(8,128)(2,1)S(1)}, bf16[128,512]{1,0:T(8,128)(2,1)S(1)}, u32[]{:S(2)}, u32[]{:S(2)}) collective-permute-start(bf16[128,512]{1,0:T(8,128)(2,1)S(1)} %get-tuple-element.86), channel_id=1, source_target_pairs={{0,28},{4,24},{8,20},{12,16},{16,12},{20,8},{24,4},{28,0},{1,29},{... | collective-permute-start | bytes 393224 | tf_op jit(solution)/shard_map/ppermute | solution.py:361
  18.1 1.0 copy-start.5
  20.6 19.4 %collective-permute-start.1 = (bf16[128,512]{1,0:T(8,128)(2,1)S(1)}, bf16[128,512]{1,0:T(8,128)(2,1)S(1)}, u32[]{:S(2)}, u32[]{:S(2)}) collective-permute-start(bf16[128,512]{1,0:T(8,128)(2,1)S(1)} %get-tuple-element.69), channel_id=1, source_target_pairs={{0,4},{4,0},{8,12},{12,8},{16,20},{20,16},{24,28},{28,24},{1,5},{5... | collective-permute-start | bytes 393224 | tf_op jit(solution)/shard_map/ppermute | solution.py:361
  22.4 20.1 %collective-permute-start.11 = (bf16[128,512]{1,0:T(8,128)(2,1)S(1)}, bf16[128,512]{1,0:T(8,128)(2,1)S(1)}, u32[]{:S(2)}, u32[]{:S(2)}) collective-permute-start(bf16[128,512]{1,0:T(8,128)(2,1)S(1)} %get-tuple-element.84), channel_id=1, source_target_pairs={{0,24},{4,28},{8,16},{12,20},{16,8},{20,12},{24,0},{28,4},{1,25},{... | collective-permute-start | bytes 393224 | tf_op jit(solution)/shard_map/ppermute | solution.py:361
  35.6 16.5 %collective-permute-start.13 = (bf16[128,512]{1,0:T(8,128)(2,1)S(1)}, bf16[128,512]{1,0:T(8,128)(2,1)S(1)}, u32[]{:S(2)}, u32[]{:S(2)}) collective-permute-start(bf16[128,512]{1,0:T(8,128)(2,1)S(1)} %get-tuple-element.87), channel_id=1, source_target_pairs={{0,28},{4,24},{8,20},{12,16},{16,12},{20,8},{24,4},{28,0},{1,29},{... | collective-permute-start | bytes 393224 | tf_op jit(solution)/shard_map/ppermute | solution.py:361
  37.5 14.5 %collective-permute-start.3 = (bf16[128,512]{1,0:T(8,128)(2,1)S(1)}, bf16[128,512]{1,0:T(8,128)(2,1)S(1)}, u32[]{:S(2)}, u32[]{:S(2)}) collective-permute-start(bf16[128,512]{1,0:T(8,128)(2,1)S(1)} %get-tuple-element.72), channel_id=1, source_target_pairs={{0,8},{4,12},{8,0},{12,4},{16,24},{20,28},{24,16},{28,20},{1,9},{5... | collective-permute-start | bytes 393224 | tf_op jit(solution)/shard_map/ppermute | solution.py:361
  40.0 12.1 %collective-permute-start.5 = (bf16[128,512]{1,0:T(8,128)(2,1)S(1)}, bf16[128,512]{1,0:T(8,128)(2,1)S(1)}, u32[]{:S(2)}, u32[]{:S(2)}) collective-permute-start(bf16[128,512]{1,0:T(8,128)(2,1)S(1)} %get-tuple-element.75), channel_id=1, source_target_pairs={{0,12},{4,8},{8,4},{12,0},{16,28},{20,24},{24,20},{28,16},{1,13},{... | collective-permute-start | bytes 393224 | tf_op jit(solution)/shard_map/ppermute | solution.py:361
  40.0 12.9 %collective-permute-start.7 = (bf16[128,512]{1,0:T(8,128)(2,1)S(1)}, bf16[128,512]{1,0:T(8,128)(2,1)S(1)}, u32[]{:S(2)}, u32[]{:S(2)}) collective-permute-start(bf16[128,512]{1,0:T(8,128)(2,1)S(1)} %get-tuple-element.78), channel_id=1, source_target_pairs={{0,16},{4,20},{8,24},{12,28},{16,0},{20,4},{24,8},{28,12},{1,17},{... | collective-permute-start | bytes 393224 | tf_op jit(solution)/shard_map/ppermute | solution.py:361
  42.5 13.5 %collective-permute-start.9 = (bf16[128,512]{1,0:T(8,128)(2,1)S(1)}, bf16[128,512]{1,0:T(8,128)(2,1)S(1)}, u32[]{:S(2)}, u32[]{:S(2)}) collective-permute-start(bf16[128,512]{1,0:T(8,128)(2,1)S(1)} %get-tuple-element.81), channel_id=1, source_target_pairs={{0,20},{4,16},{8,28},{12,24},{16,4},{20,0},{24,12},{28,8},{1,21},{... | collective-permute-start | bytes 393224 | tf_op jit(solution)/shard_map/ppermute | solution.py:361
  43.8 0.7 copy-start.6
  44.5 11.5 %copy-start.1 = (bf16[512,512]{1,0:T(8,128)(2,1)S(1)}, bf16[512,512]{1,0:T(8,128)(2,1)}, u32[]{:S(2)}) copy-start(bf16[512,512]{1,0:T(8,128)(2,1)} %refs_16_.1) | copy-start | bytes 1572868
  62.9 3.2 %collective-permute-start.14 = (bf16[2,2,4,320,128]{4,3,2,1,0:T(8,128)(2,1)S(1)}, bf16[2,2,4,320,128]{4,3,2,1,0:T(8,128)(2,1)S(1)}, u32[]{:S(2)}, u32[]{:S(2)}) collective-permute-start(bf16[2,2,4,320,128]{4,3,2,1,0:T(8,128)(2,1)S(1)} %get-tuple-element.108), channel_id=1, source_target_pairs={{0,1},{1,0},{2,3},{3,2},{4,5},{5,4},{6,7},{7,6},{8,9},{9,8},{10,11... | collective-permute-start | bytes 3932168 | tf_op jit(solution)/shard_map/ppermute | solution.py:361
  66.4 46.3 %copy-start.3 = (s32[1,512]{1,0:T(1,128)S(1)}, s32[1,512]{1,0:T(1,128)}, u32[]{:S(2)}) copy-start(s32[1,512]{1,0:T(1,128)} %place_ref.5) | copy-start | bytes 6148
  66.5 48.6 %all-to-all-start = ((bf16[8,128,512]{2,1,0:T(8,128)(2,1)}), bf16[8,128,512]{2,1,0:T(8,128)(2,1)S(1)}, u32[]{:S(2)}, u32[]{:S(2)}) async-start(bf16[8,128,512]{2,1,0:T(8,128)(2,1)} %bitcast), calls=%async_computation | async-start | bytes 2097152 | tf_op jit(solution)/shard_map/all_to_all | solution.py:444
  70.0 10.2 %collective-permute-start.15 = (bf16[2,2,320,128]{3,2,1,0:T(8,128)(2,1)S(1)}, bf16[2,2,320,128]{3,2,1,0:T(8,128)(2,1)S(1)}, u32[]{:S(2)}, u32[]{:S(2)}) collective-permute-start(bf16[2,2,320,128]{3,2,1,0:T(8,128)(2,1)S(1)} %get-tuple-element.114), channel_id=1, source_target_pairs={{0,2},{1,3},{2,0},{3,1},{4,6},{5,7},{6,4},{7,5},{8,10},{9,11},{10,... | collective-permute-start | bytes 983048 | tf_op jit(solution)/shard_map/ppermute | solution.py:361
  71.6 19.9 %collective-permute-start.16 = (bf16[2,2,320,128]{3,2,1,0:T(8,128)(2,1)S(1)}, bf16[2,2,320,128]{3,2,1,0:T(8,128)(2,1)S(1)}, u32[]{:S(2)}, u32[]{:S(2)}) collective-permute-start(bf16[2,2,320,128]{3,2,1,0:T(8,128)(2,1)S(1)} %get-tuple-element.115), channel_id=1, source_target_pairs={{0,4},{4,0},{8,12},{12,8},{16,20},{20,16},{24,28},{28,24},{1,5},{5... | collective-permute-start | bytes 983048 | tf_op jit(solution)/shard_map/ppermute | solution.py:361
  91.6 5.9 %collective-permute-start.17 = (bf16[2,320,128]{2,1,0:T(8,128)(2,1)S(1)}, bf16[2,320,128]{2,1,0:T(8,128)(2,1)S(1)}, u32[]{:S(2)}, u32[]{:S(2)}) collective-permute-start(bf16[2,320,128]{2,1,0:T(8,128)(2,1)S(1)} %get-tuple-element.120), channel_id=1, source_target_pairs={{0,4},{4,0},{8,12},{12,8},{16,20},{20,16},{24,28},{28,24},{1,5},{5... | collective-permute-start | bytes 491528 | tf_op jit(solution)/shard_map/ppermute | solution.py:361
  91.7 5.9 %collective-permute-start.18 = (bf16[2,320,128]{2,1,0:T(8,128)(2,1)S(1)}, bf16[2,320,128]{2,1,0:T(8,128)(2,1)S(1)}, u32[]{:S(2)}, u32[]{:S(2)}) collective-permute-start(bf16[2,320,128]{2,1,0:T(8,128)(2,1)S(1)} %get-tuple-element.122), channel_id=1, source_target_pairs={{0,2},{1,3},{2,0},{3,1},{4,6},{5,7},{6,4},{7,5},{8,10},{9,11},{10,... | collective-permute-start | bytes 491528 | tf_op jit(solution)/shard_map/ppermute | solution.py:361
  97.7 4.6 %collective-permute-start.19 = (bf16[320,128]{1,0:T(8,128)(2,1)S(1)}, bf16[320,128]{1,0:T(8,128)(2,1)S(1)}, u32[]{:S(2)}, u32[]{:S(2)}) collective-permute-start(bf16[320,128]{1,0:T(8,128)(2,1)S(1)} %get-tuple-element.124), channel_id=1, source_target_pairs={{0,8},{4,12},{8,0},{12,4},{16,24},{20,28},{24,16},{28,20},{1,9},{5... | collective-permute-start | bytes 245768 | tf_op jit(solution)/shard_map/ppermute | solution.py:361
  99.5 8.7 %collective-permute-start.20 = (bf16[320,128]{1,0:T(8,128)(2,1)S(1)}, bf16[320,128]{1,0:T(8,128)(2,1)S(1)}, u32[]{:S(2)}, u32[]{:S(2)}) collective-permute-start(bf16[320,128]{1,0:T(8,128)(2,1)S(1)} %get-tuple-element.125), channel_id=1, source_target_pairs={{0,16},{4,20},{8,24},{12,28},{16,0},{20,4},{24,8},{28,12},{1,17},{... | collective-permute-start | bytes 245768 | tf_op jit(solution)/shard_map/ppermute | solution.py:361
  101.7 6.5 %collective-permute-start.21 = (bf16[320,128]{1,0:T(8,128)(2,1)S(1)}, bf16[320,128]{1,0:T(8,128)(2,1)S(1)}, u32[]{:S(2)}, u32[]{:S(2)}) collective-permute-start(bf16[320,128]{1,0:T(8,128)(2,1)S(1)} %get-tuple-element.126), channel_id=1, source_target_pairs={{0,24},{4,28},{8,16},{12,20},{16,8},{20,12},{24,0},{28,4},{1,25},{... | collective-permute-start | bytes 245768 | tf_op jit(solution)/shard_map/ppermute | solution.py:361
  108.3 4.5 %collective-permute-start.23 = (bf16[320,128]{1,0:T(8,128)(2,1)S(1)}, bf16[320,128]{1,0:T(8,128)(2,1)S(1)}, u32[]{:S(2)}, u32[]{:S(2)}) collective-permute-start(bf16[320,128]{1,0:T(8,128)(2,1)S(1)} %shard_map.96.refs_0_), channel_id=1, source_target_pairs={{0,2},{1,3},{2,0},{3,1},{4,6},{5,7},{6,4},{7,5},{8,10},{9,11},{10,... | collective-permute-start | bytes 245768 | tf_op jit(solution)/shard_map/ppermute | solution.py:361
  109.8 3.2 %collective-permute-start.22 = (bf16[320,128]{1,0:T(8,128)(2,1)S(1)}, bf16[320,128]{1,0:T(8,128)(2,1)S(1)}, u32[]{:S(2)}, u32[]{:S(2)}) collective-permute-start(bf16[320,128]{1,0:T(8,128)(2,1)S(1)} %shard_map.96.refs_0_), channel_id=1, source_target_pairs={{0,1},{1,0},{2,3},{3,2},{4,5},{5,4},{6,7},{7,6},{8,9},{9,8},{10,11... | collective-permute-start | bytes 245768 | tf_op jit(solution)/shard_map/ppermute | solution.py:361
  112.8 1.3 %collective-permute-start.24 = (bf16[320,128]{1,0:T(8,128)(2,1)S(1)}, bf16[320,128]{1,0:T(8,128)(2,1)S(1)}, u32[]{:S(2)}, u32[]{:S(2)}) collective-permute-start(bf16[320,128]{1,0:T(8,128)(2,1)S(1)} %collective-permute-done.23.refs_2_), channel_id=1, source_target_pairs={{0,1},{1,0},{2,3},{3,2},{4,5},{5,4},{6,7},{7,6},{8,9},{9,8},{10,11... | collective-permute-start | bytes 245768 | tf_op jit(solution)/shard_map/ppermute | solution.py:361

commit v3 on v2

--- a/solution.py
+++ b/solution.py
@@ -15,6 +15,7 @@
 QUERIES = 256
 LANES = 128
 F32 = jnp.float32
+WAITING = 3 * 10**9
 BF16 = jnp.bfloat16
 
 
@@ -48,19 +49,36 @@
     return jax.ShapeDtypeStruct(tuple(dims), dtype)
 
 
-def spread_kernel(owners, capacity, mark, place_ref, rows_ref, *out_refs):
+def far_first(owners):
+    return [0, *range(owners // 2, owners)]
+
+
+def selection(first, capacity, place):
+    return (iota((capacity, place.shape[1]), 0) + first == place).astype(F32)
+
+
+def selected(onehot, rows):
+    return dot(onehot.astype(BF16), rows).astype(BF16)
+
+
+def marked(onehot, rows):
+    block = dot(onehot.astype(BF16), rows)
+    return (block + (1.0 - jnp.sum(onehot, axis=1, keepdims=True)) * EMPTY).astype(BF16)
+
+
+def spread_x_kernel(owners, capacity, place_ref, x_ref, *out_refs):
     me = lax.axis_index("dp")
-    place = place_ref[...]
-    rows = rows_ref[...]
-    count = rows.shape[0]
-    for k in range(owners):
-        first = (me ^ k) * capacity
-        onehot = (iota((capacity, count), 0) + first == place).astype(F32)
-        block = dot(onehot.astype(BF16), rows)
-        if mark:
-            filled = jnp.sum(onehot, axis=1, keepdims=True)
-            block = block + (1.0 - filled) * EMPTY
-        out_refs[k][...] = block.astype(BF16)
+    for k, ref in zip(far_first(owners), out_refs):
+        ref[...] = marked(selection((me ^ k) * capacity, capacity, place_ref[...]), x_ref[...])
+
+
+def spread_dy_kernel(owners, capacity, place_ref, x_ref, dy_ref, *out_refs):
+    me = lax.axis_index("dp")
+    for k, ref in enumerate(out_refs):
+        onehot = selection((me ^ k) * capacity, capacity, place_ref[...])
+        if 0 < k < owners // 2:
+            ref[:capacity] = marked(onehot, x_ref[...])
+        ref[-capacity:] = selected(onehot, dy_ref[...])
 
 
 def lookup_kernel(place_ref, out_ref):
@@ -97,7 +115,7 @@
     me = lax.axis_index("dp")
     count, width = xhat_ref.shape
     half = width // HEADS
-    valid = [blocks[k][:, 0:LANES].astype(F32) != EMPTY for k in range(owners)]
+    valid = [blocks[k][:capacity, 0:LANES].astype(F32) != EMPTY for k in range(owners)]
     counts = [jnp.sum(v.astype(F32), axis=0, keepdims=True) for v in valid]
     source = iota((owners, LANES), 0) ^ me
     starts = jnp.zeros((owners, LANES), F32)
@@ -113,7 +131,7 @@
     place_ref[...] = place
     column = target[:, 0:1].astype(jnp.int32)
     unplace_ref[...] = (iota((slots, count), 1) == column).astype(F32).astype(BF16)
-    received = jnp.concatenate([blocks[k][...] for k in range(owners)], axis=0)
+    received = jnp.concatenate([blocks[k][:capacity] for k in range(owners)], axis=0)
     x = dot(place, received)
     center = x - jnp.mean(x, axis=1, keepdims=True)
     rstd = lax.rsqrt(jnp.mean(center * center, axis=1, keepdims=True) + EPSILON)
@@ -195,32 +213,16 @@
     )
 
 
-def backward_kernel(owners, *refs):
-    blocks = refs[:owners]
-    (
-        place_ref, act_ref, slope_ref, nhat_ref, a_rstd_ref, weights_ref, tangent_ref, q_t_ref,
-        w_out_ref, dy_ref, dpre_ref, datt_ref, datt_t_ref, dkv_t_ref,
-    ) = refs[owners:]
-    count, width = dy_ref.shape
+def attend_backward(
+    pairs, act_ref, slope_ref, weights_ref, tangent_ref, q_t_ref, datt_ref, datt_t_ref,
+    dpre_ref, dkv_t_ref,
+):
+    count, width = datt_ref.shape
     half = width // HEADS
-    received = jnp.concatenate([blocks[k][...] for k in range(owners)], axis=0)
-    dy = dot(place_ref[...], received).astype(BF16)
-    dy_ref[...] = dy
-    dgated = dot_nt(dy, w_out_ref[...])
-    nhat = nhat_ref[...].astype(F32)
-    dpre_ref[:, 0:width] = (dgated * nhat * slope_ref[:, 0:width].astype(F32)).astype(BF16)
-    dnhat = dgated * act_ref[:, 0:width].astype(F32)
-    datt = a_rstd_ref[:, 0:1] * (
-        dnhat
-        - jnp.mean(dnhat, axis=1, keepdims=True)
-        - nhat * jnp.mean(dnhat * nhat, axis=1, keepdims=True)
-    )
-    datt_ref[...] = datt.astype(BF16)
-    datt_t_ref[...] = datt.T.astype(BF16)
     lane = iota((QUERIES, LANES), 1)
     steps = count // QUERIES
     heads = LANES // half
-    for pair in range(width // LANES):
+    for pair in pairs:
         lanes = slice(pair * LANES, (pair + 1) * LANES)
         dq = []
         dk_t = [[None] * steps for _ in range(heads)]
@@ -260,10 +262,37 @@
             dpre_ref[:, columns] = (grad * slope).astype(BF16)
 
 
-def input_kernel(
-    owners, capacity, dpre_ref, w_ref, xhat_ref, x_rstd_ref, dy_ref, unplace_ref, out_ref
-):
-    me = lax.axis_index("dp")
+def cotangent_kernel(owners, capacity, *refs):
+    blocks = refs[:owners]
+    (
+        place_ref, nhat_ref, a_rstd_ref, w_out_ref, act_ref, slope_ref,
+        dy_ref, dpre_ref, datt_ref, datt_t_ref,
+    ) = refs[owners:]
+    width = dy_ref.shape[1]
+    received = jnp.concatenate([blocks[k][-capacity:] for k in range(owners)], axis=0)
+    dy = dot(place_ref[...], received).astype(BF16)
+    dy_ref[...] = dy
+    dgated = dot_nt(dy, w_out_ref[...])
+    nhat = nhat_ref[...].astype(F32)
+    dpre_ref[...] = (dgated * nhat * slope_ref[:, 0:width].astype(F32)).astype(BF16)
+    dnhat = dgated * act_ref[:, 0:width].astype(F32)
+    datt = a_rstd_ref[:, 0:1] * (
+        dnhat
+        - jnp.mean(dnhat, axis=1, keepdims=True)
+        - nhat * jnp.mean(dnhat * nhat, axis=1, keepdims=True)
+    )
+    datt_ref[...] = datt.astype(BF16)
+    datt_t_ref[...] = datt.T.astype(BF16)
+
+
+def attention_kernel(dpre_u_ref, *refs):
+    dpre_ref = refs[7]
+    width = dpre_u_ref.shape[1]
+    dpre_ref[:, 0:width] = dpre_u_ref[...]
+    attend_backward(range(width // LANES), *refs)
+
+
+def input_kernel(dpre_ref, w_ref, xhat_ref, x_rstd_ref, dy_ref, dx_ref):
     dxhat = dot_nt(dpre_ref[...], w_ref[...])
     xhat = xhat_ref[...].astype(F32)
     dx = dy_ref[...].astype(F32) + x_rstd_ref[:, 0:1] * (
@@ -271,67 +300,112 @@
         - jnp.mean(dxhat, axis=1, keepdims=True)
         - xhat * jnp.mean(dxhat * xhat, axis=1, keepdims=True)
     )
-    rows = dot(unplace_ref[...], dx.astype(BF16)).astype(BF16)
+    dx_ref[...] = dx.astype(BF16)
+
+
+def return_kernel(owners, capacity, dx_ref, unplace_ref, out_ref):
+    me = lax.axis_index("dp")
+    rows = dot(unplace_ref[...], dx_ref[...]).astype(BF16)
     for k in range(owners):
         at = pl.ds(pl.multiple_of((me ^ k) * capacity, capacity), capacity)
         out_ref[at, :] = rows[k * capacity : (k + 1) * capacity]
 
 
-def weight_kernel(owners, groups, xhat_t_ref, dpre_ref, gated_t_ref, dy_ref, kept_ref, sent_ref):
-    me = lax.axis_index("dp")
+def term_rows(owners, groups, width):
+    in_rows = width // groups * (4 * width // owners) // LANES
+    return in_rows, width // groups * (width // owners) // LANES
+
+
+def store_terms(grads, kept_ref, sent_ref, groups):
     group = lax.axis_index("rep")
-    in_grad = dot(xhat_t_ref[...], dpre_ref[...])
-    out_grad = dot(gated_t_ref[...], dy_ref[...])
-    in_cols = in_grad.shape[1] // owners
-    out_cols = out_grad.shape[1] // owners
-    part = in_grad.shape[0] // groups
-    in_rows = part * in_cols // LANES
     for r in range(groups):
-        rows = slice(r * part, (r + 1) * part)
         relative = group ^ r
         for target, ref in ((0, kept_ref), (1, sent_ref)):
 
             @pl.when((relative & 1) == target)
             def _():
-                for d in range(owners):
-                    side = (me ^ d) & 1
-                    ref[relative >> 1, side, d // 2, 0:in_rows, :] = fold(
-                        in_grad[rows, d * in_cols : (d + 1) * in_cols]
-                    ).astype(BF16)
-                    ref[relative >> 1, side, d // 2, in_rows:, :] = fold(
-                        out_grad[rows, d * out_cols : (d + 1) * out_cols]
-                    ).astype(BF16)
+                at = 0
+                for grad in grads:
+                    part = grad.shape[0] // groups
+                    piece = fold(grad[r * part : (r + 1) * part]).astype(BF16)
+                    ref[relative >> 1, at : at + piece.shape[0], :] = piece
+                    at += piece.shape[0]
+
+
+def columns_of(grad, owners_in):
+    step = grad.shape[1] // owners_in
+    return [grad[:, c : c + step] for c in range(0, grad.shape[1], step)]
+
+
+def early_weight_kernel(
+    owners, groups, xhat_t_ref, dpre_ref, gated_t_ref, dy_ref, kept_ref, sent_ref
+):
+    grads = columns_of(dot(xhat_t_ref[...], dpre_ref[...]), owners // 4)
+    grads += columns_of(dot(gated_t_ref[...], dy_ref[...]), owners)
+    store_terms(grads, kept_ref, sent_ref, groups)
+
+
+def late_weight_kernel(owners, groups, xhat_t_ref, dpre_ref, kept_ref, sent_ref):
+    width = xhat_t_ref.shape[0]
+    grads = columns_of(dot(xhat_t_ref[...], dpre_ref[:, width:]), owners - owners // 4)
+    store_terms(grads, kept_ref, sent_ref, groups)
 
 
 def added(first, second):
     return first.astype(F32) + second.astype(F32)
 
 
-def core_sum_kernel(kept_ref, got_ref, a_kept_ref, a_sent_ref, b_kept_ref, b_sent_ref):
-    half = kept_ref.shape[2] // 2
-    a_sent_ref[...] = added(kept_ref[1, :, :half], got_ref[1, :, :half]).astype(BF16)
-    b_sent_ref[...] = added(kept_ref[:, 1, half:], got_ref[:, 1, half:]).astype(BF16)
-    a_kept_ref[...] = added(kept_ref[0, :, :half], got_ref[0, :, :half]).astype(BF16)
-    b_kept_ref[...] = added(kept_ref[:, 0, half:], got_ref[:, 0, half:]).astype(BF16)
-
-
-def side_sum_kernel(
-    a_ref, a_got_ref, b_ref, b_got_ref, a_kept_ref, a_sent_ref, b_kept_ref, b_sent_ref
-):
-    a_sent_ref[...] = added(a_ref[1], a_got_ref[1]).astype(BF16)
-    b_sent_ref[...] = added(b_ref[1], b_got_ref[1]).astype(BF16)
-    a_kept_ref[...] = added(a_ref[0], a_got_ref[0]).astype(BF16)
-    b_kept_ref[...] = added(b_ref[0], b_got_ref[0]).astype(BF16)
-
-
-def plane_sum_kernel(a_ref, a_got_ref, b_ref, b_got_ref, *refs):
-    outs, total_ref = refs[:-1], refs[-1]
-    half = a_ref.shape[0]
-    total_ref[:half] = added(a_ref[...], a_got_ref[...]).astype(BF16)
-    total_ref[half:] = added(b_ref[...], b_got_ref[...]).astype(BF16)
-    pair = lax.axis_index("dp") >> 1
+def core_sum_kernel(kept_ref, got_ref, out_kept_ref, out_sent_ref):
+    out_sent_ref[...] = added(kept_ref[1], got_ref[1]).astype(BF16)
+    out_kept_ref[...] = added(kept_ref[0], got_ref[0]).astype(BF16)
+
+
+def side_sum_kernel(owners, step, kept_ref, got_ref, out_kept_ref, out_sent_ref):
+    me = lax.axis_index("dp")
+    first = owners - kept_ref.shape[1] // step
+    for d in range(first, owners):
+        rows = slice((d - first) * step, (d - first + 1) * step)
+        at = (d - first) // 2 * step
+        term = added(kept_ref[:, rows, :], got_ref[:, rows, :]).astype(BF16)
+        for target, ref in ((0, out_kept_ref), (1, out_sent_ref)):
+
+            @pl.when(((me ^ d) & 1) == target)
+            def _():
+                ref[:, at : at + step, :] = term
+
+
+def split_pairs(owners, sizes, first_ref, second_ref, kept_ref, sent_ref):
+    me = lax.axis_index("dp")
+    at = 0
+    for number, step in sizes:
+        base = at // 2
+        for d in range(number):
+            rows = slice(at, at + step)
+            term = added(first_ref[rows, :], second_ref[rows, :]).astype(BF16)
+            for target, ref in ((0, kept_ref), (1, sent_ref)):
+
+                @pl.when(((me ^ d) & 1) == target)
+                def _():
+                    ref[base + d // 2 * step : base + (d // 2 + 1) * step, :] = term
+
+            at += step
+
+
+def plane_sum_kernel(owners, in_rows, out_rows, *refs):
+    early_ref, early_got_ref, late_ref, late_got_ref = refs[:4]
+    outs, total_ref = refs[4:-1], refs[-1]
+    early = early_ref.shape[0]
+    total_ref[:early] = added(early_ref[...], early_got_ref[...]).astype(BF16)
+    total_ref[early:] = added(late_ref[...], late_got_ref[...]).astype(BF16)
+    here = lax.axis_index("dp") >> 1
+    quarter = owners // 8 * in_rows
     for k, ref in enumerate(outs):
-        ref[...] = total_ref[pair ^ k]
+        pair = here ^ k
+        first = pair * in_rows
+        first = jnp.where(first < quarter, first, first - quarter + early)
+        ref[0:in_rows, :] = total_ref[pl.ds(pl.multiple_of(first, in_rows), in_rows), :]
+        first = quarter + pair * out_rows
+        ref[in_rows:, :] = total_ref[pl.ds(pl.multiple_of(first, out_rows), out_rows), :]
 
 
 def total_kernel(*refs):
@@ -361,18 +435,21 @@
     return lax.ppermute(value, axis, [(i, i ^ distance) for i in range(size)])
 
 
-def exchange(blocks, after=None):
-    got = [blocks[0]]
-    for k in range(1, len(blocks)):
-        block = blocks[k]
-        if after is not None:
-            block, after[k] = lax.optimization_barrier((block, after[k]))
-        got.append(swap(block, "dp", k))
-    return got
-
-
 def ordered(value, *earlier):
     return lax.optimization_barrier((value,) + earlier)[0]
+
+
+def exchange(far_x, blocks):
+    owners = len(blocks)
+    got_x, got = list(blocks), list(blocks)
+    for k, block in zip(far_first(owners), far_x):
+        got_x[k] = swap(block, "dp", k) if k else block
+    for k in range(1, owners):
+        if k < owners // 2:
+            got_x[k] = got[k] = swap(blocks[k], "dp", k)
+        else:
+            got[k] = swap(ordered(blocks[k], got_x[k]), "dp", k)
+    return got_x, got
 
 
 def on_device(events, grad_out, w_uvqk, w_out, send_place, send_counts, user_ids):
@@ -383,7 +460,6 @@
     slots = owners * capacity
     steps = count // QUERIES
     spans = max(high - low for low, high in map(key_range, range(steps)))
-    block_shapes = [shape((capacity, width))] * owners
     route = 2 * slots * count * width
     square = shape((count, width))
     square_t = shape((width, count))
@@ -393,14 +469,20 @@
     project = 2 * count * width * 4 * width
     attend = 2 * count * spans * width
 
-    spread = functools.partial(spread_kernel, owners, capacity)
-    x_blocks = call(functools.partial(spread, True), block_shapes, send_place, events, flops=route)
-    dy_blocks = call(
-        functools.partial(spread, False), block_shapes, send_place, grad_out, flops=route
+    far_x = call(
+        functools.partial(spread_x_kernel, owners, capacity),
+        [shape((capacity, width))] * (owners // 2 + 1), send_place, events, flops=route // 2,
+    )
+    blocks = call(
+        functools.partial(spread_dy_kernel, owners, capacity),
+        [
+            shape(((2 if 0 < k < owners // 2 else 1) * capacity, width))
+            for k in range(owners)
+        ],
+        send_place, events, grad_out, flops=route,
     )
     lookup = call(lookup_kernel, shape((count, slots)), send_place)
-    x_blocks = exchange(x_blocks)
-    dy_blocks = exchange(dy_blocks, x_blocks)
+    x_blocks, dy_blocks = exchange(far_x, blocks)
     (
         place, unplace, act, slope, xhat, xhat_t, x_rstd,
         weights, tangent, nhat, a_rstd, gated_t, q_t,
@@ -414,53 +496,72 @@
         flops=route + project + 2 * attend, transcendentals=HEADS * count * spans,
         scratch=[pltpu.VMEM((count, width), F32)], vmem=28,
     )
-    owned_dy, dpre = call(
-        functools.partial(backward_kernel, owners), [square, wide],
-        *dy_blocks, place, act, slope, nhat, a_rstd, weights, tangent, q_t, w_out,
-        flops=route + project // 4 + 4 * attend,
-        scratch=[
-            pltpu.VMEM((count, width), BF16),
-            pltpu.VMEM((width, count), BF16),
-            pltpu.VMEM((2, LANES, count), F32),
-        ],
-        vmem=28,
+    owned_dy, dpre_u, datt, datt_t = call(
+        functools.partial(cotangent_kernel, owners, capacity),
+        [square, square, square, square_t],
+        *dy_blocks, place, nhat, a_rstd, w_out, act, slope, flops=route + project // 4,
+    )
+    in_rows, out_rows = term_rows(owners, groups, width)
+    early_sizes = ((owners // 4, in_rows), (owners, out_rows))
+    late_sizes = ((owners - owners // 4, in_rows),)
+    early, late = (sum(n * rows for n, rows in sizes) for sizes in (early_sizes, late_sizes))
+    early_kept, early_sent = call(
+        functools.partial(early_weight_kernel, owners, groups),
+        [shape((2, early, LANES))] * 2, xhat_t, dpre_u, gated_t, owned_dy, flops=project // 2,
+    )
+    dpre = call(
+        attention_kernel, wide,
+        dpre_u, act, slope, weights, tangent, q_t, ordered(datt, early_sent), datt_t,
+        flops=4 * attend, scratch=[pltpu.VMEM((2, LANES, count), F32)], vmem=28,
+    )
+    early_kept, early_sent = call(
+        core_sum_kernel, [shape((early, LANES))] * 2, early_kept, swap(early_sent, "rep", 1)
+    )
+    early_got = swap(early_sent, "rep", 2)
+    late_kept, late_sent = call(
+        functools.partial(late_weight_kernel, owners, groups),
+        [shape((2, late, LANES))] * 2, xhat_t, ordered(dpre, early_sent), flops=project,
+    )
+    dx = call(
+        input_kernel, square, ordered(dpre, late_sent), w_uvqk, xhat, x_rstd, owned_dy,
+        flops=project,
+    )
+    late_kept, late_sent = call(
+        functools.partial(side_sum_kernel, owners, in_rows), [shape((2, late // 2, LANES))] * 2,
+        late_kept, swap(late_sent, "rep", 1),
+    )
+    back = call(
+        functools.partial(return_kernel, owners, capacity), shape((slots, width)),
+        ordered(dx, late_sent), unplace, flops=route,
+    )
+    late_got = swap(late_sent, "dp", 1)
+    back = lax.all_to_all(back, "dp", split_axis=0, concat_axis=0, tiled=True)
+    early_kept, early_sent = call(
+        functools.partial(split_pairs, owners, early_sizes), [shape((early // 2, LANES))] * 2,
+        early_kept, early_got, flops=WAITING,
+    )
+    late_kept, late_sent = call(
+        core_sum_kernel, [shape((late // 2, LANES))] * 2, late_kept, late_got, flops=WAITING,
     )
     pairs = owners // 2
-    in_rows = width // groups * (4 * width // owners) // LANES
-    rows = in_rows + width // groups * (width // owners) // LANES
-    kept, sent = call(
-        functools.partial(weight_kernel, owners, groups),
-        [shape((2, 2, pairs, rows, LANES))] * 2,
-        xhat_t, dpre, gated_t, owned_dy, flops=project + project // 4,
-    )
-    back = call(
-        functools.partial(input_kernel, owners, capacity), shape((slots, width)),
-        ordered(dpre, sent), w_uvqk, xhat, x_rstd, owned_dy, unplace, flops=project + route,
-    )
-    a_kept, a_sent, b_kept, b_sent = call(
-        core_sum_kernel, [shape((2, pairs // 2, rows, LANES))] * 4, kept, swap(sent, "rep", 1)
-    )
-    back = ordered(back, a_sent, b_sent)
-    back = lax.all_to_all(back, "dp", split_axis=0, concat_axis=0, tiled=True)
-    a_kept, a_sent, b_kept, b_sent = call(
-        side_sum_kernel, [shape((pairs // 2, rows, LANES))] * 4,
-        a_kept, swap(a_sent, "rep", 2), b_kept, swap(b_sent, "dp", 1),
-    )
+    rows = in_rows + out_rows
     pieces = call(
-        plane_sum_kernel, [shape((rows, LANES))] * pairs,
-        a_kept, swap(a_sent, "dp", 1), b_kept, swap(b_sent, "rep", 2),
-        scratch=[pltpu.VMEM((pairs, rows, LANES), BF16)],
+        functools.partial(plane_sum_kernel, owners, in_rows, out_rows),
+        [shape((rows, LANES))] * pairs,
+        early_kept, swap(early_sent, "dp", 1), late_kept, swap(late_sent, "rep", 2),
+        flops=WAITING, scratch=[pltpu.VMEM(((early + late) // 2, LANES), BF16)],
     )
     pieces = [pieces[0]] + [swap(pieces[k], "dp", 2 * k) for k in range(1, pairs)]
-    own = call(total_kernel, shape((rows, LANES)), *pieces)
+    own = call(total_kernel, shape((rows, LANES)), *pieces, flops=WAITING)
     far = swap(own, "rep", 2)
     shares = [own, swap(own, "rep", 1), far, swap(far, "rep", 1)]
+    grad_events = call(collect_kernel, square, lookup, back, flops=route)
+    shares[0] = ordered(own, grad_events)
     share_in, share_out = call(
         functools.partial(result_kernel, groups, in_rows),
         [shape((width, 4 * width // owners), F32), shape((width // owners, width), F32)],
-        *shares,
-    )
-    grad_events = call(collect_kernel, square, lookup, back, flops=route)
+        *shares, flops=WAITING,
+    )
     return (grad_events, share_in, share_out.T)
 
 

time: 117 us -> 112 us (0.957)
  waiting for transfers between devices: 48.1 us -> 39 us
  starting transfers between devices: 41.5 us -> 45.5 us
    ppermute x25 -> x23, waiting for transfers between devices: 48.1 us -> 39 us  [swap(): return lax.ppermute(value, axis, [(i, i ^ distance) for i in range(size)])]
    ppermute x25 -> x23, starting transfers between devices: 37.9 us -> 40.3 us  [swap(): return lax.ppermute(value, axis, [(i, i ^ distance) for i in range(size)])]
    all_to_all x1, starting transfers between devices: 3.57 us -> 5.21 us  [on_device(): back = lax.all_to_all(back, 'dp', split_axis=0, concat_axis=0, tiled=True)]
    pallas_call x13 -> x18, Pallas kernels: 22.5 us -> 23.2 us  [call(): pl.pallas_call(kernel, out_shape=out_shape, scratch_shapes=scratch, compi...]
  transfers between devices with their start and end apart: 26 -> 24, of which waited for: 14 -> 12; matrix products, arithmetic and copies ran while one was open for 0% -> 0% of each run, Pallas kernels for 11% -> 15%
where the time goes in v3:
time: 112 us
  starting transfers between devices  45.5 us (41%)
  waiting for transfers between devices  39 us (35%)
  Pallas kernels  23.2 us (21%)
  local copies, waits for them, and re-layouts  3.6 us (3%)
    ppermute x23, starting transfers between devices, swap(): return lax.ppermute(value, axis, [(i, i ^ distance) for i in range(size)])  40.3 us
    ppermute x23, waiting for transfers between devices, swap(): return lax.ppermute(value, axis, [(i, i ^ distance) for i in range(size)])  39 us
    pallas_call x18, Pallas kernels, call(): pl.pallas_call(kernel, out_shape=out_shape, scratch_shapes=scratch, compi...  23.2 us
    all_to_all x1, starting transfers between devices, on_device(): back = lax.all_to_all(back, 'dp', split_axis=0, concat_axis=0, tiled=True)  5.21 us
    unnamed x14, local copies, waits for them, and re-layouts  3.6 us
  transfers between devices with their start and end apart: 24, of which 12 were waited for; matrix products, arithmetic and copies ran while one was open for 0% of the time, Pallas kernels for 15%

profile of v3, /device:TPU:0, one launch (start us, length us, event | category | flops | bytes accessed | tf_op | source)
XLA Modules:
  0.0 112.1 jit_solution(5325372884028702595)
XLA Ops:
  0.7 0.8 copy-done.2
  1.5 1.0 copy-done.4
  2.5 0.5 shard_map.87
  3.0 4.1 %collective-permute-start.3 = (bf16[128,512]{1,0:T(8,128)(2,1)S(1)}, bf16[128,512]{1,0:T(8,128)(2,1)S(1)}, u32[]{:S(2)}, u32[]{:S(2)}) collective-permute-start(bf16[128,512]{1,0:T(8,128)(2,1)S(1)} %get-tuple-element.65), channel_id=1, source_target_pairs={{0,16},{4,20},{8,24},{12,28},{16,0},{20,4},{24,8},{28,12},{1,17},{... | collective-permute-start | bytes 393224 | tf_op jit(solution)/shard_map/ppermute | solution.py:435
  7.1 2.3 %collective-permute-start.9 = (bf16[128,512]{1,0:T(8,128)(2,1)S(1)}, bf16[128,512]{1,0:T(8,128)(2,1)S(1)}, u32[]{:S(2)}, u32[]{:S(2)}) collective-permute-start(bf16[128,512]{1,0:T(8,128)(2,1)S(1)} %get-tuple-element.74), channel_id=1, source_target_pairs={{0,28},{4,24},{8,20},{12,16},{16,12},{20,8},{24,4},{28,0},{1,29},{... | collective-permute-start | bytes 393224 | tf_op jit(solution)/shard_map/ppermute | solution.py:435
  9.4 1.0 copy-done.5
  10.5 0.9 shard_map.86
  11.4 0.6 collective-permute-start
  12.3 2.7 %collective-permute-start.2 = (bf16[256,512]{1,0:T(8,128)(2,1)S(1)}, bf16[256,512]{1,0:T(8,128)(2,1)S(1)}, u32[]{:S(2)}, u32[]{:S(2)}) collective-permute-start(bf16[256,512]{1,0:T(8,128)(2,1)S(1)} %get-tuple-element.63), channel_id=1, source_target_pairs={{0,12},{4,8},{8,4},{12,0},{16,28},{20,24},{24,20},{28,16},{1,13},{... | collective-permute-start | bytes 786440 | tf_op jit(solution)/shard_map/ppermute | solution.py:435
  15.0 2.2 %collective-permute-done.3.refs_4_ = bf16[128,512]{1,0:T(8,128)(2,1)S(1)} collective-permute-done((bf16[128,512]{1,0:T(8,128)(2,1)S(1)}, bf16[128,512]{1,0:T(8,128)(2,1)S(1)}, u32[]{:S(2)}, u32[]{:S(2)}) %collective-permute-start.3) | collective-permute-done | bytes 131104 | tf_op jit(solution)/shard_map/ppermute | solution.py:435
  17.1 0.8 collective-permute-start.5
  18.0 2.4 %collective-permute-start.7 = (bf16[128,512]{1,0:T(8,128)(2,1)S(1)}, bf16[128,512]{1,0:T(8,128)(2,1)S(1)}, u32[]{:S(2)}, u32[]{:S(2)}) collective-permute-start(bf16[128,512]{1,0:T(8,128)(2,1)S(1)} %get-tuple-element.71), channel_id=1, source_target_pairs={{0,24},{4,28},{8,16},{12,20},{16,8},{20,12},{24,0},{28,4},{1,25},{... | collective-permute-start | bytes 393224 | tf_op jit(solution)/shard_map/ppermute | solution.py:435
  20.4 7.3 %collective-permute-done.5.refs_5_ = bf16[128,512]{1,0:T(8,128)(2,1)S(1)} collective-permute-done((bf16[128,512]{1,0:T(8,128)(2,1)S(1)}, bf16[128,512]{1,0:T(8,128)(2,1)S(1)}, u32[]{:S(2)}, u32[]{:S(2)}) %collective-permute-start.5) | collective-permute-done | bytes 131104 | tf_op jit(solution)/shard_map/ppermute | solution.py:435
  27.7 4.3 %collective-permute-start.10 = (bf16[128,512]{1,0:T(8,128)(2,1)S(1)}, bf16[128,512]{1,0:T(8,128)(2,1)S(1)}, u32[]{:S(2)}, u32[]{:S(2)}) collective-permute-start(bf16[128,512]{1,0:T(8,128)(2,1)S(1)} %get-tuple-element.75), channel_id=1, source_target_pairs={{0,28},{4,24},{8,20},{12,16},{16,12},{20,8},{24,4},{28,0},{1,29},{... | collective-permute-start | bytes 393224 | tf_op jit(solution)/shard_map/ppermute | solution.py:435
  32.0 2.0 %collective-permute-done.7.refs_6_ = bf16[128,512]{1,0:T(8,128)(2,1)S(1)} collective-permute-done((bf16[128,512]{1,0:T(8,128)(2,1)S(1)}, bf16[128,512]{1,0:T(8,128)(2,1)S(1)}, u32[]{:S(2)}, u32[]{:S(2)}) %collective-permute-start.7) | collective-permute-done | bytes 131104 | tf_op jit(solution)/shard_map/ppermute | solution.py:435
  34.0 4.7 %collective-permute-start.4 = (bf16[128,512]{1,0:T(8,128)(2,1)S(1)}, bf16[128,512]{1,0:T(8,128)(2,1)S(1)}, u32[]{:S(2)}, u32[]{:S(2)}) collective-permute-start(bf16[128,512]{1,0:T(8,128)(2,1)S(1)} %get-tuple-element.66), channel_id=1, source_target_pairs={{0,16},{4,20},{8,24},{12,28},{16,0},{20,4},{24,8},{28,12},{1,17},{... | collective-permute-start | bytes 393224 | tf_op jit(solution)/shard_map/ppermute | solution.py:435
  39.0 0.9 collective-permute-start.8
  39.9 0.7 copy-done.6
  40.5 7.5 %shard_map.88 = (bf16[512,1024]{1,0:T(8,128)(2,1)S(1)}, bf16[1024,512]{1,0:T(8,128)(2,1)S(1)}, bf16[512,2048]{1,0:T(8,128)(2,1)S(1)}, bf16[512,2048]{1,0:T(8,128...) custom-call(bf16[128,512]{1,0:T(8,128)(2,1)S(1)} %get-tuple-element., ...), custom_call_target="tpu_custom_call" | custom-call | flops 2147483648 | bytes 21366784 | tf_op jit(solution)/shard_map/pallas_call | solution.py:37
  48.1 2.8 %collective-permute-done.4.refs_4_ = bf16[128,512]{1,0:T(8,128)(2,1)S(1)} collective-permute-done((bf16[128,512]{1,0:T(8,128)(2,1)S(1)}, bf16[128,512]{1,0:T(8,128)(2,1)S(1)}, u32[]{:S(2)}, u32[]{:S(2)}) %collective-permute-start.4) | collective-permute-done | bytes 131104 | tf_op jit(solution)/shard_map/ppermute | solution.py:435
  50.9 2.9 %collective-permute-done.6.refs_5_ = bf16[128,512]{1,0:T(8,128)(2,1)S(1)} collective-permute-done((bf16[128,512]{1,0:T(8,128)(2,1)S(1)}, bf16[128,512]{1,0:T(8,128)(2,1)S(1)}, u32[]{:S(2)}, u32[]{:S(2)}) %collective-permute-start.6) | collective-permute-done | bytes 131104 | tf_op jit(solution)/shard_map/ppermute | solution.py:435
  53.8 1.5 %shard_map.89 = (bf16[512,512]{1,0:T(8,128)(2,1)S(1)}, bf16[512,512]{1,0:T(8,128)(2,1)S(1)}, bf16[512,512]{1,0:T(8,128)(2,1)S(1)}, bf16[512,512]{1,0:T(8,128)(2,1)S(1)}) custom-call(bf16[128,512]{1,0:T(8,128)(2,1)S(1)} %get-tuple-element.60.refs_0_, bf16[256,512]{1,0:T(8,128)(2,1)S(1)} %collective-permute-done.refs_1_, ...), custom_call_target="tpu_custom_call" | custom-call | flops 805306368 | bytes 10092544 | tf_op jit(solution)/shard_map/pallas_call | solution.py:37
  55.4 1.3 %shard_map.90 = (bf16[2,1024,128]{2,1,0:T(8,128)(2,1)S(1)}, bf16[2,1024,128]{2,1,0:T(8,128)(2,1)S(1)}) custom-call(bf16[512,512]{1,0:T(8,128)(2,1)S(1)} %get-tuple-element.87.xhat_t_ref, bf16[512,512]{1,0:T(8,128)(2,1)S(1)} %get-tuple-element.82.dpre_ref.dpre_u_ref, bf16[512,512]{1,0:T(8,128)(2,1)S(1)} %get-tuple-element.88.gated_t_ref, ...), custom_call_target="tpu_custom_call" | custom-call | flops 536870912 | bytes 3145728 | tf_op jit(solution)/shard_map/pallas_call | solution.py:37
  56.8 3.3 %shard_map.91.dpre_ref = bf16[512,2048]{1,0:T(8,128)(2,1)S(1)} custom-call(bf16[512,512]{1,0:T(8,128)(2,1)S(1)} %get-tuple-element.82.dpre_ref.dpre_u_ref, bf16[512,2048]{1,0:T(8,128)(2,1)S(1)} %get-tuple-element.80.refs_12_.refs_0_, bf16[512,2048]{1,0:T(8,128)(2,1)S(1)} %get-tuple-element.81.refs_13_.refs_1_, ...), custom_call_target="tpu_custom_call" | custom-call | flops 1073741824 | bytes 16777216 | tf_op jit(solution)/shard_map/pallas_call | solution.py:37
  60.2 1.2 %shard_map.93 = (bf16[2,1536,128]{2,1,0:T(8,128)(2,1)S(1)}, bf16[2,1536,128]{2,1,0:T(8,128)(2,1)S(1)}) custom-call(bf16[512,512]{1,0:T(8,128)(2,1)S(1)} %get-tuple-element.87.xhat_t_ref, bf16[512,2048]{1,0:T(8,128)(2,1)S(1)} %shard_map.91.dpre_ref), custom_call_target="tpu_custom_call" | custom-call | flops 1073741824 | bytes 4194304 | tf_op jit(solution)/shard_map/pallas_call | solution.py:37
  61.4 0.6 collective-permute-start.12
  62.0 1.6 %shard_map.94.dx_ref = bf16[512,512]{1,0:T(8,128)(2,1)S(1)} custom-call(bf16[512,2048]{1,0:T(8,128)(2,1)S(1)} %shard_map.91.dpre_ref, bf16[512,2048]{1,0:T(8,128)(2,1)S(1)} %copy-done, bf16[512,512]{1,0:T(8,128)(2,1)S(1)} %get-tuple-element.98.xhat_ref, f32[512,128]{1,0:T(8,128)S(1)} %get-tuple-element.99.x_rstd_ref, ...), custom_call_target="tpu_custom_call" | custom-call | flops 1073741824 | bytes 6029312 | tf_op jit(solution)/shard_map/pallas_call | solution.py:37
  63.5 0.3 collective-permute-done.12.got_ref
  63.9 0.3 shard_map.95
  64.2 1.4 %collective-permute-start.15 = (bf16[2,768,128]{2,1,0:T(8,128)(2,1)S(1)}, bf16[2,768,128]{2,1,0:T(8,128)(2,1)S(1)}, u32[]{:S(2)}, u32[]{:S(2)}) collective-permute-start(bf16[2,768,128]{2,1,0:T(8,128)(2,1)S(1)} %get-tuple-element.101), channel_id=1, source_target_pairs={{0,4},{4,0},{8,12},{12,8},{16,20},{20,16},{24,28},{28,24},{1,5},{5... | collective-permute-start | bytes 1179656 | tf_op jit(solution)/shard_map/ppermute | solution.py:435
  65.6 1.7 %shard_map.96 = bf16[1024,512]{1,0:T(8,128)(2,1)} custom-call(bf16[512,512]{1,0:T(8,128)(2,1)S(1)} %shard_map.94.dx_ref, bf16[1024,512]{1,0:T(8,128)(2,1)S(1)} %get-tuple-element.103.unplace_ref), custom_call_target="tpu_custom_call" | custom-call | flops 536870912 | bytes 2621440 | tf_op jit(solution)/shard_map/pallas_call | solution.py:37
  67.3 5.2 %all-to-all-start = ((bf16[8,128,512]{2,1,0:T(8,128)(2,1)}), bf16[8,128,512]{2,1,0:T(8,128)(2,1)S(1)}, u32[]{:S(2)}, u32[]{:S(2)}) async-start(bf16[8,128,512]{2,1,0:T(8,128)(2,1)} %bitcast), calls=%async_computation | async-start | bytes 2097152 | tf_op jit(solution)/shard_map/all_to_all | solution.py:538
  72.5 1.5 %collective-permute-start.13 = (bf16[1024,128]{1,0:T(8,128)(2,1)S(1)}, bf16[1024,128]{1,0:T(8,128)(2,1)S(1)}, u32[]{:S(2)}, u32[]{:S(2)}) collective-permute-start(bf16[1024,128]{1,0:T(8,128)(2,1)S(1)} %get-tuple-element.94), channel_id=1, source_target_pairs={{0,2},{1,3},{2,0},{3,1},{4,6},{5,7},{6,4},{7,5},{8,10},{9,11},{10,... | collective-permute-start | bytes 786440 | tf_op jit(solution)/shard_map/ppermute | solution.py:435
  74.1 3.1 %collective-permute-done.15.got_ref = bf16[2,768,128]{2,1,0:T(8,128)(2,1)S(1)} collective-permute-done((bf16[2,768,128]{2,1,0:T(8,128)(2,1)S(1)}, bf16[2,768,128]{2,1,0:T(8,128)(2,1)S(1)}, u32[]{:S(2)}, u32[]{:S(2)}) %collective-permute-start.15) | collective-permute-done | bytes 393248 | tf_op jit(solution)/shard_map/ppermute | solution.py:435
  77.2 1.6 %collective-permute-start.16 = (bf16[768,128]{1,0:T(8,128)(2,1)S(1)}, bf16[768,128]{1,0:T(8,128)(2,1)S(1)}, u32[]{:S(2)}, u32[]{:S(2)}) collective-permute-start(bf16[768,128]{1,0:T(8,128)(2,1)S(1)} %get-tuple-element.109), channel_id=1, source_target_pairs={{0,2},{1,3},{2,0},{3,1},{4,6},{5,7},{6,4},{7,5},{8,10},{9,11},{10,... | collective-permute-start | bytes 589832 | tf_op jit(solution)/shard_map/ppermute | solution.py:435
  78.8 2.9 %collective-permute-done.13.second_ref = bf16[1024,128]{1,0:T(8,128)(2,1)S(1)} collective-permute-done((bf16[1024,128]{1,0:T(8,128)(2,1)S(1)}, bf16[1024,128]{1,0:T(8,128)(2,1)S(1)}, u32[]{:S(2)}, u32[]{:S(2)}) %collective-permute-start.13) | collective-permute-done | bytes 262176 | tf_op jit(solution)/shard_map/ppermute | solution.py:435
  81.8 2.1 %collective-permute-start.14 = (bf16[512,128]{1,0:T(8,128)(2,1)S(1)}, bf16[512,128]{1,0:T(8,128)(2,1)S(1)}, u32[]{:S(2)}, u32[]{:S(2)}) collective-permute-start(bf16[512,128]{1,0:T(8,128)(2,1)S(1)} %get-tuple-element.106), channel_id=1, source_target_pairs={{0,4},{4,0},{8,12},{12,8},{16,20},{20,16},{24,28},{28,24},{1,5},{5... | collective-permute-start | bytes 393224 | tf_op jit(solution)/shard_map/ppermute | solution.py:435
  84.0 3.7 %collective-permute-done.14.refs_1_ = bf16[512,128]{1,0:T(8,128)(2,1)S(1)} collective-permute-done((bf16[512,128]{1,0:T(8,128)(2,1)S(1)}, bf16[512,128]{1,0:T(8,128)(2,1)S(1)}, u32[]{:S(2)}, u32[]{:S(2)}) %collective-permute-start.14) | collective-permute-done | bytes 131104 | tf_op jit(solution)/shard_map/ppermute | solution.py:435
  87.9 5.6 %collective-permute-start.17 = (bf16[320,128]{1,0:T(8,128)(2,1)S(1)}, bf16[320,128]{1,0:T(8,128)(2,1)S(1)}, u32[]{:S(2)}, u32[]{:S(2)}) collective-permute-start(bf16[320,128]{1,0:T(8,128)(2,1)S(1)} %get-tuple-element.111), channel_id=1, source_target_pairs={{0,8},{4,12},{8,0},{12,4},{16,24},{20,28},{24,16},{28,20},{1,9},{5... | collective-permute-start | bytes 245768 | tf_op jit(solution)/shard_map/ppermute | solution.py:435
  93.5 2.1 %collective-permute-start.18 = (bf16[320,128]{1,0:T(8,128)(2,1)S(1)}, bf16[320,128]{1,0:T(8,128)(2,1)S(1)}, u32[]{:S(2)}, u32[]{:S(2)}) collective-permute-start(bf16[320,128]{1,0:T(8,128)(2,1)S(1)} %get-tuple-element.112), channel_id=1, source_target_pairs={{0,16},{4,20},{8,24},{12,28},{16,0},{20,4},{24,8},{28,12},{1,17},{... | collective-permute-start | bytes 245768 | tf_op jit(solution)/shard_map/ppermute | solution.py:435
  95.5 0.4 collective-permute-start.19
  95.9 3.1 %collective-permute-done.17.refs_1_ = bf16[320,128]{1,0:T(8,128)(2,1)S(1)} collective-permute-done((bf16[320,128]{1,0:T(8,128)(2,1)S(1)}, bf16[320,128]{1,0:T(8,128)(2,1)S(1)}, u32[]{:S(2)}, u32[]{:S(2)}) %collective-permute-start.17) | collective-permute-done | bytes 81952 | tf_op jit(solution)/shard_map/ppermute | solution.py:435
  99.0 5.7 %collective-permute-done.18.refs_2_ = bf16[320,128]{1,0:T(8,128)(2,1)S(1)} collective-permute-done((bf16[320,128]{1,0:T(8,128)(2,1)S(1)}, bf16[320,128]{1,0:T(8,128)(2,1)S(1)}, u32[]{:S(2)}, u32[]{:S(2)}) %collective-permute-start.18) | collective-permute-done | bytes 81952 | tf_op jit(solution)/shard_map/ppermute | solution.py:435
  104.8 1.6 %collective-permute-start.21 = (bf16[320,128]{1,0:T(8,128)(2,1)S(1)}, bf16[320,128]{1,0:T(8,128)(2,1)S(1)}, u32[]{:S(2)}, u32[]{:S(2)}) collective-permute-start(bf16[320,128]{1,0:T(8,128)(2,1)S(1)} %shard_map.101.refs_0_), channel_id=1, source_target_pairs={{0,2},{1,3},{2,0},{3,1},{4,6},{5,7},{6,4},{7,5},{8,10},{9,11},{10,... | collective-permute-start | bytes 245768 | tf_op jit(solution)/shard_map/ppermute | solution.py:435
  106.4 2.9 %collective-permute-done.21.refs_2_ = bf16[320,128]{1,0:T(8,128)(2,1)S(1)} collective-permute-done((bf16[320,128]{1,0:T(8,128)(2,1)S(1)}, bf16[320,128]{1,0:T(8,128)(2,1)S(1)}, u32[]{:S(2)}, u32[]{:S(2)}) %collective-permute-start.21) | collective-permute-done | bytes 81952 | tf_op jit(solution)/shard_map/ppermute | solution.py:435
  109.3 0.3 shard_map.85.lookup_ref
  109.6 1.5 %shard_map.97 = bf16[512,512]{1,0:T(8,128)(2,1)} custom-call(bf16[512,1024]{1,0:T(8,128)(2,1)S(1)} %shard_map.85.lookup_ref, bf16[1024,512]{1,0:T(8,128)(2,1)S(1)} %bitcast.3), custom_call_target="tpu_custom_call" | custom-call | flops 536870912 | bytes 2621440 | tf_op jit(solution)/shard_map/pallas_call | solution.py:37
  111.1 1.0 shard_map.102
  (32 shorter events, 1.1 us)
Async XLA Ops:
  0.6 39.2 %copy-start = (bf16[512,2048]{1,0:T(8,128)(2,1)S(1)}, bf16[512,2048]{1,0:T(8,128)(2,1)}, u32[]{:S(2)}) copy-start(bf16[512,2048]{1,0:T(8,128)(2,1)} %w_ref.1) | copy-start | bytes 6291460
  0.6 0.8 copy-start.2
  1.5 1.0 copy-start.4
  3.0 14.1 %collective-permute-start.3 = (bf16[128,512]{1,0:T(8,128)(2,1)S(1)}, bf16[128,512]{1,0:T(8,128)(2,1)S(1)}, u32[]{:S(2)}, u32[]{:S(2)}) collective-permute-start(bf16[128,512]{1,0:T(8,128)(2,1)S(1)} %get-tuple-element.65), channel_id=1, source_target_pairs={{0,16},{4,20},{8,24},{12,28},{16,0},{20,4},{24,8},{28,12},{1,17},{... | collective-permute-start | bytes 393224 | tf_op jit(solution)/shard_map/ppermute | solution.py:435
  7.1 10.8 %collective-permute-start.9 = (bf16[128,512]{1,0:T(8,128)(2,1)S(1)}, bf16[128,512]{1,0:T(8,128)(2,1)S(1)}, u32[]{:S(2)}, u32[]{:S(2)}) collective-permute-start(bf16[128,512]{1,0:T(8,128)(2,1)S(1)} %get-tuple-element.74), channel_id=1, source_target_pairs={{0,28},{4,24},{8,20},{12,16},{16,12},{20,8},{24,4},{28,0},{1,29},{... | collective-permute-start | bytes 393224 | tf_op jit(solution)/shard_map/ppermute | solution.py:435
  9.4 1.0 copy-start.5
  11.4 27.3 %collective-permute-start = (bf16[256,512]{1,0:T(8,128)(2,1)S(1)}, bf16[256,512]{1,0:T(8,128)(2,1)S(1)}, u32[]{:S(2)}, u32[]{:S(2)}) collective-permute-start(bf16[256,512]{1,0:T(8,128)(2,1)S(1)} %get-tuple-element.61), channel_id=1, source_target_pairs={{0,4},{4,0},{8,12},{12,8},{16,20},{20,16},{24,28},{28,24},{1,5},{5... | collective-permute-start | bytes 786440 | tf_op jit(solution)/shard_map/ppermute | solution.py:435
  12.0 26.9 %collective-permute-start.1 = (bf16[256,512]{1,0:T(8,128)(2,1)S(1)}, bf16[256,512]{1,0:T(8,128)(2,1)S(1)}, u32[]{:S(2)}, u32[]{:S(2)}) collective-permute-start(bf16[256,512]{1,0:T(8,128)(2,1)S(1)} %get-tuple-element.62), channel_id=1, source_target_pairs={{0,8},{4,12},{8,0},{12,4},{16,24},{20,28},{24,16},{28,20},{1,9},{5... | collective-permute-start | bytes 786440 | tf_op jit(solution)/shard_map/ppermute | solution.py:435
  12.3 27.6 %collective-permute-start.2 = (bf16[256,512]{1,0:T(8,128)(2,1)S(1)}, bf16[256,512]{1,0:T(8,128)(2,1)S(1)}, u32[]{:S(2)}, u32[]{:S(2)}) collective-permute-start(bf16[256,512]{1,0:T(8,128)(2,1)S(1)} %get-tuple-element.63), channel_id=1, source_target_pairs={{0,12},{4,8},{8,4},{12,0},{16,28},{20,24},{24,20},{28,16},{1,13},{... | collective-permute-start | bytes 786440 | tf_op jit(solution)/shard_map/ppermute | solution.py:435
  17.1 10.6 %collective-permute-start.5 = (bf16[128,512]{1,0:T(8,128)(2,1)S(1)}, bf16[128,512]{1,0:T(8,128)(2,1)S(1)}, u32[]{:S(2)}, u32[]{:S(2)}) collective-permute-start(bf16[128,512]{1,0:T(8,128)(2,1)S(1)} %get-tuple-element.68), channel_id=1, source_target_pairs={{0,20},{4,16},{8,28},{12,24},{16,4},{20,0},{24,12},{28,8},{1,21},{... | collective-permute-start | bytes 393224 | tf_op jit(solution)/shard_map/ppermute | solution.py:435
  18.0 16.1 %collective-permute-start.7 = (bf16[128,512]{1,0:T(8,128)(2,1)S(1)}, bf16[128,512]{1,0:T(8,128)(2,1)S(1)}, u32[]{:S(2)}, u32[]{:S(2)}) collective-permute-start(bf16[128,512]{1,0:T(8,128)(2,1)S(1)} %get-tuple-element.71), channel_id=1, source_target_pairs={{0,24},{4,28},{8,16},{12,20},{16,8},{20,12},{24,0},{28,4},{1,25},{... | collective-permute-start | bytes 393224 | tf_op jit(solution)/shard_map/ppermute | solution.py:435
  27.7 20.4 %collective-permute-start.10 = (bf16[128,512]{1,0:T(8,128)(2,1)S(1)}, bf16[128,512]{1,0:T(8,128)(2,1)S(1)}, u32[]{:S(2)}, u32[]{:S(2)}) collective-permute-start(bf16[128,512]{1,0:T(8,128)(2,1)S(1)} %get-tuple-element.75), channel_id=1, source_target_pairs={{0,28},{4,24},{8,20},{12,16},{16,12},{20,8},{24,4},{28,0},{1,29},{... | collective-permute-start | bytes 393224 | tf_op jit(solution)/shard_map/ppermute | solution.py:435
  34.0 16.8 %collective-permute-start.4 = (bf16[128,512]{1,0:T(8,128)(2,1)S(1)}, bf16[128,512]{1,0:T(8,128)(2,1)S(1)}, u32[]{:S(2)}, u32[]{:S(2)}) collective-permute-start(bf16[128,512]{1,0:T(8,128)(2,1)S(1)} %get-tuple-element.66), channel_id=1, source_target_pairs={{0,16},{4,20},{8,24},{12,28},{16,0},{20,4},{24,8},{28,12},{1,17},{... | collective-permute-start | bytes 393224 | tf_op jit(solution)/shard_map/ppermute | solution.py:435
  38.7 15.1 %collective-permute-start.6 = (bf16[128,512]{1,0:T(8,128)(2,1)S(1)}, bf16[128,512]{1,0:T(8,128)(2,1)S(1)}, u32[]{:S(2)}, u32[]{:S(2)}) collective-permute-start(bf16[128,512]{1,0:T(8,128)(2,1)S(1)} %get-tuple-element.69), channel_id=1, source_target_pairs={{0,20},{4,16},{8,28},{12,24},{16,4},{20,0},{24,12},{28,8},{1,21},{... | collective-permute-start | bytes 393224 | tf_op jit(solution)/shard_map/ppermute | solution.py:435
  39.0 14.9 %collective-permute-start.8 = (bf16[128,512]{1,0:T(8,128)(2,1)S(1)}, bf16[128,512]{1,0:T(8,128)(2,1)S(1)}, u32[]{:S(2)}, u32[]{:S(2)}) collective-permute-start(bf16[128,512]{1,0:T(8,128)(2,1)S(1)} %get-tuple-element.72), channel_id=1, source_target_pairs={{0,24},{4,28},{8,16},{12,20},{16,8},{20,12},{24,0},{28,4},{1,25},{... | collective-permute-start | bytes 393224 | tf_op jit(solution)/shard_map/ppermute | solution.py:435
  39.9 0.7 copy-start.6
  40.5 13.3 %copy-start.1 = (bf16[512,512]{1,0:T(8,128)(2,1)S(1)}, bf16[512,512]{1,0:T(8,128)(2,1)}, u32[]{:S(2)}) copy-start(bf16[512,512]{1,0:T(8,128)(2,1)} %refs_11_.1) | copy-start | bytes 1572868
  56.7 3.4 %collective-permute-start.11 = (bf16[2,1024,128]{2,1,0:T(8,128)(2,1)S(1)}, bf16[2,1024,128]{2,1,0:T(8,128)(2,1)S(1)}, u32[]{:S(2)}, u32[]{:S(2)}) collective-permute-start(bf16[2,1024,128]{2,1,0:T(8,128)(2,1)S(1)} %get-tuple-element.90), channel_id=1, source_target_pairs={{0,1},{1,0},{2,3},{3,2},{4,5},{5,4},{6,7},{7,6},{8,9},{9,8},{10,11... | collective-permute-start | bytes 1572872 | tf_op jit(solution)/shard_map/ppermute | solution.py:435
  61.4 2.5 %collective-permute-start.12 = (bf16[2,1536,128]{2,1,0:T(8,128)(2,1)S(1)}, bf16[2,1536,128]{2,1,0:T(8,128)(2,1)S(1)}, u32[]{:S(2)}, u32[]{:S(2)}) collective-permute-start(bf16[2,1536,128]{2,1,0:T(8,128)(2,1)S(1)} %get-tuple-element.96), channel_id=1, source_target_pairs={{0,1},{1,0},{2,3},{3,2},{4,5},{5,4},{6,7},{7,6},{8,9},{9,8},{10,11... | collective-permute-start | bytes 2359304 | tf_op jit(solution)/shard_map/ppermute | solution.py:435
  64.2 12.9 %collective-permute-start.15 = (bf16[2,768,128]{2,1,0:T(8,128)(2,1)S(1)}, bf16[2,768,128]{2,1,0:T(8,128)(2,1)S(1)}, u32[]{:S(2)}, u32[]{:S(2)}) collective-permute-start(bf16[2,768,128]{2,1,0:T(8,128)(2,1)S(1)} %get-tuple-element.101), channel_id=1, source_target_pairs={{0,4},{4,0},{8,12},{12,8},{16,20},{20,16},{24,28},{28,24},{1,5},{5... | collective-permute-start | bytes 1179656 | tf_op jit(solution)/shard_map/ppermute | solution.py:435
  67.3 42.3 %all-to-all-start = ((bf16[8,128,512]{2,1,0:T(8,128)(2,1)}), bf16[8,128,512]{2,1,0:T(8,128)(2,1)S(1)}, u32[]{:S(2)}, u32[]{:S(2)}) async-start(bf16[8,128,512]{2,1,0:T(8,128)(2,1)} %bitcast), calls=%async_computation | async-start | bytes 2097152 | tf_op jit(solution)/shard_map/all_to_all | solution.py:538
  72.5 9.2 %collective-permute-start.13 = (bf16[1024,128]{1,0:T(8,128)(2,1)S(1)}, bf16[1024,128]{1,0:T(8,128)(2,1)S(1)}, u32[]{:S(2)}, u32[]{:S(2)}) collective-permute-start(bf16[1024,128]{1,0:T(8,128)(2,1)S(1)} %get-tuple-element.94), channel_id=1, source_target_pairs={{0,2},{1,3},{2,0},{3,1},{4,6},{5,7},{6,4},{7,5},{8,10},{9,11},{10,... | collective-permute-start | bytes 786440 | tf_op jit(solution)/shard_map/ppermute | solution.py:435
  77.2 10.5 %collective-permute-start.16 = (bf16[768,128]{1,0:T(8,128)(2,1)S(1)}, bf16[768,128]{1,0:T(8,128)(2,1)S(1)}, u32[]{:S(2)}, u32[]{:S(2)}) collective-permute-start(bf16[768,128]{1,0:T(8,128)(2,1)S(1)} %get-tuple-element.109), channel_id=1, source_target_pairs={{0,2},{1,3},{2,0},{3,1},{4,6},{5,7},{6,4},{7,5},{8,10},{9,11},{10,... | collective-permute-start | bytes 589832 | tf_op jit(solution)/shard_map/ppermute | solution.py:435
  81.8 5.9 %collective-permute-start.14 = (bf16[512,128]{1,0:T(8,128)(2,1)S(1)}, bf16[512,128]{1,0:T(8,128)(2,1)S(1)}, u32[]{:S(2)}, u32[]{:S(2)}) collective-permute-start(bf16[512,128]{1,0:T(8,128)(2,1)S(1)} %get-tuple-element.106), channel_id=1, source_target_pairs={{0,4},{4,0},{8,12},{12,8},{16,20},{20,16},{24,28},{28,24},{1,5},{5... | collective-permute-start | bytes 393224 | tf_op jit(solution)/shard_map/ppermute | solution.py:435
  87.9 11.2 %collective-permute-start.17 = (bf16[320,128]{1,0:T(8,128)(2,1)S(1)}, bf16[320,128]{1,0:T(8,128)(2,1)S(1)}, u32[]{:S(2)}, u32[]{:S(2)}) collective-permute-start(bf16[320,128]{1,0:T(8,128)(2,1)S(1)} %get-tuple-element.111), channel_id=1, source_target_pairs={{0,8},{4,12},{8,0},{12,4},{16,24},{20,28},{24,16},{28,20},{1,9},{5... | collective-permute-start | bytes 245768 | tf_op jit(solution)/shard_map/ppermute | solution.py:435
  93.5 11.3 %collective-permute-start.18 = (bf16[320,128]{1,0:T(8,128)(2,1)S(1)}, bf16[320,128]{1,0:T(8,128)(2,1)S(1)}, u32[]{:S(2)}, u32[]{:S(2)}) collective-permute-start(bf16[320,128]{1,0:T(8,128)(2,1)S(1)} %get-tuple-element.112), channel_id=1, source_target_pairs={{0,16},{4,20},{8,24},{12,28},{16,0},{20,4},{24,8},{28,12},{1,17},{... | collective-permute-start | bytes 245768 | tf_op jit(solution)/shard_map/ppermute | solution.py:435
  95.5 9.2 %collective-permute-start.19 = (bf16[320,128]{1,0:T(8,128)(2,1)S(1)}, bf16[320,128]{1,0:T(8,128)(2,1)S(1)}, u32[]{:S(2)}, u32[]{:S(2)}) collective-permute-start(bf16[320,128]{1,0:T(8,128)(2,1)S(1)} %get-tuple-element.113), channel_id=1, source_target_pairs={{0,24},{4,28},{8,16},{12,20},{16,8},{20,12},{24,0},{28,4},{1,25},{... | collective-permute-start | bytes 245768 | tf_op jit(solution)/shard_map/ppermute | solution.py:435
  104.7 4.6 %copy-start.3 = (s32[1,512]{1,0:T(1,128)S(1)}, s32[1,512]{1,0:T(1,128)}, u32[]{:S(2)}) copy-start(s32[1,512]{1,0:T(1,128)} %place_ref.5) | copy-start | bytes 6148
  104.8 4.5 %collective-permute-start.21 = (bf16[320,128]{1,0:T(8,128)(2,1)S(1)}, bf16[320,128]{1,0:T(8,128)(2,1)S(1)}, u32[]{:S(2)}, u32[]{:S(2)}) collective-permute-start(bf16[320,128]{1,0:T(8,128)(2,1)S(1)} %shard_map.101.refs_0_), channel_id=1, source_target_pairs={{0,2},{1,3},{2,0},{3,1},{4,6},{5,7},{6,4},{7,5},{8,10},{9,11},{10,... | collective-permute-start | bytes 245768 | tf_op jit(solution)/shard_map/ppermute | solution.py:435
  106.4 4.8 %collective-permute-start.20 = (bf16[320,128]{1,0:T(8,128)(2,1)S(1)}, bf16[320,128]{1,0:T(8,128)(2,1)S(1)}, u32[]{:S(2)}, u32[]{:S(2)}) collective-permute-start(bf16[320,128]{1,0:T(8,128)(2,1)S(1)} %shard_map.101.refs_0_), channel_id=1, source_target_pairs={{0,1},{1,0},{2,3},{3,2},{4,5},{5,4},{6,7},{7,6},{8,9},{9,8},{10,11... | collective-permute-start | bytes 245768 | tf_op jit(solution)/shard_map/ppermute | solution.py:435
  109.3 1.8 %collective-permute-start.22 = (bf16[320,128]{1,0:T(8,128)(2,1)S(1)}, bf16[320,128]{1,0:T(8,128)(2,1)S(1)}, u32[]{:S(2)}, u32[]{:S(2)}) collective-permute-start(bf16[320,128]{1,0:T(8,128)(2,1)S(1)} %collective-permute-done.21.refs_2_), channel_id=1, source_target_pairs={{0,1},{1,0},{2,3},{3,2},{4,5},{5,4},{6,7},{7,6},{8,9},{9,8},{10,11... | collective-permute-start | bytes 245768 | tf_op jit(solution)/shard_map/ppermute | solution.py:435

commit v4 on v3

--- a/solution.py
+++ b/solution.py
@@ -448,7 +448,7 @@
         if k < owners // 2:
             got_x[k] = got[k] = swap(blocks[k], "dp", k)
         else:
-            got[k] = swap(ordered(blocks[k], got_x[k]), "dp", k)
+            got[k] = swap(ordered(blocks[k], got_x[k ^ 1]), "dp", k)
     return got_x, got
 
 

time: 112 us -> 112 us (level)
  no operation moved by 1% of the time
where the time goes in v4:
time: 112 us
  starting transfers between devices  45.6 us (41%)
  waiting for transfers between devices  38.4 us (34%)
  Pallas kernels  23.2 us (21%)
  local copies, waits for them, and re-layouts  3.6 us (3%)
    ppermute x23, starting transfers between devices, swap(): return lax.ppermute(value, axis, [(i, i ^ distance) for i in range(size)])  40.9 us
    ppermute x23, waiting for transfers between devices, swap(): return lax.ppermute(value, axis, [(i, i ^ distance) for i in range(size)])  38.4 us
    pallas_call x18, Pallas kernels, call(): pl.pallas_call(kernel, out_shape=out_shape, scratch_shapes=scratch, compi...  23.2 us
    all_to_all x1, starting transfers between devices, on_device(): back = lax.all_to_all(back, 'dp', split_axis=0, concat_axis=0, tiled=True)  4.68 us
    unnamed x14, local copies, waits for them, and re-layouts  3.6 us
  transfers between devices with their start and end apart: 24, of which 12 were waited for; matrix products, arithmetic and copies ran while one was open for 0% of the time, Pallas kernels for 15%

profile of v4, /device:TPU:0, one launch (start us, length us, event | category | flops | bytes accessed | tf_op | source)
XLA Modules:
  0.0 111.6 jit_solution(1943935969398248084)
XLA Ops:
  0.7 0.8 copy-done.2
  1.5 1.0 copy-done.4
  2.5 0.5 shard_map.87
  3.0 5.0 %collective-permute-start.3 = (bf16[128,512]{1,0:T(8,128)(2,1)S(1)}, bf16[128,512]{1,0:T(8,128)(2,1)S(1)}, u32[]{:S(2)}, u32[]{:S(2)}) collective-permute-start(bf16[128,512]{1,0:T(8,128)(2,1)S(1)} %get-tuple-element.65), channel_id=1, source_target_pairs={{0,20},{4,16},{8,28},{12,24},{16,4},{20,0},{24,12},{28,8},{1,21},{... | collective-permute-start | bytes 393224 | tf_op jit(solution)/shard_map/ppermute | solution.py:435
  8.1 1.3 %collective-permute-start.9 = (bf16[128,512]{1,0:T(8,128)(2,1)S(1)}, bf16[128,512]{1,0:T(8,128)(2,1)S(1)}, u32[]{:S(2)}, u32[]{:S(2)}) collective-permute-start(bf16[128,512]{1,0:T(8,128)(2,1)S(1)} %get-tuple-element.74), channel_id=1, source_target_pairs={{0,24},{4,28},{8,16},{12,20},{16,8},{20,12},{24,0},{28,4},{1,25},{... | collective-permute-start | bytes 393224 | tf_op jit(solution)/shard_map/ppermute | solution.py:435
  9.4 1.0 copy-done.5
  10.5 0.9 shard_map.86
  11.4 0.6 collective-permute-start
  12.0 0.2 collective-permute-start.1
  12.2 2.7 %collective-permute-start.2 = (bf16[256,512]{1,0:T(8,128)(2,1)S(1)}, bf16[256,512]{1,0:T(8,128)(2,1)S(1)}, u32[]{:S(2)}, u32[]{:S(2)}) collective-permute-start(bf16[256,512]{1,0:T(8,128)(2,1)S(1)} %get-tuple-element.63), channel_id=1, source_target_pairs={{0,12},{4,8},{8,4},{12,0},{16,28},{20,24},{24,20},{28,16},{1,13},{... | collective-permute-start | bytes 786440 | tf_op jit(solution)/shard_map/ppermute | solution.py:435
  15.0 3.1 %collective-permute-done.3.refs_5_ = bf16[128,512]{1,0:T(8,128)(2,1)S(1)} collective-permute-done((bf16[128,512]{1,0:T(8,128)(2,1)S(1)}, bf16[128,512]{1,0:T(8,128)(2,1)S(1)}, u32[]{:S(2)}, u32[]{:S(2)}) %collective-permute-start.3) | collective-permute-done | bytes 131104 | tf_op jit(solution)/shard_map/ppermute | solution.py:435
  18.1 3.8 %collective-permute-start.7 = (bf16[128,512]{1,0:T(8,128)(2,1)S(1)}, bf16[128,512]{1,0:T(8,128)(2,1)S(1)}, u32[]{:S(2)}, u32[]{:S(2)}) collective-permute-start(bf16[128,512]{1,0:T(8,128)(2,1)S(1)} %get-tuple-element.71), channel_id=1, source_target_pairs={{0,28},{4,24},{8,20},{12,16},{16,12},{20,8},{24,4},{28,0},{1,29},{... | collective-permute-start | bytes 393224 | tf_op jit(solution)/shard_map/ppermute | solution.py:435
  21.8 7.7 %collective-permute-done.5.refs_4_ = bf16[128,512]{1,0:T(8,128)(2,1)S(1)} collective-permute-done((bf16[128,512]{1,0:T(8,128)(2,1)S(1)}, bf16[128,512]{1,0:T(8,128)(2,1)S(1)}, u32[]{:S(2)}, u32[]{:S(2)}) %collective-permute-start.5) | collective-permute-done | bytes 131104 | tf_op jit(solution)/shard_map/ppermute | solution.py:435
  29.6 1.1 %collective-permute-start.10 = (bf16[128,512]{1,0:T(8,128)(2,1)S(1)}, bf16[128,512]{1,0:T(8,128)(2,1)S(1)}, u32[]{:S(2)}, u32[]{:S(2)}) collective-permute-start(bf16[128,512]{1,0:T(8,128)(2,1)S(1)} %get-tuple-element.75), channel_id=1, source_target_pairs={{0,28},{4,24},{8,20},{12,16},{16,12},{20,8},{24,4},{28,0},{1,29},{... | collective-permute-start | bytes 393224 | tf_op jit(solution)/shard_map/ppermute | solution.py:435
  30.7 2.0 %collective-permute-done.7.refs_7_ = bf16[128,512]{1,0:T(8,128)(2,1)S(1)} collective-permute-done((bf16[128,512]{1,0:T(8,128)(2,1)S(1)}, bf16[128,512]{1,0:T(8,128)(2,1)S(1)}, u32[]{:S(2)}, u32[]{:S(2)}) %collective-permute-start.7) | collective-permute-done | bytes 131104 | tf_op jit(solution)/shard_map/ppermute | solution.py:435
  32.7 9.4 %collective-permute-start.4 = (bf16[128,512]{1,0:T(8,128)(2,1)S(1)}, bf16[128,512]{1,0:T(8,128)(2,1)S(1)}, u32[]{:S(2)}, u32[]{:S(2)}) collective-permute-start(bf16[128,512]{1,0:T(8,128)(2,1)S(1)} %get-tuple-element.66), channel_id=1, source_target_pairs={{0,16},{4,20},{8,24},{12,28},{16,0},{20,4},{24,8},{28,12},{1,17},{... | collective-permute-start | bytes 393224 | tf_op jit(solution)/shard_map/ppermute | solution.py:435
  42.2 1.0 collective-permute-start.8
  43.2 0.7 copy-done.6
  43.9 7.5 %shard_map.88 = (bf16[512,1024]{1,0:T(8,128)(2,1)S(1)}, bf16[1024,512]{1,0:T(8,128)(2,1)S(1)}, bf16[512,2048]{1,0:T(8,128)(2,1)S(1)}, bf16[512,2048]{1,0:T(8,128...) custom-call(bf16[128,512]{1,0:T(8,128)(2,1)S(1)} %get-tuple-element., ...), custom_call_target="tpu_custom_call" | custom-call | flops 2147483648 | bytes 21366784 | tf_op jit(solution)/shard_map/pallas_call | solution.py:37
  51.4 0.3 collective-permute-done.4.refs_4_
  51.7 2.5 %collective-permute-done.6.refs_5_ = bf16[128,512]{1,0:T(8,128)(2,1)S(1)} collective-permute-done((bf16[128,512]{1,0:T(8,128)(2,1)S(1)}, bf16[128,512]{1,0:T(8,128)(2,1)S(1)}, u32[]{:S(2)}, u32[]{:S(2)}) %collective-permute-start.6) | collective-permute-done | bytes 131104 | tf_op jit(solution)/shard_map/ppermute | solution.py:435
  54.2 1.5 %shard_map.89 = (bf16[512,512]{1,0:T(8,128)(2,1)S(1)}, bf16[512,512]{1,0:T(8,128)(2,1)S(1)}, bf16[512,512]{1,0:T(8,128)(2,1)S(1)}, bf16[512,512]{1,0:T(8,128)(2,1)S(1)}) custom-call(bf16[128,512]{1,0:T(8,128)(2,1)S(1)} %get-tuple-element.60.refs_0_, bf16[256,512]{1,0:T(8,128)(2,1)S(1)} %collective-permute-done.refs_1_, ...), custom_call_target="tpu_custom_call" | custom-call | flops 805306368 | bytes 10092544 | tf_op jit(solution)/shard_map/pallas_call | solution.py:37
  55.8 1.3 %shard_map.90 = (bf16[2,1024,128]{2,1,0:T(8,128)(2,1)S(1)}, bf16[2,1024,128]{2,1,0:T(8,128)(2,1)S(1)}) custom-call(bf16[512,512]{1,0:T(8,128)(2,1)S(1)} %get-tuple-element.87.xhat_t_ref, bf16[512,512]{1,0:T(8,128)(2,1)S(1)} %get-tuple-element.82.dpre_ref.dpre_u_ref, bf16[512,512]{1,0:T(8,128)(2,1)S(1)} %get-tuple-element.88.gated_t_ref, ...), custom_call_target="tpu_custom_call" | custom-call | flops 536870912 | bytes 3145728 | tf_op jit(solution)/shard_map/pallas_call | solution.py:37
  57.2 3.3 %shard_map.91.dpre_ref = bf16[512,2048]{1,0:T(8,128)(2,1)S(1)} custom-call(bf16[512,512]{1,0:T(8,128)(2,1)S(1)} %get-tuple-element.82.dpre_ref.dpre_u_ref, bf16[512,2048]{1,0:T(8,128)(2,1)S(1)} %get-tuple-element.80.refs_12_.refs_0_, bf16[512,2048]{1,0:T(8,128)(2,1)S(1)} %get-tuple-element.81.refs_13_.refs_1_, ...), custom_call_target="tpu_custom_call" | custom-call | flops 1073741824 | bytes 16777216 | tf_op jit(solution)/shard_map/pallas_call | solution.py:37
  60.6 1.2 %shard_map.93 = (bf16[2,1536,128]{2,1,0:T(8,128)(2,1)S(1)}, bf16[2,1536,128]{2,1,0:T(8,128)(2,1)S(1)}) custom-call(bf16[512,512]{1,0:T(8,128)(2,1)S(1)} %get-tuple-element.87.xhat_t_ref, bf16[512,2048]{1,0:T(8,128)(2,1)S(1)} %shard_map.91.dpre_ref), custom_call_target="tpu_custom_call" | custom-call | flops 1073741824 | bytes 4194304 | tf_op jit(solution)/shard_map/pallas_call | solution.py:37
  61.8 0.5 collective-permute-start.12
  62.4 1.6 %shard_map.94.dx_ref = bf16[512,512]{1,0:T(8,128)(2,1)S(1)} custom-call(bf16[512,2048]{1,0:T(8,128)(2,1)S(1)} %shard_map.91.dpre_ref, bf16[512,2048]{1,0:T(8,128)(2,1)S(1)} %copy-done, bf16[512,512]{1,0:T(8,128)(2,1)S(1)} %get-tuple-element.98.xhat_ref, f32[512,128]{1,0:T(8,128)S(1)} %get-tuple-element.99.x_rstd_ref, ...), custom_call_target="tpu_custom_call" | custom-call | flops 1073741824 | bytes 6029312 | tf_op jit(solution)/shard_map/pallas_call | solution.py:37
  63.9 0.3 collective-permute-done.12.got_ref
  64.3 0.3 shard_map.95
  64.6 1.1 collective-permute-start.15
  65.6 1.7 %shard_map.96 = bf16[1024,512]{1,0:T(8,128)(2,1)} custom-call(bf16[512,512]{1,0:T(8,128)(2,1)S(1)} %shard_map.94.dx_ref, bf16[1024,512]{1,0:T(8,128)(2,1)S(1)} %get-tuple-element.103.unplace_ref), custom_call_target="tpu_custom_call" | custom-call | flops 536870912 | bytes 2621440 | tf_op jit(solution)/shard_map/pallas_call | solution.py:37
  67.3 4.7 %all-to-all-start = ((bf16[8,128,512]{2,1,0:T(8,128)(2,1)}), bf16[8,128,512]{2,1,0:T(8,128)(2,1)S(1)}, u32[]{:S(2)}, u32[]{:S(2)}) async-start(bf16[8,128,512]{2,1,0:T(8,128)(2,1)} %bitcast), calls=%async_computation | async-start | bytes 2097152 | tf_op jit(solution)/shard_map/all_to_all | solution.py:538
  72.0 1.5 %collective-permute-start.13 = (bf16[1024,128]{1,0:T(8,128)(2,1)S(1)}, bf16[1024,128]{1,0:T(8,128)(2,1)S(1)}, u32[]{:S(2)}, u32[]{:S(2)}) collective-permute-start(bf16[1024,128]{1,0:T(8,128)(2,1)S(1)} %get-tuple-element.94), channel_id=1, source_target_pairs={{0,2},{1,3},{2,0},{3,1},{4,6},{5,7},{6,4},{7,5},{8,10},{9,11},{10,... | collective-permute-start | bytes 786440 | tf_op jit(solution)/shard_map/ppermute | solution.py:435
  73.5 4.5 %collective-permute-done.15.got_ref = bf16[2,768,128]{2,1,0:T(8,128)(2,1)S(1)} collective-permute-done((bf16[2,768,128]{2,1,0:T(8,128)(2,1)S(1)}, bf16[2,768,128]{2,1,0:T(8,128)(2,1)S(1)}, u32[]{:S(2)}, u32[]{:S(2)}) %collective-permute-start.15) | collective-permute-done | bytes 393248 | tf_op jit(solution)/shard_map/ppermute | solution.py:435
  78.2 1.1 collective-permute-start.16
  79.2 2.0 %collective-permute-done.13.second_ref = bf16[1024,128]{1,0:T(8,128)(2,1)S(1)} collective-permute-done((bf16[1024,128]{1,0:T(8,128)(2,1)S(1)}, bf16[1024,128]{1,0:T(8,128)(2,1)S(1)}, u32[]{:S(2)}, u32[]{:S(2)}) %collective-permute-start.13) | collective-permute-done | bytes 262176 | tf_op jit(solution)/shard_map/ppermute | solution.py:435
  81.3 1.4 %collective-permute-start.14 = (bf16[512,128]{1,0:T(8,128)(2,1)S(1)}, bf16[512,128]{1,0:T(8,128)(2,1)S(1)}, u32[]{:S(2)}, u32[]{:S(2)}) collective-permute-start(bf16[512,128]{1,0:T(8,128)(2,1)S(1)} %get-tuple-element.106), channel_id=1, source_target_pairs={{0,4},{4,0},{8,12},{12,8},{16,20},{20,16},{24,28},{28,24},{1,5},{5... | collective-permute-start | bytes 393224 | tf_op jit(solution)/shard_map/ppermute | solution.py:435
  82.8 4.5 %collective-permute-done.14.refs_1_ = bf16[512,128]{1,0:T(8,128)(2,1)S(1)} collective-permute-done((bf16[512,128]{1,0:T(8,128)(2,1)S(1)}, bf16[512,128]{1,0:T(8,128)(2,1)S(1)}, u32[]{:S(2)}, u32[]{:S(2)}) %collective-permute-start.14) | collective-permute-done | bytes 131104 | tf_op jit(solution)/shard_map/ppermute | solution.py:435
  87.4 5.9 %collective-permute-start.17 = (bf16[320,128]{1,0:T(8,128)(2,1)S(1)}, bf16[320,128]{1,0:T(8,128)(2,1)S(1)}, u32[]{:S(2)}, u32[]{:S(2)}) collective-permute-start(bf16[320,128]{1,0:T(8,128)(2,1)S(1)} %get-tuple-element.111), channel_id=1, source_target_pairs={{0,8},{4,12},{8,0},{12,4},{16,24},{20,28},{24,16},{28,20},{1,9},{5... | collective-permute-start | bytes 245768 | tf_op jit(solution)/shard_map/ppermute | solution.py:435
  93.3 1.7 %collective-permute-start.18 = (bf16[320,128]{1,0:T(8,128)(2,1)S(1)}, bf16[320,128]{1,0:T(8,128)(2,1)S(1)}, u32[]{:S(2)}, u32[]{:S(2)}) collective-permute-start(bf16[320,128]{1,0:T(8,128)(2,1)S(1)} %get-tuple-element.112), channel_id=1, source_target_pairs={{0,16},{4,20},{8,24},{12,28},{16,0},{20,4},{24,8},{28,12},{1,17},{... | collective-permute-start | bytes 245768 | tf_op jit(solution)/shard_map/ppermute | solution.py:435
  95.0 0.7 collective-permute-start.19
  95.7 2.8 %collective-permute-done.17.refs_1_ = bf16[320,128]{1,0:T(8,128)(2,1)S(1)} collective-permute-done((bf16[320,128]{1,0:T(8,128)(2,1)S(1)}, bf16[320,128]{1,0:T(8,128)(2,1)S(1)}, u32[]{:S(2)}, u32[]{:S(2)}) %collective-permute-start.17) | collective-permute-done | bytes 81952 | tf_op jit(solution)/shard_map/ppermute | solution.py:435
  98.5 5.7 %collective-permute-done.18.refs_2_ = bf16[320,128]{1,0:T(8,128)(2,1)S(1)} collective-permute-done((bf16[320,128]{1,0:T(8,128)(2,1)S(1)}, bf16[320,128]{1,0:T(8,128)(2,1)S(1)}, u32[]{:S(2)}, u32[]{:S(2)}) %collective-permute-start.18) | collective-permute-done | bytes 81952 | tf_op jit(solution)/shard_map/ppermute | solution.py:435
  104.3 1.6 %collective-permute-start.21 = (bf16[320,128]{1,0:T(8,128)(2,1)S(1)}, bf16[320,128]{1,0:T(8,128)(2,1)S(1)}, u32[]{:S(2)}, u32[]{:S(2)}) collective-permute-start(bf16[320,128]{1,0:T(8,128)(2,1)S(1)} %shard_map.101.refs_0_), channel_id=1, source_target_pairs={{0,2},{1,3},{2,0},{3,1},{4,6},{5,7},{6,4},{7,5},{8,10},{9,11},{10,... | collective-permute-start | bytes 245768 | tf_op jit(solution)/shard_map/ppermute | solution.py:435
  105.9 2.9 %collective-permute-done.21.refs_2_ = bf16[320,128]{1,0:T(8,128)(2,1)S(1)} collective-permute-done((bf16[320,128]{1,0:T(8,128)(2,1)S(1)}, bf16[320,128]{1,0:T(8,128)(2,1)S(1)}, u32[]{:S(2)}, u32[]{:S(2)}) %collective-permute-start.21) | collective-permute-done | bytes 81952 | tf_op jit(solution)/shard_map/ppermute | solution.py:435
  108.8 0.3 shard_map.85.lookup_ref
  109.1 1.5 %shard_map.97 = bf16[512,512]{1,0:T(8,128)(2,1)} custom-call(bf16[512,1024]{1,0:T(8,128)(2,1)S(1)} %shard_map.85.lookup_ref, bf16[1024,512]{1,0:T(8,128)(2,1)S(1)} %bitcast.3), custom_call_target="tpu_custom_call" | custom-call | flops 536870912 | bytes 2621440 | tf_op jit(solution)/shard_map/pallas_call | solution.py:37
  110.6 1.0 shard_map.102
  (32 shorter events, 0.7 us)
Async XLA Ops:
  0.6 42.6 %copy-start = (bf16[512,2048]{1,0:T(8,128)(2,1)S(1)}, bf16[512,2048]{1,0:T(8,128)(2,1)}, u32[]{:S(2)}) copy-start(bf16[512,2048]{1,0:T(8,128)(2,1)} %w_ref.1) | copy-start | bytes 6291460
  0.6 0.8 copy-start.2
  1.5 1.0 copy-start.4
  3.0 15.0 %collective-permute-start.3 = (bf16[128,512]{1,0:T(8,128)(2,1)S(1)}, bf16[128,512]{1,0:T(8,128)(2,1)S(1)}, u32[]{:S(2)}, u32[]{:S(2)}) collective-permute-start(bf16[128,512]{1,0:T(8,128)(2,1)S(1)} %get-tuple-element.65), channel_id=1, source_target_pairs={{0,20},{4,16},{8,28},{12,24},{16,4},{20,0},{24,12},{28,8},{1,21},{... | collective-permute-start | bytes 393224 | tf_op jit(solution)/shard_map/ppermute | solution.py:435
  8.1 10.0 %collective-permute-start.9 = (bf16[128,512]{1,0:T(8,128)(2,1)S(1)}, bf16[128,512]{1,0:T(8,128)(2,1)S(1)}, u32[]{:S(2)}, u32[]{:S(2)}) collective-permute-start(bf16[128,512]{1,0:T(8,128)(2,1)S(1)} %get-tuple-element.74), channel_id=1, source_target_pairs={{0,24},{4,28},{8,16},{12,20},{16,8},{20,12},{24,0},{28,4},{1,25},{... | collective-permute-start | bytes 393224 | tf_op jit(solution)/shard_map/ppermute | solution.py:435
  9.4 1.0 copy-start.5
  11.4 30.8 %collective-permute-start = (bf16[256,512]{1,0:T(8,128)(2,1)S(1)}, bf16[256,512]{1,0:T(8,128)(2,1)S(1)}, u32[]{:S(2)}, u32[]{:S(2)}) collective-permute-start(bf16[256,512]{1,0:T(8,128)(2,1)S(1)} %get-tuple-element.61), channel_id=1, source_target_pairs={{0,4},{4,0},{8,12},{12,8},{16,20},{20,16},{24,28},{28,24},{1,5},{5... | collective-permute-start | bytes 786440 | tf_op jit(solution)/shard_map/ppermute | solution.py:435
  12.0 30.2 %collective-permute-start.1 = (bf16[256,512]{1,0:T(8,128)(2,1)S(1)}, bf16[256,512]{1,0:T(8,128)(2,1)S(1)}, u32[]{:S(2)}, u32[]{:S(2)}) collective-permute-start(bf16[256,512]{1,0:T(8,128)(2,1)S(1)} %get-tuple-element.62), channel_id=1, source_target_pairs={{0,8},{4,12},{8,0},{12,4},{16,24},{20,28},{24,16},{28,20},{1,9},{5... | collective-permute-start | bytes 786440 | tf_op jit(solution)/shard_map/ppermute | solution.py:435
  12.2 30.9 %collective-permute-start.2 = (bf16[256,512]{1,0:T(8,128)(2,1)S(1)}, bf16[256,512]{1,0:T(8,128)(2,1)S(1)}, u32[]{:S(2)}, u32[]{:S(2)}) collective-permute-start(bf16[256,512]{1,0:T(8,128)(2,1)S(1)} %get-tuple-element.63), channel_id=1, source_target_pairs={{0,12},{4,8},{8,4},{12,0},{16,28},{20,24},{24,20},{28,16},{1,13},{... | collective-permute-start | bytes 786440 | tf_op jit(solution)/shard_map/ppermute | solution.py:435
  18.1 11.5 %collective-permute-start.5 = (bf16[128,512]{1,0:T(8,128)(2,1)S(1)}, bf16[128,512]{1,0:T(8,128)(2,1)S(1)}, u32[]{:S(2)}, u32[]{:S(2)}) collective-permute-start(bf16[128,512]{1,0:T(8,128)(2,1)S(1)} %get-tuple-element.68), channel_id=1, source_target_pairs={{0,16},{4,20},{8,24},{12,28},{16,0},{20,4},{24,8},{28,12},{1,17},{... | collective-permute-start | bytes 393224 | tf_op jit(solution)/shard_map/ppermute | solution.py:435
  18.1 14.6 %collective-permute-start.7 = (bf16[128,512]{1,0:T(8,128)(2,1)S(1)}, bf16[128,512]{1,0:T(8,128)(2,1)S(1)}, u32[]{:S(2)}, u32[]{:S(2)}) collective-permute-start(bf16[128,512]{1,0:T(8,128)(2,1)S(1)} %get-tuple-element.71), channel_id=1, source_target_pairs={{0,28},{4,24},{8,20},{12,16},{16,12},{20,8},{24,4},{28,0},{1,29},{... | collective-permute-start | bytes 393224 | tf_op jit(solution)/shard_map/ppermute | solution.py:435
  29.6 21.8 %collective-permute-start.10 = (bf16[128,512]{1,0:T(8,128)(2,1)S(1)}, bf16[128,512]{1,0:T(8,128)(2,1)S(1)}, u32[]{:S(2)}, u32[]{:S(2)}) collective-permute-start(bf16[128,512]{1,0:T(8,128)(2,1)S(1)} %get-tuple-element.75), channel_id=1, source_target_pairs={{0,28},{4,24},{8,20},{12,16},{16,12},{20,8},{24,4},{28,0},{1,29},{... | collective-permute-start | bytes 393224 | tf_op jit(solution)/shard_map/ppermute | solution.py:435
  32.7 19.0 %collective-permute-start.4 = (bf16[128,512]{1,0:T(8,128)(2,1)S(1)}, bf16[128,512]{1,0:T(8,128)(2,1)S(1)}, u32[]{:S(2)}, u32[]{:S(2)}) collective-permute-start(bf16[128,512]{1,0:T(8,128)(2,1)S(1)} %get-tuple-element.66), channel_id=1, source_target_pairs={{0,16},{4,20},{8,24},{12,28},{16,0},{20,4},{24,8},{28,12},{1,17},{... | collective-permute-start | bytes 393224 | tf_op jit(solution)/shard_map/ppermute | solution.py:435
  42.2 12.1 %collective-permute-start.6 = (bf16[128,512]{1,0:T(8,128)(2,1)S(1)}, bf16[128,512]{1,0:T(8,128)(2,1)S(1)}, u32[]{:S(2)}, u32[]{:S(2)}) collective-permute-start(bf16[128,512]{1,0:T(8,128)(2,1)S(1)} %get-tuple-element.69), channel_id=1, source_target_pairs={{0,20},{4,16},{8,28},{12,24},{16,4},{20,0},{24,12},{28,8},{1,21},{... | collective-permute-start | bytes 393224 | tf_op jit(solution)/shard_map/ppermute | solution.py:435
  42.2 12.1 %collective-permute-start.8 = (bf16[128,512]{1,0:T(8,128)(2,1)S(1)}, bf16[128,512]{1,0:T(8,128)(2,1)S(1)}, u32[]{:S(2)}, u32[]{:S(2)}) collective-permute-start(bf16[128,512]{1,0:T(8,128)(2,1)S(1)} %get-tuple-element.72), channel_id=1, source_target_pairs={{0,24},{4,28},{8,16},{12,20},{16,8},{20,12},{24,0},{28,4},{1,25},{... | collective-permute-start | bytes 393224 | tf_op jit(solution)/shard_map/ppermute | solution.py:435
  43.2 0.7 copy-start.6
  43.9 10.4 %copy-start.1 = (bf16[512,512]{1,0:T(8,128)(2,1)S(1)}, bf16[512,512]{1,0:T(8,128)(2,1)}, u32[]{:S(2)}) copy-start(bf16[512,512]{1,0:T(8,128)(2,1)} %refs_11_.1) | copy-start | bytes 1572868
  57.1 3.4 %collective-permute-start.11 = (bf16[2,1024,128]{2,1,0:T(8,128)(2,1)S(1)}, bf16[2,1024,128]{2,1,0:T(8,128)(2,1)S(1)}, u32[]{:S(2)}, u32[]{:S(2)}) collective-permute-start(bf16[2,1024,128]{2,1,0:T(8,128)(2,1)S(1)} %get-tuple-element.90), channel_id=1, source_target_pairs={{0,1},{1,0},{2,3},{3,2},{4,5},{5,4},{6,7},{7,6},{8,9},{9,8},{10,11... | collective-permute-start | bytes 1572872 | tf_op jit(solution)/shard_map/ppermute | solution.py:435
  61.8 2.5 %collective-permute-start.12 = (bf16[2,1536,128]{2,1,0:T(8,128)(2,1)S(1)}, bf16[2,1536,128]{2,1,0:T(8,128)(2,1)S(1)}, u32[]{:S(2)}, u32[]{:S(2)}) collective-permute-start(bf16[2,1536,128]{2,1,0:T(8,128)(2,1)S(1)} %get-tuple-element.96), channel_id=1, source_target_pairs={{0,1},{1,0},{2,3},{3,2},{4,5},{5,4},{6,7},{7,6},{8,9},{9,8},{10,11... | collective-permute-start | bytes 2359304 | tf_op jit(solution)/shard_map/ppermute | solution.py:435
  64.6 13.5 %collective-permute-start.15 = (bf16[2,768,128]{2,1,0:T(8,128)(2,1)S(1)}, bf16[2,768,128]{2,1,0:T(8,128)(2,1)S(1)}, u32[]{:S(2)}, u32[]{:S(2)}) collective-permute-start(bf16[2,768,128]{2,1,0:T(8,128)(2,1)S(1)} %get-tuple-element.101), channel_id=1, source_target_pairs={{0,4},{4,0},{8,12},{12,8},{16,20},{20,16},{24,28},{28,24},{1,5},{5... | collective-permute-start | bytes 1179656 | tf_op jit(solution)/shard_map/ppermute | solution.py:435
  67.3 41.8 %all-to-all-start = ((bf16[8,128,512]{2,1,0:T(8,128)(2,1)}), bf16[8,128,512]{2,1,0:T(8,128)(2,1)S(1)}, u32[]{:S(2)}, u32[]{:S(2)}) async-start(bf16[8,128,512]{2,1,0:T(8,128)(2,1)} %bitcast), calls=%async_computation | async-start | bytes 2097152 | tf_op jit(solution)/shard_map/all_to_all | solution.py:538
  72.0 9.2 %collective-permute-start.13 = (bf16[1024,128]{1,0:T(8,128)(2,1)S(1)}, bf16[1024,128]{1,0:T(8,128)(2,1)S(1)}, u32[]{:S(2)}, u32[]{:S(2)}) collective-permute-start(bf16[1024,128]{1,0:T(8,128)(2,1)S(1)} %get-tuple-element.94), channel_id=1, source_target_pairs={{0,2},{1,3},{2,0},{3,1},{4,6},{5,7},{6,4},{7,5},{8,10},{9,11},{10,... | collective-permute-start | bytes 786440 | tf_op jit(solution)/shard_map/ppermute | solution.py:435
  78.2 9.1 %collective-permute-start.16 = (bf16[768,128]{1,0:T(8,128)(2,1)S(1)}, bf16[768,128]{1,0:T(8,128)(2,1)S(1)}, u32[]{:S(2)}, u32[]{:S(2)}) collective-permute-start(bf16[768,128]{1,0:T(8,128)(2,1)S(1)} %get-tuple-element.109), channel_id=1, source_target_pairs={{0,2},{1,3},{2,0},{3,1},{4,6},{5,7},{6,4},{7,5},{8,10},{9,11},{10,... | collective-permute-start | bytes 589832 | tf_op jit(solution)/shard_map/ppermute | solution.py:435
  81.3 5.9 %collective-permute-start.14 = (bf16[512,128]{1,0:T(8,128)(2,1)S(1)}, bf16[512,128]{1,0:T(8,128)(2,1)S(1)}, u32[]{:S(2)}, u32[]{:S(2)}) collective-permute-start(bf16[512,128]{1,0:T(8,128)(2,1)S(1)} %get-tuple-element.106), channel_id=1, source_target_pairs={{0,4},{4,0},{8,12},{12,8},{16,20},{20,16},{24,28},{28,24},{1,5},{5... | collective-permute-start | bytes 393224 | tf_op jit(solution)/shard_map/ppermute | solution.py:435
  87.4 11.1 %collective-permute-start.17 = (bf16[320,128]{1,0:T(8,128)(2,1)S(1)}, bf16[320,128]{1,0:T(8,128)(2,1)S(1)}, u32[]{:S(2)}, u32[]{:S(2)}) collective-permute-start(bf16[320,128]{1,0:T(8,128)(2,1)S(1)} %get-tuple-element.111), channel_id=1, source_target_pairs={{0,8},{4,12},{8,0},{12,4},{16,24},{20,28},{24,16},{28,20},{1,9},{5... | collective-permute-start | bytes 245768 | tf_op jit(solution)/shard_map/ppermute | solution.py:435
  93.3 10.9 %collective-permute-start.18 = (bf16[320,128]{1,0:T(8,128)(2,1)S(1)}, bf16[320,128]{1,0:T(8,128)(2,1)S(1)}, u32[]{:S(2)}, u32[]{:S(2)}) collective-permute-start(bf16[320,128]{1,0:T(8,128)(2,1)S(1)} %get-tuple-element.112), channel_id=1, source_target_pairs={{0,16},{4,20},{8,24},{12,28},{16,0},{20,4},{24,8},{28,12},{1,17},{... | collective-permute-start | bytes 245768 | tf_op jit(solution)/shard_map/ppermute | solution.py:435
  95.0 9.2 %collective-permute-start.19 = (bf16[320,128]{1,0:T(8,128)(2,1)S(1)}, bf16[320,128]{1,0:T(8,128)(2,1)S(1)}, u32[]{:S(2)}, u32[]{:S(2)}) collective-permute-start(bf16[320,128]{1,0:T(8,128)(2,1)S(1)} %get-tuple-element.113), channel_id=1, source_target_pairs={{0,24},{4,28},{8,16},{12,20},{16,8},{20,12},{24,0},{28,4},{1,25},{... | collective-permute-start | bytes 245768 | tf_op jit(solution)/shard_map/ppermute | solution.py:435
  104.2 4.6 %copy-start.3 = (s32[1,512]{1,0:T(1,128)S(1)}, s32[1,512]{1,0:T(1,128)}, u32[]{:S(2)}) copy-start(s32[1,512]{1,0:T(1,128)} %place_ref.5) | copy-start | bytes 6148
  104.3 4.5 %collective-permute-start.21 = (bf16[320,128]{1,0:T(8,128)(2,1)S(1)}, bf16[320,128]{1,0:T(8,128)(2,1)S(1)}, u32[]{:S(2)}, u32[]{:S(2)}) collective-permute-start(bf16[320,128]{1,0:T(8,128)(2,1)S(1)} %shard_map.101.refs_0_), channel_id=1, source_target_pairs={{0,2},{1,3},{2,0},{3,1},{4,6},{5,7},{6,4},{7,5},{8,10},{9,11},{10,... | collective-permute-start | bytes 245768 | tf_op jit(solution)/shard_map/ppermute | solution.py:435
  105.9 4.8 %collective-permute-start.20 = (bf16[320,128]{1,0:T(8,128)(2,1)S(1)}, bf16[320,128]{1,0:T(8,128)(2,1)S(1)}, u32[]{:S(2)}, u32[]{:S(2)}) collective-permute-start(bf16[320,128]{1,0:T(8,128)(2,1)S(1)} %shard_map.101.refs_0_), channel_id=1, source_target_pairs={{0,1},{1,0},{2,3},{3,2},{4,5},{5,4},{6,7},{7,6},{8,9},{9,8},{10,11... | collective-permute-start | bytes 245768 | tf_op jit(solution)/shard_map/ppermute | solution.py:435
  108.8 1.8 %collective-permute-start.22 = (bf16[320,128]{1,0:T(8,128)(2,1)S(1)}, bf16[320,128]{1,0:T(8,128)(2,1)S(1)}, u32[]{:S(2)}, u32[]{:S(2)}) collective-permute-start(bf16[320,128]{1,0:T(8,128)(2,1)S(1)} %collective-permute-done.21.refs_2_), channel_id=1, source_target_pairs={{0,1},{1,0},{2,3},{3,2},{4,5},{5,4},{6,7},{7,6},{8,9},{9,8},{10,11... | collective-permute-start | bytes 245768 | tf_op jit(solution)/shard_map/ppermute | solution.py:435

commit v5 on v4

--- a/solution.py
+++ b/solution.py
@@ -250,8 +250,8 @@
         for inner in range(heads):
             for j in range(steps):
                 at = slice(j * QUERIES, (j + 1) * QUERIES)
-                dkv_t_ref[0, inner * half : (inner + 1) * half, at] = dv_t[inner][j]
-                dkv_t_ref[1, inner * half : (inner + 1) * half, at] = dk_t[inner][j]
+                dkv_t_ref[0, inner * half : (inner + 1) * half, at] = dv_t[inner][j].astype(BF16)
+                dkv_t_ref[1, inner * half : (inner + 1) * half, at] = dk_t[inner][j].astype(BF16)
         for part, grad in (
             (1, dkv_t_ref[0].T),
             (2, jnp.concatenate(dq, axis=0)),
@@ -259,7 +259,7 @@
         ):
             columns = slice(part * width + lanes.start, part * width + lanes.stop)
             slope = slope_ref[:, columns].astype(F32)
-            dpre_ref[:, columns] = (grad * slope).astype(BF16)
+            dpre_ref[:, columns] = (grad.astype(F32) * slope).astype(BF16)
 
 
 def cotangent_kernel(owners, capacity, *refs):
@@ -282,7 +282,7 @@
         - nhat * jnp.mean(dnhat * nhat, axis=1, keepdims=True)
     )
     datt_ref[...] = datt.astype(BF16)
-    datt_t_ref[...] = datt.T.astype(BF16)
+    datt_t_ref[...] = datt.astype(BF16).T
 
 
 def attention_kernel(dpre_u_ref, *refs):
@@ -512,7 +512,7 @@
     dpre = call(
         attention_kernel, wide,
         dpre_u, act, slope, weights, tangent, q_t, ordered(datt, early_sent), datt_t,
-        flops=4 * attend, scratch=[pltpu.VMEM((2, LANES, count), F32)], vmem=28,
+        flops=4 * attend, scratch=[pltpu.VMEM((2, LANES, count), BF16)], vmem=28,
     )
     early_kept, early_sent = call(
         core_sum_kernel, [shape((early, LANES))] * 2, early_kept, swap(early_sent, "rep", 1)

time: 112 us -> 112 us (level)
  no operation moved by 1% of the time
where the time goes in v5:
time: 112 us
  starting transfers between devices  45.5 us (41%)
  waiting for transfers between devices  38.5 us (34%)
  Pallas kernels  23.2 us (21%)
  local copies, waits for them, and re-layouts  3.6 us (3%)
    ppermute x23, starting transfers between devices, swap(): return lax.ppermute(value, axis, [(i, i ^ distance) for i in range(size)])  40.8 us
    ppermute x23, waiting for transfers between devices, swap(): return lax.ppermute(value, axis, [(i, i ^ distance) for i in range(size)])  38.5 us
    pallas_call x18, Pallas kernels, call(): pl.pallas_call(kernel, out_shape=out_shape, scratch_shapes=scratch, compi...  23.2 us
    all_to_all x1, starting transfers between devices, on_device(): back = lax.all_to_all(back, 'dp', split_axis=0, concat_axis=0, tiled=True)  4.68 us
    unnamed x14, local copies, waits for them, and re-layouts  3.6 us
  transfers between devices with their start and end apart: 24, of which 12 were waited for; matrix products, arithmetic and copies ran while one was open for 0% of the time, Pallas kernels for 15%

profile of v5, /device:TPU:0, one launch (start us, length us, event | category | flops | bytes accessed | tf_op | source)
XLA Modules:
  0.0 111.6 jit_solution(9284187585678743518)
XLA Ops:
  0.7 0.8 copy-done.2
  1.5 1.0 copy-done.4
  2.5 0.5 shard_map.87
  3.0 5.0 %collective-permute-start.3 = (bf16[128,512]{1,0:T(8,128)(2,1)S(1)}, bf16[128,512]{1,0:T(8,128)(2,1)S(1)}, u32[]{:S(2)}, u32[]{:S(2)}) collective-permute-start(bf16[128,512]{1,0:T(8,128)(2,1)S(1)} %get-tuple-element.65), channel_id=1, source_target_pairs={{0,20},{4,16},{8,28},{12,24},{16,4},{20,0},{24,12},{28,8},{1,21},{... | collective-permute-start | bytes 393224 | tf_op jit(solution)/shard_map/ppermute | solution.py:435
  8.1 1.3 %collective-permute-start.9 = (bf16[128,512]{1,0:T(8,128)(2,1)S(1)}, bf16[128,512]{1,0:T(8,128)(2,1)S(1)}, u32[]{:S(2)}, u32[]{:S(2)}) collective-permute-start(bf16[128,512]{1,0:T(8,128)(2,1)S(1)} %get-tuple-element.74), channel_id=1, source_target_pairs={{0,24},{4,28},{8,16},{12,20},{16,8},{20,12},{24,0},{28,4},{1,25},{... | collective-permute-start | bytes 393224 | tf_op jit(solution)/shard_map/ppermute | solution.py:435
  9.4 1.0 copy-done.5
  10.5 0.9 shard_map.86
  11.4 0.6 collective-permute-start
  12.0 0.2 collective-permute-start.1
  12.2 2.7 %collective-permute-start.2 = (bf16[256,512]{1,0:T(8,128)(2,1)S(1)}, bf16[256,512]{1,0:T(8,128)(2,1)S(1)}, u32[]{:S(2)}, u32[]{:S(2)}) collective-permute-start(bf16[256,512]{1,0:T(8,128)(2,1)S(1)} %get-tuple-element.63), channel_id=1, source_target_pairs={{0,12},{4,8},{8,4},{12,0},{16,28},{20,24},{24,20},{28,16},{1,13},{... | collective-permute-start | bytes 786440 | tf_op jit(solution)/shard_map/ppermute | solution.py:435
  15.0 3.1 %collective-permute-done.3.refs_5_ = bf16[128,512]{1,0:T(8,128)(2,1)S(1)} collective-permute-done((bf16[128,512]{1,0:T(8,128)(2,1)S(1)}, bf16[128,512]{1,0:T(8,128)(2,1)S(1)}, u32[]{:S(2)}, u32[]{:S(2)}) %collective-permute-start.3) | collective-permute-done | bytes 131104 | tf_op jit(solution)/shard_map/ppermute | solution.py:435
  18.1 3.8 %collective-permute-start.7 = (bf16[128,512]{1,0:T(8,128)(2,1)S(1)}, bf16[128,512]{1,0:T(8,128)(2,1)S(1)}, u32[]{:S(2)}, u32[]{:S(2)}) collective-permute-start(bf16[128,512]{1,0:T(8,128)(2,1)S(1)} %get-tuple-element.71), channel_id=1, source_target_pairs={{0,28},{4,24},{8,20},{12,16},{16,12},{20,8},{24,4},{28,0},{1,29},{... | collective-permute-start | bytes 393224 | tf_op jit(solution)/shard_map/ppermute | solution.py:435
  21.8 7.7 %collective-permute-done.5.refs_4_ = bf16[128,512]{1,0:T(8,128)(2,1)S(1)} collective-permute-done((bf16[128,512]{1,0:T(8,128)(2,1)S(1)}, bf16[128,512]{1,0:T(8,128)(2,1)S(1)}, u32[]{:S(2)}, u32[]{:S(2)}) %collective-permute-start.5) | collective-permute-done | bytes 131104 | tf_op jit(solution)/shard_map/ppermute | solution.py:435
  29.6 1.1 %collective-permute-start.10 = (bf16[128,512]{1,0:T(8,128)(2,1)S(1)}, bf16[128,512]{1,0:T(8,128)(2,1)S(1)}, u32[]{:S(2)}, u32[]{:S(2)}) collective-permute-start(bf16[128,512]{1,0:T(8,128)(2,1)S(1)} %get-tuple-element.75), channel_id=1, source_target_pairs={{0,28},{4,24},{8,20},{12,16},{16,12},{20,8},{24,4},{28,0},{1,29},{... | collective-permute-start | bytes 393224 | tf_op jit(solution)/shard_map/ppermute | solution.py:435
  30.7 2.0 %collective-permute-done.7.refs_7_ = bf16[128,512]{1,0:T(8,128)(2,1)S(1)} collective-permute-done((bf16[128,512]{1,0:T(8,128)(2,1)S(1)}, bf16[128,512]{1,0:T(8,128)(2,1)S(1)}, u32[]{:S(2)}, u32[]{:S(2)}) %collective-permute-start.7) | collective-permute-done | bytes 131104 | tf_op jit(solution)/shard_map/ppermute | solution.py:435
  32.7 9.4 %collective-permute-start.4 = (bf16[128,512]{1,0:T(8,128)(2,1)S(1)}, bf16[128,512]{1,0:T(8,128)(2,1)S(1)}, u32[]{:S(2)}, u32[]{:S(2)}) collective-permute-start(bf16[128,512]{1,0:T(8,128)(2,1)S(1)} %get-tuple-element.66), channel_id=1, source_target_pairs={{0,16},{4,20},{8,24},{12,28},{16,0},{20,4},{24,8},{28,12},{1,17},{... | collective-permute-start | bytes 393224 | tf_op jit(solution)/shard_map/ppermute | solution.py:435
  42.2 1.0 collective-permute-start.8
  43.2 0.7 copy-done.6
  43.9 7.5 %shard_map.88 = (bf16[512,1024]{1,0:T(8,128)(2,1)S(1)}, bf16[1024,512]{1,0:T(8,128)(2,1)S(1)}, bf16[512,2048]{1,0:T(8,128)(2,1)S(1)}, bf16[512,2048]{1,0:T(8,128...) custom-call(bf16[128,512]{1,0:T(8,128)(2,1)S(1)} %get-tuple-element., ...), custom_call_target="tpu_custom_call" | custom-call | flops 2147483648 | bytes 21366784 | tf_op jit(solution)/shard_map/pallas_call | solution.py:37
  51.4 0.3 collective-permute-done.4.refs_4_
  51.7 2.5 %collective-permute-done.6.refs_5_ = bf16[128,512]{1,0:T(8,128)(2,1)S(1)} collective-permute-done((bf16[128,512]{1,0:T(8,128)(2,1)S(1)}, bf16[128,512]{1,0:T(8,128)(2,1)S(1)}, u32[]{:S(2)}, u32[]{:S(2)}) %collective-permute-start.6) | collective-permute-done | bytes 131104 | tf_op jit(solution)/shard_map/ppermute | solution.py:435
  54.2 1.5 %shard_map.89 = (bf16[512,512]{1,0:T(8,128)(2,1)S(1)}, bf16[512,512]{1,0:T(8,128)(2,1)S(1)}, bf16[512,512]{1,0:T(8,128)(2,1)S(1)}, bf16[512,512]{1,0:T(8,128)(2,1)S(1)}) custom-call(bf16[128,512]{1,0:T(8,128)(2,1)S(1)} %get-tuple-element.60.refs_0_, bf16[256,512]{1,0:T(8,128)(2,1)S(1)} %collective-permute-done.refs_1_, ...), custom_call_target="tpu_custom_call" | custom-call | flops 805306368 | bytes 10092544 | tf_op jit(solution)/shard_map/pallas_call | solution.py:37
  55.8 1.3 %shard_map.90 = (bf16[2,1024,128]{2,1,0:T(8,128)(2,1)S(1)}, bf16[2,1024,128]{2,1,0:T(8,128)(2,1)S(1)}) custom-call(bf16[512,512]{1,0:T(8,128)(2,1)S(1)} %get-tuple-element.87.xhat_t_ref, bf16[512,512]{1,0:T(8,128)(2,1)S(1)} %get-tuple-element.82.dpre_ref.dpre_u_ref, bf16[512,512]{1,0:T(8,128)(2,1)S(1)} %get-tuple-element.88.gated_t_ref, ...), custom_call_target="tpu_custom_call" | custom-call | flops 536870912 | bytes 3145728 | tf_op jit(solution)/shard_map/pallas_call | solution.py:37
  57.2 3.3 %shard_map.91.dpre_ref = bf16[512,2048]{1,0:T(8,128)(2,1)S(1)} custom-call(bf16[512,512]{1,0:T(8,128)(2,1)S(1)} %get-tuple-element.82.dpre_ref.dpre_u_ref, bf16[512,2048]{1,0:T(8,128)(2,1)S(1)} %get-tuple-element.80.refs_12_.refs_0_, bf16[512,2048]{1,0:T(8,128)(2,1)S(1)} %get-tuple-element.81.refs_13_.refs_1_, ...), custom_call_target="tpu_custom_call" | custom-call | flops 1073741824 | bytes 16777216 | tf_op jit(solution)/shard_map/pallas_call | solution.py:37
  60.6 1.2 %shard_map.93 = (bf16[2,1536,128]{2,1,0:T(8,128)(2,1)S(1)}, bf16[2,1536,128]{2,1,0:T(8,128)(2,1)S(1)}) custom-call(bf16[512,512]{1,0:T(8,128)(2,1)S(1)} %get-tuple-element.87.xhat_t_ref, bf16[512,2048]{1,0:T(8,128)(2,1)S(1)} %shard_map.91.dpre_ref), custom_call_target="tpu_custom_call" | custom-call | flops 1073741824 | bytes 4194304 | tf_op jit(solution)/shard_map/pallas_call | solution.py:37
  61.8 0.6 collective-permute-start.12
  62.3 1.6 %shard_map.94.dx_ref = bf16[512,512]{1,0:T(8,128)(2,1)S(1)} custom-call(bf16[512,2048]{1,0:T(8,128)(2,1)S(1)} %shard_map.91.dpre_ref, bf16[512,2048]{1,0:T(8,128)(2,1)S(1)} %copy-done, bf16[512,512]{1,0:T(8,128)(2,1)S(1)} %get-tuple-element.98.xhat_ref, f32[512,128]{1,0:T(8,128)S(1)} %get-tuple-element.99.x_rstd_ref, ...), custom_call_target="tpu_custom_call" | custom-call | flops 1073741824 | bytes 6029312 | tf_op jit(solution)/shard_map/pallas_call | solution.py:37
  63.9 0.3 collective-permute-done.12.got_ref
  64.2 0.3 shard_map.95
  64.6 1.0 collective-permute-start.15
  65.6 1.7 %shard_map.96 = bf16[1024,512]{1,0:T(8,128)(2,1)} custom-call(bf16[512,512]{1,0:T(8,128)(2,1)S(1)} %shard_map.94.dx_ref, bf16[1024,512]{1,0:T(8,128)(2,1)S(1)} %get-tuple-element.103.unplace_ref), custom_call_target="tpu_custom_call" | custom-call | flops 536870912 | bytes 2621440 | tf_op jit(solution)/shard_map/pallas_call | solution.py:37
  67.3 4.7 %all-to-all-start = ((bf16[8,128,512]{2,1,0:T(8,128)(2,1)}), bf16[8,128,512]{2,1,0:T(8,128)(2,1)S(1)}, u32[]{:S(2)}, u32[]{:S(2)}) async-start(bf16[8,128,512]{2,1,0:T(8,128)(2,1)} %bitcast), calls=%async_computation | async-start | bytes 2097152 | tf_op jit(solution)/shard_map/all_to_all | solution.py:538
  72.0 1.5 %collective-permute-start.13 = (bf16[1024,128]{1,0:T(8,128)(2,1)S(1)}, bf16[1024,128]{1,0:T(8,128)(2,1)S(1)}, u32[]{:S(2)}, u32[]{:S(2)}) collective-permute-start(bf16[1024,128]{1,0:T(8,128)(2,1)S(1)} %get-tuple-element.94), channel_id=1, source_target_pairs={{0,2},{1,3},{2,0},{3,1},{4,6},{5,7},{6,4},{7,5},{8,10},{9,11},{10,... | collective-permute-start | bytes 786440 | tf_op jit(solution)/shard_map/ppermute | solution.py:435
  73.5 4.5 %collective-permute-done.15.got_ref = bf16[2,768,128]{2,1,0:T(8,128)(2,1)S(1)} collective-permute-done((bf16[2,768,128]{2,1,0:T(8,128)(2,1)S(1)}, bf16[2,768,128]{2,1,0:T(8,128)(2,1)S(1)}, u32[]{:S(2)}, u32[]{:S(2)}) %collective-permute-start.15) | collective-permute-done | bytes 393248 | tf_op jit(solution)/shard_map/ppermute | solution.py:435
  78.1 1.0 collective-permute-start.16
  79.1 2.1 %collective-permute-done.13.second_ref = bf16[1024,128]{1,0:T(8,128)(2,1)S(1)} collective-permute-done((bf16[1024,128]{1,0:T(8,128)(2,1)S(1)}, bf16[1024,128]{1,0:T(8,128)(2,1)S(1)}, u32[]{:S(2)}, u32[]{:S(2)}) %collective-permute-start.13) | collective-permute-done | bytes 262176 | tf_op jit(solution)/shard_map/ppermute | solution.py:435
  81.3 1.4 %collective-permute-start.14 = (bf16[512,128]{1,0:T(8,128)(2,1)S(1)}, bf16[512,128]{1,0:T(8,128)(2,1)S(1)}, u32[]{:S(2)}, u32[]{:S(2)}) collective-permute-start(bf16[512,128]{1,0:T(8,128)(2,1)S(1)} %get-tuple-element.106), channel_id=1, source_target_pairs={{0,4},{4,0},{8,12},{12,8},{16,20},{20,16},{24,28},{28,24},{1,5},{5... | collective-permute-start | bytes 393224 | tf_op jit(solution)/shard_map/ppermute | solution.py:435
  82.7 4.5 %collective-permute-done.14.refs_1_ = bf16[512,128]{1,0:T(8,128)(2,1)S(1)} collective-permute-done((bf16[512,128]{1,0:T(8,128)(2,1)S(1)}, bf16[512,128]{1,0:T(8,128)(2,1)S(1)}, u32[]{:S(2)}, u32[]{:S(2)}) %collective-permute-start.14) | collective-permute-done | bytes 131104 | tf_op jit(solution)/shard_map/ppermute | solution.py:435
  87.4 5.9 %collective-permute-start.17 = (bf16[320,128]{1,0:T(8,128)(2,1)S(1)}, bf16[320,128]{1,0:T(8,128)(2,1)S(1)}, u32[]{:S(2)}, u32[]{:S(2)}) collective-permute-start(bf16[320,128]{1,0:T(8,128)(2,1)S(1)} %get-tuple-element.111), channel_id=1, source_target_pairs={{0,8},{4,12},{8,0},{12,4},{16,24},{20,28},{24,16},{28,20},{1,9},{5... | collective-permute-start | bytes 245768 | tf_op jit(solution)/shard_map/ppermute | solution.py:435
  93.2 1.7 %collective-permute-start.18 = (bf16[320,128]{1,0:T(8,128)(2,1)S(1)}, bf16[320,128]{1,0:T(8,128)(2,1)S(1)}, u32[]{:S(2)}, u32[]{:S(2)}) collective-permute-start(bf16[320,128]{1,0:T(8,128)(2,1)S(1)} %get-tuple-element.112), channel_id=1, source_target_pairs={{0,16},{4,20},{8,24},{12,28},{16,0},{20,4},{24,8},{28,12},{1,17},{... | collective-permute-start | bytes 245768 | tf_op jit(solution)/shard_map/ppermute | solution.py:435
  95.0 0.7 collective-permute-start.19
  95.7 2.8 %collective-permute-done.17.refs_1_ = bf16[320,128]{1,0:T(8,128)(2,1)S(1)} collective-permute-done((bf16[320,128]{1,0:T(8,128)(2,1)S(1)}, bf16[320,128]{1,0:T(8,128)(2,1)S(1)}, u32[]{:S(2)}, u32[]{:S(2)}) %collective-permute-start.17) | collective-permute-done | bytes 81952 | tf_op jit(solution)/shard_map/ppermute | solution.py:435
  98.5 5.7 %collective-permute-done.18.refs_2_ = bf16[320,128]{1,0:T(8,128)(2,1)S(1)} collective-permute-done((bf16[320,128]{1,0:T(8,128)(2,1)S(1)}, bf16[320,128]{1,0:T(8,128)(2,1)S(1)}, u32[]{:S(2)}, u32[]{:S(2)}) %collective-permute-start.18) | collective-permute-done | bytes 81952 | tf_op jit(solution)/shard_map/ppermute | solution.py:435
  104.2 1.6 %collective-permute-start.21 = (bf16[320,128]{1,0:T(8,128)(2,1)S(1)}, bf16[320,128]{1,0:T(8,128)(2,1)S(1)}, u32[]{:S(2)}, u32[]{:S(2)}) collective-permute-start(bf16[320,128]{1,0:T(8,128)(2,1)S(1)} %shard_map.101.refs_0_), channel_id=1, source_target_pairs={{0,2},{1,3},{2,0},{3,1},{4,6},{5,7},{6,4},{7,5},{8,10},{9,11},{10,... | collective-permute-start | bytes 245768 | tf_op jit(solution)/shard_map/ppermute | solution.py:435
  105.8 2.9 %collective-permute-done.21.refs_2_ = bf16[320,128]{1,0:T(8,128)(2,1)S(1)} collective-permute-done((bf16[320,128]{1,0:T(8,128)(2,1)S(1)}, bf16[320,128]{1,0:T(8,128)(2,1)S(1)}, u32[]{:S(2)}, u32[]{:S(2)}) %collective-permute-start.21) | collective-permute-done | bytes 81952 | tf_op jit(solution)/shard_map/ppermute | solution.py:435
  108.8 0.3 shard_map.85.lookup_ref
  109.1 1.5 %shard_map.97 = bf16[512,512]{1,0:T(8,128)(2,1)} custom-call(bf16[512,1024]{1,0:T(8,128)(2,1)S(1)} %shard_map.85.lookup_ref, bf16[1024,512]{1,0:T(8,128)(2,1)S(1)} %bitcast.3), custom_call_target="tpu_custom_call" | custom-call | flops 536870912 | bytes 2621440 | tf_op jit(solution)/shard_map/pallas_call | solution.py:37
  110.6 1.0 shard_map.102
  (32 shorter events, 0.7 us)
Async XLA Ops:
  0.6 42.6 %copy-start = (bf16[512,2048]{1,0:T(8,128)(2,1)S(1)}, bf16[512,2048]{1,0:T(8,128)(2,1)}, u32[]{:S(2)}) copy-start(bf16[512,2048]{1,0:T(8,128)(2,1)} %w_ref.1) | copy-start | bytes 6291460
  0.6 0.8 copy-start.2
  1.5 1.0 copy-start.4
  3.0 15.0 %collective-permute-start.3 = (bf16[128,512]{1,0:T(8,128)(2,1)S(1)}, bf16[128,512]{1,0:T(8,128)(2,1)S(1)}, u32[]{:S(2)}, u32[]{:S(2)}) collective-permute-start(bf16[128,512]{1,0:T(8,128)(2,1)S(1)} %get-tuple-element.65), channel_id=1, source_target_pairs={{0,20},{4,16},{8,28},{12,24},{16,4},{20,0},{24,12},{28,8},{1,21},{... | collective-permute-start | bytes 393224 | tf_op jit(solution)/shard_map/ppermute | solution.py:435
  8.1 10.0 %collective-permute-start.9 = (bf16[128,512]{1,0:T(8,128)(2,1)S(1)}, bf16[128,512]{1,0:T(8,128)(2,1)S(1)}, u32[]{:S(2)}, u32[]{:S(2)}) collective-permute-start(bf16[128,512]{1,0:T(8,128)(2,1)S(1)} %get-tuple-element.74), channel_id=1, source_target_pairs={{0,24},{4,28},{8,16},{12,20},{16,8},{20,12},{24,0},{28,4},{1,25},{... | collective-permute-start | bytes 393224 | tf_op jit(solution)/shard_map/ppermute | solution.py:435
  9.4 1.0 copy-start.5
  11.4 30.8 %collective-permute-start = (bf16[256,512]{1,0:T(8,128)(2,1)S(1)}, bf16[256,512]{1,0:T(8,128)(2,1)S(1)}, u32[]{:S(2)}, u32[]{:S(2)}) collective-permute-start(bf16[256,512]{1,0:T(8,128)(2,1)S(1)} %get-tuple-element.61), channel_id=1, source_target_pairs={{0,4},{4,0},{8,12},{12,8},{16,20},{20,16},{24,28},{28,24},{1,5},{5... | collective-permute-start | bytes 786440 | tf_op jit(solution)/shard_map/ppermute | solution.py:435
  12.0 30.2 %collective-permute-start.1 = (bf16[256,512]{1,0:T(8,128)(2,1)S(1)}, bf16[256,512]{1,0:T(8,128)(2,1)S(1)}, u32[]{:S(2)}, u32[]{:S(2)}) collective-permute-start(bf16[256,512]{1,0:T(8,128)(2,1)S(1)} %get-tuple-element.62), channel_id=1, source_target_pairs={{0,8},{4,12},{8,0},{12,4},{16,24},{20,28},{24,16},{28,20},{1,9},{5... | collective-permute-start | bytes 786440 | tf_op jit(solution)/shard_map/ppermute | solution.py:435
  12.2 30.9 %collective-permute-start.2 = (bf16[256,512]{1,0:T(8,128)(2,1)S(1)}, bf16[256,512]{1,0:T(8,128)(2,1)S(1)}, u32[]{:S(2)}, u32[]{:S(2)}) collective-permute-start(bf16[256,512]{1,0:T(8,128)(2,1)S(1)} %get-tuple-element.63), channel_id=1, source_target_pairs={{0,12},{4,8},{8,4},{12,0},{16,28},{20,24},{24,20},{28,16},{1,13},{... | collective-permute-start | bytes 786440 | tf_op jit(solution)/shard_map/ppermute | solution.py:435
  18.1 11.5 %collective-permute-start.5 = (bf16[128,512]{1,0:T(8,128)(2,1)S(1)}, bf16[128,512]{1,0:T(8,128)(2,1)S(1)}, u32[]{:S(2)}, u32[]{:S(2)}) collective-permute-start(bf16[128,512]{1,0:T(8,128)(2,1)S(1)} %get-tuple-element.68), channel_id=1, source_target_pairs={{0,16},{4,20},{8,24},{12,28},{16,0},{20,4},{24,8},{28,12},{1,17},{... | collective-permute-start | bytes 393224 | tf_op jit(solution)/shard_map/ppermute | solution.py:435
  18.1 14.6 %collective-permute-start.7 = (bf16[128,512]{1,0:T(8,128)(2,1)S(1)}, bf16[128,512]{1,0:T(8,128)(2,1)S(1)}, u32[]{:S(2)}, u32[]{:S(2)}) collective-permute-start(bf16[128,512]{1,0:T(8,128)(2,1)S(1)} %get-tuple-element.71), channel_id=1, source_target_pairs={{0,28},{4,24},{8,20},{12,16},{16,12},{20,8},{24,4},{28,0},{1,29},{... | collective-permute-start | bytes 393224 | tf_op jit(solution)/shard_map/ppermute | solution.py:435
  29.6 21.8 %collective-permute-start.10 = (bf16[128,512]{1,0:T(8,128)(2,1)S(1)}, bf16[128,512]{1,0:T(8,128)(2,1)S(1)}, u32[]{:S(2)}, u32[]{:S(2)}) collective-permute-start(bf16[128,512]{1,0:T(8,128)(2,1)S(1)} %get-tuple-element.75), channel_id=1, source_target_pairs={{0,28},{4,24},{8,20},{12,16},{16,12},{20,8},{24,4},{28,0},{1,29},{... | collective-permute-start | bytes 393224 | tf_op jit(solution)/shard_map/ppermute | solution.py:435
  32.7 19.0 %collective-permute-start.4 = (bf16[128,512]{1,0:T(8,128)(2,1)S(1)}, bf16[128,512]{1,0:T(8,128)(2,1)S(1)}, u32[]{:S(2)}, u32[]{:S(2)}) collective-permute-start(bf16[128,512]{1,0:T(8,128)(2,1)S(1)} %get-tuple-element.66), channel_id=1, source_target_pairs={{0,16},{4,20},{8,24},{12,28},{16,0},{20,4},{24,8},{28,12},{1,17},{... | collective-permute-start | bytes 393224 | tf_op jit(solution)/shard_map/ppermute | solution.py:435
  42.2 12.1 %collective-permute-start.6 = (bf16[128,512]{1,0:T(8,128)(2,1)S(1)}, bf16[128,512]{1,0:T(8,128)(2,1)S(1)}, u32[]{:S(2)}, u32[]{:S(2)}) collective-permute-start(bf16[128,512]{1,0:T(8,128)(2,1)S(1)} %get-tuple-element.69), channel_id=1, source_target_pairs={{0,20},{4,16},{8,28},{12,24},{16,4},{20,0},{24,12},{28,8},{1,21},{... | collective-permute-start | bytes 393224 | tf_op jit(solution)/shard_map/ppermute | solution.py:435
  42.2 12.1 %collective-permute-start.8 = (bf16[128,512]{1,0:T(8,128)(2,1)S(1)}, bf16[128,512]{1,0:T(8,128)(2,1)S(1)}, u32[]{:S(2)}, u32[]{:S(2)}) collective-permute-start(bf16[128,512]{1,0:T(8,128)(2,1)S(1)} %get-tuple-element.72), channel_id=1, source_target_pairs={{0,24},{4,28},{8,16},{12,20},{16,8},{20,12},{24,0},{28,4},{1,25},{... | collective-permute-start | bytes 393224 | tf_op jit(solution)/shard_map/ppermute | solution.py:435
  43.2 0.7 copy-start.6
  43.9 10.4 %copy-start.1 = (bf16[512,512]{1,0:T(8,128)(2,1)S(1)}, bf16[512,512]{1,0:T(8,128)(2,1)}, u32[]{:S(2)}) copy-start(bf16[512,512]{1,0:T(8,128)(2,1)} %refs_11_.1) | copy-start | bytes 1572868
  57.1 3.4 %collective-permute-start.11 = (bf16[2,1024,128]{2,1,0:T(8,128)(2,1)S(1)}, bf16[2,1024,128]{2,1,0:T(8,128)(2,1)S(1)}, u32[]{:S(2)}, u32[]{:S(2)}) collective-permute-start(bf16[2,1024,128]{2,1,0:T(8,128)(2,1)S(1)} %get-tuple-element.90), channel_id=1, source_target_pairs={{0,1},{1,0},{2,3},{3,2},{4,5},{5,4},{6,7},{7,6},{8,9},{9,8},{10,11... | collective-permute-start | bytes 1572872 | tf_op jit(solution)/shard_map/ppermute | solution.py:435
  61.8 2.5 %collective-permute-start.12 = (bf16[2,1536,128]{2,1,0:T(8,128)(2,1)S(1)}, bf16[2,1536,128]{2,1,0:T(8,128)(2,1)S(1)}, u32[]{:S(2)}, u32[]{:S(2)}) collective-permute-start(bf16[2,1536,128]{2,1,0:T(8,128)(2,1)S(1)} %get-tuple-element.96), channel_id=1, source_target_pairs={{0,1},{1,0},{2,3},{3,2},{4,5},{5,4},{6,7},{7,6},{8,9},{9,8},{10,11... | collective-permute-start | bytes 2359304 | tf_op jit(solution)/shard_map/ppermute | solution.py:435
  64.6 13.4 %collective-permute-start.15 = (bf16[2,768,128]{2,1,0:T(8,128)(2,1)S(1)}, bf16[2,768,128]{2,1,0:T(8,128)(2,1)S(1)}, u32[]{:S(2)}, u32[]{:S(2)}) collective-permute-start(bf16[2,768,128]{2,1,0:T(8,128)(2,1)S(1)} %get-tuple-element.101), channel_id=1, source_target_pairs={{0,4},{4,0},{8,12},{12,8},{16,20},{20,16},{24,28},{28,24},{1,5},{5... | collective-permute-start | bytes 1179656 | tf_op jit(solution)/shard_map/ppermute | solution.py:435
  67.3 41.8 %all-to-all-start = ((bf16[8,128,512]{2,1,0:T(8,128)(2,1)}), bf16[8,128,512]{2,1,0:T(8,128)(2,1)S(1)}, u32[]{:S(2)}, u32[]{:S(2)}) async-start(bf16[8,128,512]{2,1,0:T(8,128)(2,1)} %bitcast), calls=%async_computation | async-start | bytes 2097152 | tf_op jit(solution)/shard_map/all_to_all | solution.py:538
  72.0 9.2 %collective-permute-start.13 = (bf16[1024,128]{1,0:T(8,128)(2,1)S(1)}, bf16[1024,128]{1,0:T(8,128)(2,1)S(1)}, u32[]{:S(2)}, u32[]{:S(2)}) collective-permute-start(bf16[1024,128]{1,0:T(8,128)(2,1)S(1)} %get-tuple-element.94), channel_id=1, source_target_pairs={{0,2},{1,3},{2,0},{3,1},{4,6},{5,7},{6,4},{7,5},{8,10},{9,11},{10,... | collective-permute-start | bytes 786440 | tf_op jit(solution)/shard_map/ppermute | solution.py:435
  78.1 9.2 %collective-permute-start.16 = (bf16[768,128]{1,0:T(8,128)(2,1)S(1)}, bf16[768,128]{1,0:T(8,128)(2,1)S(1)}, u32[]{:S(2)}, u32[]{:S(2)}) collective-permute-start(bf16[768,128]{1,0:T(8,128)(2,1)S(1)} %get-tuple-element.109), channel_id=1, source_target_pairs={{0,2},{1,3},{2,0},{3,1},{4,6},{5,7},{6,4},{7,5},{8,10},{9,11},{10,... | collective-permute-start | bytes 589832 | tf_op jit(solution)/shard_map/ppermute | solution.py:435
  81.3 5.9 %collective-permute-start.14 = (bf16[512,128]{1,0:T(8,128)(2,1)S(1)}, bf16[512,128]{1,0:T(8,128)(2,1)S(1)}, u32[]{:S(2)}, u32[]{:S(2)}) collective-permute-start(bf16[512,128]{1,0:T(8,128)(2,1)S(1)} %get-tuple-element.106), channel_id=1, source_target_pairs={{0,4},{4,0},{8,12},{12,8},{16,20},{20,16},{24,28},{28,24},{1,5},{5... | collective-permute-start | bytes 393224 | tf_op jit(solution)/shard_map/ppermute | solution.py:435
  87.4 11.1 %collective-permute-start.17 = (bf16[320,128]{1,0:T(8,128)(2,1)S(1)}, bf16[320,128]{1,0:T(8,128)(2,1)S(1)}, u32[]{:S(2)}, u32[]{:S(2)}) collective-permute-start(bf16[320,128]{1,0:T(8,128)(2,1)S(1)} %get-tuple-element.111), channel_id=1, source_target_pairs={{0,8},{4,12},{8,0},{12,4},{16,24},{20,28},{24,16},{28,20},{1,9},{5... | collective-permute-start | bytes 245768 | tf_op jit(solution)/shard_map/ppermute | solution.py:435
  93.2 10.9 %collective-permute-start.18 = (bf16[320,128]{1,0:T(8,128)(2,1)S(1)}, bf16[320,128]{1,0:T(8,128)(2,1)S(1)}, u32[]{:S(2)}, u32[]{:S(2)}) collective-permute-start(bf16[320,128]{1,0:T(8,128)(2,1)S(1)} %get-tuple-element.112), channel_id=1, source_target_pairs={{0,16},{4,20},{8,24},{12,28},{16,0},{20,4},{24,8},{28,12},{1,17},{... | collective-permute-start | bytes 245768 | tf_op jit(solution)/shard_map/ppermute | solution.py:435
  95.0 9.2 %collective-permute-start.19 = (bf16[320,128]{1,0:T(8,128)(2,1)S(1)}, bf16[320,128]{1,0:T(8,128)(2,1)S(1)}, u32[]{:S(2)}, u32[]{:S(2)}) collective-permute-start(bf16[320,128]{1,0:T(8,128)(2,1)S(1)} %get-tuple-element.113), channel_id=1, source_target_pairs={{0,24},{4,28},{8,16},{12,20},{16,8},{20,12},{24,0},{28,4},{1,25},{... | collective-permute-start | bytes 245768 | tf_op jit(solution)/shard_map/ppermute | solution.py:435
  104.2 4.6 %copy-start.3 = (s32[1,512]{1,0:T(1,128)S(1)}, s32[1,512]{1,0:T(1,128)}, u32[]{:S(2)}) copy-start(s32[1,512]{1,0:T(1,128)} %place_ref.5) | copy-start | bytes 6148
  104.2 4.5 %collective-permute-start.21 = (bf16[320,128]{1,0:T(8,128)(2,1)S(1)}, bf16[320,128]{1,0:T(8,128)(2,1)S(1)}, u32[]{:S(2)}, u32[]{:S(2)}) collective-permute-start(bf16[320,128]{1,0:T(8,128)(2,1)S(1)} %shard_map.101.refs_0_), channel_id=1, source_target_pairs={{0,2},{1,3},{2,0},{3,1},{4,6},{5,7},{6,4},{7,5},{8,10},{9,11},{10,... | collective-permute-start | bytes 245768 | tf_op jit(solution)/shard_map/ppermute | solution.py:435
  105.8 4.7 %collective-permute-start.20 = (bf16[320,128]{1,0:T(8,128)(2,1)S(1)}, bf16[320,128]{1,0:T(8,128)(2,1)S(1)}, u32[]{:S(2)}, u32[]{:S(2)}) collective-permute-start(bf16[320,128]{1,0:T(8,128)(2,1)S(1)} %shard_map.101.refs_0_), channel_id=1, source_target_pairs={{0,1},{1,0},{2,3},{3,2},{4,5},{5,4},{6,7},{7,6},{8,9},{9,8},{10,11... | collective-permute-start | bytes 245768 | tf_op jit(solution)/shard_map/ppermute | solution.py:435
  108.7 1.9 %collective-permute-start.22 = (bf16[320,128]{1,0:T(8,128)(2,1)S(1)}, bf16[320,128]{1,0:T(8,128)(2,1)S(1)}, u32[]{:S(2)}, u32[]{:S(2)}) collective-permute-start(bf16[320,128]{1,0:T(8,128)(2,1)S(1)} %collective-permute-done.21.refs_2_), channel_id=1, source_target_pairs={{0,1},{1,0},{2,3},{3,2},{4,5},{5,4},{6,7},{7,6},{8,9},{9,8},{10,11... | collective-permute-start | bytes 245768 | tf_op jit(solution)/shard_map/ppermute | solution.py:435
